TPU v7x, 512 devices: a whole 4x4x16 slice. The times are simulated.
512 devices in a mesh: leaf: 128 (over z, x, core), sub: 4 (over y).
Axes of the slice: x: 4, y: 4, z: 16, core: 2. Of those that a mesh axis runs over, the one named last changes fastest.
Arguments:
- points: float32 [3, 2097152], P(None, ('leaf', 'sub')), may hold values from -6 to 6
- charges: bfloat16 [8, 2097152], P(None, ('leaf', 'sub')), may hold values from -6 to 6
- order: int32 [2097152], P(('leaf', 'sub')), may hold values from 0 to 4095, as said below
- basis: bfloat16 [8192, 64, 256], P(('leaf', 'sub')), may hold values from -0.5 to 0.5
- transfer: float32 [8192, 64, 64], P(('leaf', 'sub')), may hold values from -0.375 to 0.375
- leaf_proxy: float32 [8192, 3, 64], P(('leaf', 'sub')), may hold values from -6 to 6
- cluster_proxy: float32 [512, 3, 64], P(('leaf', 'sub')), may hold values from -6 to 6
- near: int32 [8192, 5], P(('leaf', 'sub')), may hold values from -1 to 8191, as said below
- far_leaf: int32 [8192, 8], P(('leaf', 'sub')), may hold values from -1 to 8191, as said below
- far_cluster: int32 [512, 16], P(('leaf', 'sub')), may hold values from -1 to 511, as said below
Outputs:
- potential: float32 [8, 2097152], P(None, ('leaf', 'sub'))
Inputs may be any that keep to these rules, and one draw needn't show every extreme that they name: `order`: in each aligned block of 4096 tree positions the entries are a permutation of 0 to 4095. `near`: row g lists distinct leaves h with |h - g| <= 2, g among them, valid entries first and then -1; some row has no -1. `far_leaf`: row g lists distinct leaves h with 2 < |h - g| <= 6, valid entries first and then -1; some row has no -1. `far_cluster`: row c lists distinct clusters of other groups at most 4 groups away from c's group, a group being the 4 clusters c // 4 * 4 to c // 4 * 4 + 3; valid entries first and then -1; some row has no -1.
All inputs are finite; a program needn't handle non-finite values.
Results may differ from a plain program's by a relative error of at most 0.0019.
Values sent between devices are 32-bit elements; how exact they have to be, the bound alone decides.
No kernel may reach another device: no remote copies, remote signals or barrier semaphores. Data moves between devices by JAX's collectives and lax.ppermute only.
A program may use at most 64 MiB of HBM per device.

v0:
```python
import jax
import jax.numpy as jnp
from jax import lax
from jax.sharding import PartitionSpec as P

REACH = 2
BAND = 4
FREACH = 6


KERNEL_FACTOR = 0.0625
SMOOTHING_SQUARE = 0.01


def extended(cells, sides, width):
    for axis, dim in sides:
        count = lax.axis_size(axis)
        ends = count - 1
        head = lax.slice_in_dim(cells, 0, width, axis=dim)
        tail = lax.slice_in_dim(cells, cells.shape[dim] - width, cells.shape[dim], axis=dim)
        cells = jnp.concatenate(
            [
                lax.ppermute(tail, axis, [(i, (i + 1) % count) for i in range(ends)]),
                cells,
                lax.ppermute(head, axis, [((i + 1) % count, i) for i in range(ends)]),
            ],
            axis=dim,
        )
    return cells


def passed_along(value, axis, steps):
    count = lax.axis_size(axis)
    initial, last = (max(0, -steps), min(count, count - steps))
    return lax.ppermute(value, axis, [(source, source + steps) for source in range(initial, last)])


def kernel_block(source, target):
    difference_x = source[..., 0, :, None] - target[..., 0, None, :]
    difference_y = source[..., 1, :, None] - target[..., 1, None, :]
    difference_z = source[..., 2, :, None] - target[..., 2, None, :]
    return KERNEL_FACTOR / jnp.sqrt(
        difference_x * difference_x
        + difference_y * difference_y
        + difference_z * difference_z
        + SMOOTHING_SQUARE
    )


def shards(
    points, charges, order, basis, transfer, leaf_proxy, cluster_proxy, near, far_leaf, far_cluster
):
    highest_level = lax.Precision.HIGHEST
    leaf_dev, rank, leaf = basis.shape
    nrhs, count = charges.shape
    tree_charges = jnp.take(charges, order, axis=1)
    tree_points = jnp.take(points, order, axis=1)
    first = lax.axis_index(("leaf", "sub")) * leaf_dev
    stacked = jnp.concatenate([tree_charges.astype(jnp.float32), tree_points], axis=0)
    window = extended(stacked, ((("leaf", "sub"), 1),), REACH * leaf)
    window_leaves = window.reshape(nrhs + 3, leaf_dev + 2 * REACH, leaf).transpose(1, 0, 2)
    own_charges = tree_charges.reshape(nrhs, leaf_dev, leaf).transpose(1, 0, 2)
    coeffs = jnp.einsum("glp,grp->glr", own_charges, basis, preferred_element_type=jnp.float32)
    leaf_table = jnp.concatenate([coeffs, leaf_proxy], axis=1)
    leaf_window = extended(leaf_table, ((("leaf", "sub"), 0),), FREACH)
    parent_index = jnp.einsum("glr,grs->ls", coeffs, transfer, precision=highest_level)
    cluster_entry = jnp.concatenate([parent_index, cluster_proxy[0]], axis=0)[None]
    group_table = lax.all_gather(cluster_entry, "sub", axis=0, tiled=True)
    pieces = []
    for offset in range(-BAND, BAND + 1):
        if offset == 0:
            pieces.append(group_table)
        else:
            pieces.append(passed_along(group_table, "leaf", -offset))
    cluster_table = jnp.concatenate(pieces, axis=0)
    base = (lax.axis_index("leaf") - BAND) * lax.axis_size("sub")
    mine = cluster_proxy[0]
    targets = far_cluster[0]
    cluster_keep = (targets >= 0).astype(jnp.float32)[:, None, None]
    entries = jnp.take(cluster_table, jnp.where(targets >= 0, targets - base, 0), axis=0)
    couplings = kernel_block(entries[:, nrhs:], mine)
    coupled_blocks = jnp.einsum(
        "fla,fab->lb", entries[:, :nrhs] * cluster_keep, couplings, precision=highest_level
    )
    down = jnp.zeros((leaf_dev, nrhs, rank), jnp.float32)
    for slot in range(far_leaf.shape[1]):
        target = far_leaf[:, slot]
        keep_mask = (target >= 0).astype(jnp.float32)[:, None, None]
        picked = jnp.take(leaf_window, jnp.where(target >= 0, target - first + FREACH, 0), axis=0)
        coupling_matrix = kernel_block(picked[:, nrhs:], leaf_proxy)
        down = down + jnp.einsum(
            "glr,grs->gls", picked[:, :nrhs] * keep_mask, coupling_matrix, precision=highest_level
        )
    down = down + jnp.einsum("ls,grs->glr", coupled_blocks, transfer, precision=highest_level)
    far_field = jnp.einsum("glr,grp->glp", down, basis.astype(jnp.float32), precision=highest_level)
    own_points = window_leaves[REACH : REACH + leaf_dev, nrhs:]
    empty = jnp.zeros((leaf_dev, nrhs, leaf), jnp.float32)
    near_sum = empty
    for slot in range(near.shape[1]):
        near_target = near[:, slot]
        near_keep_mask = (near_target >= 0).astype(jnp.float32)[:, None, None]
        blocks = jnp.take(
            window_leaves, jnp.where(near_target >= 0, near_target - first + REACH, 0), axis=0
        )
        dense = kernel_block(blocks[:, nrhs:], own_points).astype(jnp.bfloat16)
        weights = (blocks[:, :nrhs] * near_keep_mask).astype(jnp.bfloat16)
        near_sum = near_sum + jnp.einsum(
            "glp,gpq->glq", weights, dense, preferred_element_type=jnp.float32
        )
    result = near_sum + far_field
    return result.transpose(1, 0, 2).reshape(nrhs, count)


def solution(mesh):
    in_specs = (
        P(None, ("leaf", "sub")),
        P(None, ("leaf", "sub")),
        P(("leaf", "sub")),
        P(("leaf", "sub"), None, None),
        P(("leaf", "sub"), None, None),
        P(("leaf", "sub"), None, None),
        P(("leaf", "sub"), None, None),
        P(("leaf", "sub"), None),
        P(("leaf", "sub"), None),
        P(("leaf", "sub"), None),
    )
    out_specs = P(None, ("leaf", "sub"))
    return jax.shard_map(shards, mesh=mesh, in_specs=in_specs, out_specs=out_specs, check_vma=False)
```

profile of v0, /device:TPU:384, one launch (start us, length us, event | category | flops | bytes accessed | tf_op | source)
XLA Modules:
  0.0 152.3 jit_solution(13735359662395589300)
XLA Ops:
  0.0 0.8 fusion.212
  0.8 0.7 compare_and_fusion
  1.5 1.3 copy.26
  2.9 12.1 %gather_fusion = bf16[4096,8]{1,0:T(8,128)(2,1)S(1)} fusion(bf16[8,4096]{0,1:T(8,128)(2,1)S(1)} %copy.26, s32[4096]{0:T(1024)S(1)} %fusion.212), kind=kCustom, calls=%fused_computation.13 | custom fusion | bytes 147456 | tf_op jit(solution)/shard_map/jit(_take)/gather | solution.py:56
  16.1 12.4 %all-gather.1 = f32[4,11,64]{2,1,0:T(8,128)S(1)} all-gather(f32[1,11,64]{2,1,0:T(8,128)S(1)} %maximum_bitcast_fusion), channel_id=2, replica_groups=mesh['leaf'=128,'sub'=4] {'sub'}, dimensions={0}, use_global_device_ids=true | all-gather | bytes 14080 | tf_op jit(solution)/shard_map/all_gather | solution.py:68
  28.5 4.9 %collective-permute-start.4 = (f32[4,11,64]{2,1,0:T(8,128)S(1)}, f32[4,11,64]{2,1,0:T(8,128)}, u32[]{:S(2)}, u32[]{:S(2)}) collective-permute-start(f32[4,11,64]{2,1,0:T(8,128)S(1)} %all-gather.1), channel_id=1, source_target_pairs={{0,16},{4,20},{8,24},{12,28},{16,32},{20,36},{24,40},{28,44},{32,4... | collective-permute-start | bytes 33800 | tf_op jit(solution)/shard_map/ppermute | solution.py:35
  33.4 1.9 %collective-permute-start.5 = (f32[4,11,64]{2,1,0:T(8,128)S(1)}, f32[4,11,64]{2,1,0:T(8,128)S(1)}, u32[]{:S(2)}, u32[]{:S(2)}) collective-permute-start(f32[4,11,64]{2,1,0:T(8,128)S(1)} %all-gather.1), channel_id=1, source_target_pairs={{0,12},{4,16},{8,20},{12,24},{16,28},{20,32},{24,36},{28,40},{32,4... | collective-permute-start | bytes 33800 | tf_op jit(solution)/shard_map/ppermute | solution.py:35
  35.4 2.5 %collective-permute-start.6 = (f32[4,11,64]{2,1,0:T(8,128)S(1)}, f32[4,11,64]{2,1,0:T(8,128)S(1)}, u32[]{:S(2)}, u32[]{:S(2)}) collective-permute-start(f32[4,11,64]{2,1,0:T(8,128)S(1)} %all-gather.1), channel_id=1, source_target_pairs={{0,8},{4,12},{8,16},{12,20},{16,24},{20,28},{24,32},{28,36},{32,40... | collective-permute-start | bytes 33800 | tf_op jit(solution)/shard_map/ppermute | solution.py:35
  37.9 3.6 %collective-permute-start.7 = (f32[4,11,64]{2,1,0:T(8,128)S(1)}, f32[4,11,64]{2,1,0:T(8,128)S(1)}, u32[]{:S(2)}, u32[]{:S(2)}) collective-permute-start(f32[4,11,64]{2,1,0:T(8,128)S(1)} %all-gather.1), channel_id=1, source_target_pairs={{0,4},{4,8},{8,12},{12,16},{16,20},{20,24},{24,28},{28,32},{32,36}... | collective-permute-start | bytes 33800 | tf_op jit(solution)/shard_map/ppermute | solution.py:35
  41.5 5.4 %collective-permute-start.8 = (f32[4,11,64]{2,1,0:T(8,128)S(1)}, f32[4,11,64]{2,1,0:T(8,128)S(1)}, u32[]{:S(2)}, u32[]{:S(2)}) collective-permute-start(f32[4,11,64]{2,1,0:T(8,128)S(1)} %all-gather.1), channel_id=1, source_target_pairs={{4,0},{8,4},{12,8},{16,12},{20,16},{24,20},{28,24},{32,28},{36,32}... | collective-permute-start | bytes 33800 | tf_op jit(solution)/shard_map/ppermute | solution.py:35
  46.9 2.9 %bitcast_select_fusion = bf16[8,4096]{0,1:T(8,128)(2,1)} fusion(bf16[4096,8]{1,0:T(8,128)(2,1)S(1)} %gather_fusion, pred[4096]{0:T(1024)(128)(4,1)S(1)} %compare_and_fusion), kind=kLoop, calls=%fused_computation.42 | loop fusion | flops 32768 | bytes 135168 | tf_op jit(solution)/shard_map/jit(_take)/select_n | solution.py:56
  49.7 0.6 slice_bitcast_fusion.2
  50.4 0.6 fusion.222
  51.0 0.6 compare_and_fusion.9
  51.6 0.7 compare_and_fusion.1
  52.3 0.6 fusion.238
  52.9 0.6 slice_bitcast_fusion.5
  53.5 0.6 fusion.240
  55.1 0.6 copy.28
  55.7 14.2 %gather_fusion.1 = f32[4096,3]{1,0:T(8,128)} fusion(f32[3,4096]{0,1:T(8,128)S(1)} %copy.28, s32[4096]{0:T(1024)S(1)} %fusion.212), kind=kCustom, calls=%fused_computation.14 | custom fusion | bytes 114688 | tf_op jit(solution)/shard_map/jit(_take)/gather | solution.py:57
  69.9 3.6 %select_bitcast_fusion = f32[3,4096]{0,1:T(8,128)S(1)} fusion(f32[4096,3]{1,0:T(8,128)} %gather_fusion.1, pred[4096]{0:T(1024)(128)(4,1)S(1)} %compare_and_fusion), kind=kLoop, calls=%fused_computation.21 | loop fusion | flops 12288 | bytes 102400 | tf_op jit(solution)/shard_map/jit(_take)/select_n | solution.py:57
  73.7 0.6 copy.29
  74.3 1.5 %copy.27 = bf16[8,4096]{1,0:T(8,128)(2,1)S(1)} copy(bf16[8,4096]{0,1:T(8,128)(2,1)} %bitcast_select_fusion) | data formatting | bytes 131072 | tf_op jit(solution)/shard_map/jit(_take)/select_n | solution.py:56
  76.2 3.3 %collective-permute-start.9 = (f32[4,11,64]{2,1,0:T(8,128)S(1)}, f32[4,11,64]{2,1,0:T(8,128)S(1)}, u32[]{:S(2)}, u32[]{:S(2)}) collective-permute-start(f32[4,11,64]{2,1,0:T(8,128)S(1)} %all-gather.1), channel_id=1, source_target_pairs={{8,0},{12,4},{16,8},{20,12},{24,16},{28,20},{32,24},{36,28},{40,32... | collective-permute-start | bytes 33800 | tf_op jit(solution)/shard_map/ppermute | solution.py:35
  79.5 0.8 constant_dynamic-update-slice_fusion.8
  80.2 2.1 %collective-permute-start.10 = (f32[4,11,64]{2,1,0:T(8,128)S(1)}, f32[4,11,64]{2,1,0:T(8,128)S(1)}, u32[]{:S(2)}, u32[]{:S(2)}) collective-permute-start(f32[4,11,64]{2,1,0:T(8,128)S(1)} %all-gather.1), channel_id=1, source_target_pairs={{12,0},{16,4},{20,8},{24,12},{28,16},{32,20},{36,24},{40,28},{44,3... | collective-permute-start | bytes 33800 | tf_op jit(solution)/shard_map/ppermute | solution.py:35
  82.4 4.5 %collective-permute-start.11 = (f32[4,11,64]{2,1,0:T(8,128)S(1)}, f32[4,11,64]{2,1,0:T(8,128)S(1)}, u32[]{:S(2)}, u32[]{:S(2)}) collective-permute-start(f32[4,11,64]{2,1,0:T(8,128)S(1)} %all-gather.1), channel_id=1, source_target_pairs={{16,0},{20,4},{24,8},{28,12},{32,16},{36,20},{40,24},{44,28},{48,3... | collective-permute-start | bytes 33800 | tf_op jit(solution)/shard_map/ppermute | solution.py:35
  86.9 5.6 %collective-permute-start.1 = (f32[11,512]{1,0:T(8,128)S(1)}, f32[11,512]{1,0:T(8,128)S(1)}, u32[]{:S(2)}, u32[]{:S(2)}) collective-permute-start(f32[11,512]{1,0:T(8,128)S(1)} %get-tuple-element.52), channel_id=1, source_target_pairs={{1,0},{2,1},{3,2},{4,3},{5,4},{6,5},{7,6},{8,7},{9,8},{10,9},{11,1... | collective-permute-start | bytes 67592 | tf_op jit(solution)/shard_map/ppermute | solution.py:25
  92.6 1.9 %collective-permute-start = (f32[11,512]{1,0:T(8,128)S(1)}, f32[11,512]{1,0:T(8,128)S(1)}, u32[]{:S(2)}, u32[]{:S(2)}) collective-permute-start(f32[11,512]{1,0:T(8,128)S(1)} %get-tuple-element.51), channel_id=1, source_target_pairs={{0,1},{1,2},{2,3},{3,4},{4,5},{5,6},{6,7},{7,8},{8,9},{9,10},{10,1... | collective-permute-start | bytes 67592 | tf_op jit(solution)/shard_map/ppermute | solution.py:23
  94.5 9.1 %collective-permute-start.3 = (f32[6,11,64]{2,1,0:T(8,128)S(1)}, f32[6,11,64]{2,1,0:T(8,128)S(1)}, u32[]{:S(2)}, u32[]{:S(2)}) collective-permute-start(f32[6,11,64]{2,1,0:T(8,128)S(1)} %get-tuple-element.81), channel_id=1, source_target_pairs={{1,0},{2,1},{3,2},{4,3},{5,4},{6,5},{7,6},{8,7},{9,8},{10,9},{11,1... | collective-permute-start | bytes 50696 | tf_op jit(solution)/shard_map/ppermute | solution.py:25
  103.6 2.1 %collective-permute-start.2 = (f32[6,11,64]{2,1,0:T(8,128)S(1)}, f32[6,11,64]{2,1,0:T(8,128)S(1)}, u32[]{:S(2)}, u32[]{:S(2)}) collective-permute-start(f32[6,11,64]{2,1,0:T(8,128)S(1)} %get-tuple-element.80), channel_id=1, source_target_pairs={{0,1},{1,2},{2,3},{3,4},{4,5},{5,6},{6,7},{7,8},{8,9},{9,10},{10,1... | collective-permute-start | bytes 50696 | tf_op jit(solution)/shard_map/ppermute | solution.py:23
  106.5 0.8 fusion.10
  107.3 7.1 %collective-permute-done.2 = f32[6,11,64]{2,1,0:T(8,128)S(1)} collective-permute-done((f32[6,11,64]{2,1,0:T(8,128)S(1)}, f32[6,11,64]{2,1,0:T(8,128)S(1)}, u32[]{:S(2)}, u32[]{:S(2)}) %collective-permute-start.2) | collective-permute-done | bytes 16928 | tf_op jit(solution)/shard_map/ppermute | solution.py:23
  120.2 1.2 fusion.99
  121.4 1.2 convolution_add_fusion.7
  122.6 1.2 convolution_add_fusion.6
  123.8 1.2 convolution_add_fusion.5
  125.0 1.2 convolution_add_fusion.4
  126.2 1.2 convolution_add_fusion.3
  127.3 1.2 convolution_add_fusion.2
  128.5 1.2 convolution_add_fusion.1
  129.7 1.3 fusion.9
  135.1 3.2 %fusion = f32[16,8,256]{2,1,0:T(8,128)S(1)} fusion(f32[16,256]{1,0:T(8,128)S(1)} %get-tuple-element.135, f32[16,256]{1,0:T(8,128)S(1)} %get-tuple-element.137, f32[16,256]{1,0:T(8,128)S(1)} %get-tuple-element.136, f32[16,256]{1,0:T(8,128)S(1)} %get-tuple-element.138, f32[16,256]{1,0:T(8,128)S(1)} %get-tuple-element.139, ...), kind=kOutput, calls=%fused_computation.22 | convolution fusion | flops 28377088 | bytes 360960 | tf_op jit(solution)/shard_map/glp,gpq->glq/dot_general | solution.py:107
  138.4 3.2 %fusion.8 = f32[16,8,256]{2,1,0:T(8,128)S(1)} fusion(f32[16,8,256]{2,1,0:T(8,128)S(1)} %fusion, f32[16,256]{1,0:T(8,128)S(1)} %bitcast.227, f32[16,256]{1,0:T(8,128)S(1)} %bitcast.228, f32[16,256]{1,0:T(8,128)S(1)} %bitcast.229, f32[16,256]{1,0:T(8,128)S(1)} %get-tuple-element.135, f32[16,256]{1,0:T(8,128)S(1)} %get-tuple-element.136, ...), kind=kOutput, calls=%fused_computation.31 | convolution fusion | flops 28409856 | bytes 492032 | tf_op jit(solution)/shard_map/glp,gpq->glq/dot_general | solution.py:107
  141.6 3.2 %fusion.7 = f32[16,8,256]{2,1,0:T(8,128)S(1)} fusion(f32[16,8,256]{2,1,0:T(8,128)S(1)} %fusion.8, f32[16,256]{1,0:T(8,128)S(1)} %bitcast.230, f32[16,256]{1,0:T(8,128)S(1)} %bitcast.231, f32[16,256]{1,0:T(8,128)S(1)} %bitcast.232, f32[16,256]{1,0:T(8,128)S(1)} %get-tuple-element.135, f32[16,256]{1,0:T(8,128)S(1)} %get-tuple-element.136, ...), kind=kOutput, calls=%fused_computation.30 | convolution fusion | flops 28409856 | bytes 492032 | tf_op jit(solution)/shard_map/glp,gpq->glq/dot_general | solution.py:107
  144.8 3.2 %fusion.6 = f32[16,8,256]{2,1,0:T(8,128)S(1)} fusion(f32[16,8,256]{2,1,0:T(8,128)S(1)} %fusion.7, f32[16,256]{1,0:T(8,128)S(1)} %bitcast.233, f32[16,256]{1,0:T(8,128)S(1)} %bitcast.234, f32[16,256]{1,0:T(8,128)S(1)} %bitcast.235, f32[16,256]{1,0:T(8,128)S(1)} %get-tuple-element.135, f32[16,256]{1,0:T(8,128)S(1)} %get-tuple-element.136, ...), kind=kOutput, calls=%fused_computation.29 | convolution fusion | flops 28409856 | bytes 492032 | tf_op jit(solution)/shard_map/glp,gpq->glq/dot_general | solution.py:107
  148.1 3.2 %fusion.5 = f32[16,8,256]{2,1,0:T(8,128)S(1)} fusion(f32[16,8,256]{2,1,0:T(8,128)S(1)} %fusion.6, f32[16,256]{1,0:T(8,128)S(1)} %bitcast.236, f32[16,256]{1,0:T(8,128)S(1)} %bitcast.237, f32[16,256]{1,0:T(8,128)S(1)} %bitcast.238, f32[16,256]{1,0:T(8,128)S(1)} %get-tuple-element.135, f32[16,256]{1,0:T(8,128)S(1)} %get-tuple-element.136, ...), kind=kOutput, calls=%fused_computation.28 | convolution fusion | flops 28409856 | bytes 492032 | tf_op jit(solution)/shard_map/glp,gpq->glq/dot_general | solution.py:107
  151.3 1.0 convolution_add_fusion
  (211 shorter events, 12.1 us)
Async XLA Ops:
  0.0 15.4 %copy-start = (bf16[16,64,256]{2,1,0:T(8,128)(2,1)S(1)}, bf16[16,64,256]{2,1,0:T(8,128)(2,1)}, u32[]{:S(2)}) copy-start(bf16[16,64,256]{2,1,0:T(8,128)(2,1)} %param.17) | copy-start | bytes 1572868
  0.0 15.4 %copy-start.7 = (f32[1,3,64]{2,0,1:T(1,128)S(1)}, f32[1,3,64]{2,0,1:T(1,128)}, u32[]{:S(2)}) copy-start(f32[1,3,64]{2,0,1:T(1,128)} %param.20) | copy-start | bytes 2308
  0.0 15.7 %copy-start.1 = (f32[16,64,64]{2,1,0:T(8,128)S(1)}, f32[16,64,64]{2,1,0:T(8,128)}, u32[]{:S(2)}) copy-start(f32[16,64,64]{2,1,0:T(8,128)} %param.18) | copy-start | bytes 786436
  15.0 34.7 %copy-start.2 = (f32[16,3,64]{2,0,1:T(8,128)S(1)}, f32[16,3,64]{2,0,1:T(8,128)}, u32[]{:S(2)}) copy-start(f32[16,3,64]{2,0,1:T(8,128)} %param.19) | copy-start | bytes 36868
  15.0 35.4 %copy-start.6 = (s32[16,5]{0,1:T(8,128)S(1)}, s32[16,5]{0,1:T(8,128)}, u32[]{:S(2)}) copy-start(s32[16,5]{0,1:T(8,128)} %param.21) | copy-start | bytes 964
  15.0 36.6 %copy-start.4 = (s32[16,8]{0,1:T(8,128)S(1)}, s32[16,8]{0,1:T(8,128)}, u32[]{:S(2)}) copy-start(s32[16,8]{0,1:T(8,128)} %param.22) | copy-start | bytes 1540
  15.0 37.8 %copy-start.8 = (f32[1,3,64]{2,0,1:T(1,128)S(1)}, f32[1,3,64]{2,0,1:T(1,128)}, u32[]{:S(2)}) copy-start(f32[1,3,64]{2,0,1:T(1,128)} %param.20) | copy-start | bytes 2308
  15.1 38.4 %copy-start.53 = (s32[1,16]{1,0:T(1,128)S(1)}, s32[1,16]{1,0:T(1,128)}, u32[]{:S(2)}) copy-start(s32[1,16]{1,0:T(1,128)} %param.23) | copy-start | bytes 196
  15.1 40.0 %copy-start.3 = (f32[3,4096]{1,0:T(4,128)S(1)}, f32[3,4096]{1,0:T(4,128)}, u32[]{:S(2)}) copy-start(f32[3,4096]{1,0:T(4,128)} %param.14) | copy-start | bytes 147460
  28.5 47.7 %collective-permute-start.4 = (f32[4,11,64]{2,1,0:T(8,128)S(1)}, f32[4,11,64]{2,1,0:T(8,128)}, u32[]{:S(2)}, u32[]{:S(2)}) collective-permute-start(f32[4,11,64]{2,1,0:T(8,128)S(1)} %all-gather.1), channel_id=1, source_target_pairs={{0,16},{4,20},{8,24},{12,28},{16,32},{20,36},{24,40},{28,44},{32,4... | collective-permute-start | bytes 33800 | tf_op jit(solution)/shard_map/ppermute | solution.py:35
  33.4 46.8 %collective-permute-start.5 = (f32[4,11,64]{2,1,0:T(8,128)S(1)}, f32[4,11,64]{2,1,0:T(8,128)S(1)}, u32[]{:S(2)}, u32[]{:S(2)}) collective-permute-start(f32[4,11,64]{2,1,0:T(8,128)S(1)} %all-gather.1), channel_id=1, source_target_pairs={{0,12},{4,16},{8,20},{12,24},{16,28},{20,32},{24,36},{28,40},{32,4... | collective-permute-start | bytes 33800 | tf_op jit(solution)/shard_map/ppermute | solution.py:35
  35.4 47.0 %collective-permute-start.6 = (f32[4,11,64]{2,1,0:T(8,128)S(1)}, f32[4,11,64]{2,1,0:T(8,128)S(1)}, u32[]{:S(2)}, u32[]{:S(2)}) collective-permute-start(f32[4,11,64]{2,1,0:T(8,128)S(1)} %all-gather.1), channel_id=1, source_target_pairs={{0,8},{4,12},{8,16},{12,20},{16,24},{20,28},{24,32},{28,36},{32,40... | collective-permute-start | bytes 33800 | tf_op jit(solution)/shard_map/ppermute | solution.py:35
  37.9 49.0 %collective-permute-start.7 = (f32[4,11,64]{2,1,0:T(8,128)S(1)}, f32[4,11,64]{2,1,0:T(8,128)S(1)}, u32[]{:S(2)}, u32[]{:S(2)}) collective-permute-start(f32[4,11,64]{2,1,0:T(8,128)S(1)} %all-gather.1), channel_id=1, source_target_pairs={{0,4},{4,8},{8,12},{12,16},{16,20},{20,24},{24,28},{28,32},{32,36}... | collective-permute-start | bytes 33800 | tf_op jit(solution)/shard_map/ppermute | solution.py:35
  41.5 51.1 %collective-permute-start.8 = (f32[4,11,64]{2,1,0:T(8,128)S(1)}, f32[4,11,64]{2,1,0:T(8,128)S(1)}, u32[]{:S(2)}, u32[]{:S(2)}) collective-permute-start(f32[4,11,64]{2,1,0:T(8,128)S(1)} %all-gather.1), channel_id=1, source_target_pairs={{4,0},{8,4},{12,8},{16,12},{20,16},{24,20},{28,24},{32,28},{36,32}... | collective-permute-start | bytes 33800 | tf_op jit(solution)/shard_map/ppermute | solution.py:35
  74.3 32.0 %copy-start.35 = (pred[16]{0:T(512)(128)(4,1)S(1)}, pred[16]{0:T(512)(128)(4,1)}, u32[]{:S(2)}) copy-start(pred[16]{0:T(512)(128)(4,1)} %compare_and_fusion.14) | copy-start | bytes 52
  74.3 32.2 %copy-start.50 = (f32[64]{0:T(128)S(1)}, f32[64]{0:T(128)}, u32[]{:S(2)}) copy-start(f32[64]{0:T(128)} %get-tuple-element.120) | copy-start | bytes 772
  74.3 32.2 %copy-start.51 = (f32[64]{0:T(128)S(1)}, f32[64]{0:T(128)}, u32[]{:S(2)}) copy-start(f32[64]{0:T(128)} %get-tuple-element.121) | copy-start | bytes 772
  74.3 32.2 %copy-start.52 = (f32[64]{0:T(128)S(1)}, f32[64]{0:T(128)}, u32[]{:S(2)}) copy-start(f32[64]{0:T(128)} %get-tuple-element.122) | copy-start | bytes 772
  74.3 32.2 %copy-start.54 = (f32[16]{0:T(128)S(1)}, f32[16]{0:T(128)}, u32[]{:S(2)}) copy-start(f32[16]{0:T(128)} %fusion.239) | copy-start | bytes 196
  75.9 39.2 %copy-start.21 = (pred[16]{0:T(512)(128)(4,1)S(1)}, pred[16]{0:T(512)(128)(4,1)}, u32[]{:S(2)}) copy-start(pred[16]{0:T(512)(128)(4,1)} %get-tuple-element.93) | copy-start | bytes 52
  75.9 39.9 %copy-start.20 = (pred[16]{0:T(512)(128)(4,1)S(1)}, pred[16]{0:T(512)(128)(4,1)}, u32[]{:S(2)}) copy-start(pred[16]{0:T(512)(128)(4,1)} %get-tuple-element.95) | copy-start | bytes 52
  76.2 18.3 %collective-permute-start.9 = (f32[4,11,64]{2,1,0:T(8,128)S(1)}, f32[4,11,64]{2,1,0:T(8,128)S(1)}, u32[]{:S(2)}, u32[]{:S(2)}) collective-permute-start(f32[4,11,64]{2,1,0:T(8,128)S(1)} %all-gather.1), channel_id=1, source_target_pairs={{8,0},{12,4},{16,8},{20,12},{24,16},{28,20},{32,24},{36,28},{40,32... | collective-permute-start | bytes 33800 | tf_op jit(solution)/shard_map/ppermute | solution.py:35
  80.2 23.4 %collective-permute-start.10 = (f32[4,11,64]{2,1,0:T(8,128)S(1)}, f32[4,11,64]{2,1,0:T(8,128)S(1)}, u32[]{:S(2)}, u32[]{:S(2)}) collective-permute-start(f32[4,11,64]{2,1,0:T(8,128)S(1)} %all-gather.1), channel_id=1, source_target_pairs={{12,0},{16,4},{20,8},{24,12},{28,16},{32,20},{36,24},{40,28},{44,3... | collective-permute-start | bytes 33800 | tf_op jit(solution)/shard_map/ppermute | solution.py:35
  82.4 23.4 %collective-permute-start.11 = (f32[4,11,64]{2,1,0:T(8,128)S(1)}, f32[4,11,64]{2,1,0:T(8,128)S(1)}, u32[]{:S(2)}, u32[]{:S(2)}) collective-permute-start(f32[4,11,64]{2,1,0:T(8,128)S(1)} %all-gather.1), channel_id=1, source_target_pairs={{16,0},{20,4},{24,8},{28,12},{32,16},{36,20},{40,24},{44,28},{48,3... | collective-permute-start | bytes 33800 | tf_op jit(solution)/shard_map/ppermute | solution.py:35
  86.9 44.1 %collective-permute-start.1 = (f32[11,512]{1,0:T(8,128)S(1)}, f32[11,512]{1,0:T(8,128)S(1)}, u32[]{:S(2)}, u32[]{:S(2)}) collective-permute-start(f32[11,512]{1,0:T(8,128)S(1)} %get-tuple-element.52), channel_id=1, source_target_pairs={{1,0},{2,1},{3,2},{4,3},{5,4},{6,5},{7,6},{8,7},{9,8},{10,9},{11,1... | collective-permute-start | bytes 67592 | tf_op jit(solution)/shard_map/ppermute | solution.py:25
  92.6 23.9 %copy-start.19 = (pred[16]{0:T(512)(128)(4,1)S(1)}, pred[16]{0:T(512)(128)(4,1)}, u32[]{:S(2)}) copy-start(pred[16]{0:T(512)(128)(4,1)} %get-tuple-element.97) | copy-start | bytes 52
  92.6 38.5 %collective-permute-start = (f32[11,512]{1,0:T(8,128)S(1)}, f32[11,512]{1,0:T(8,128)S(1)}, u32[]{:S(2)}, u32[]{:S(2)}) collective-permute-start(f32[11,512]{1,0:T(8,128)S(1)} %get-tuple-element.51), channel_id=1, source_target_pairs={{0,1},{1,2},{2,3},{3,4},{4,5},{5,6},{6,7},{7,8},{8,9},{9,10},{10,1... | collective-permute-start | bytes 67592 | tf_op jit(solution)/shard_map/ppermute | solution.py:23
  94.5 12.8 %collective-permute-start.3 = (f32[6,11,64]{2,1,0:T(8,128)S(1)}, f32[6,11,64]{2,1,0:T(8,128)S(1)}, u32[]{:S(2)}, u32[]{:S(2)}) collective-permute-start(f32[6,11,64]{2,1,0:T(8,128)S(1)} %get-tuple-element.81), channel_id=1, source_target_pairs={{1,0},{2,1},{3,2},{4,3},{5,4},{6,5},{7,6},{8,7},{9,8},{10,9},{11,1... | collective-permute-start | bytes 50696 | tf_op jit(solution)/shard_map/ppermute | solution.py:25
  103.6 10.8 %collective-permute-start.2 = (f32[6,11,64]{2,1,0:T(8,128)S(1)}, f32[6,11,64]{2,1,0:T(8,128)S(1)}, u32[]{:S(2)}, u32[]{:S(2)}) collective-permute-start(f32[6,11,64]{2,1,0:T(8,128)S(1)} %get-tuple-element.80), channel_id=1, source_target_pairs={{0,1},{1,2},{2,3},{3,4},{4,5},{5,6},{6,7},{7,8},{8,9},{9,10},{10,1... | collective-permute-start | bytes 50696 | tf_op jit(solution)/shard_map/ppermute | solution.py:23
  106.3 10.9 %copy-start.18 = (pred[16]{0:T(512)(128)(4,1)S(1)}, pred[16]{0:T(512)(128)(4,1)}, u32[]{:S(2)}) copy-start(pred[16]{0:T(512)(128)(4,1)} %get-tuple-element.99) | copy-start | bytes 52
  106.5 11.4 %copy-start.17 = (pred[16]{0:T(512)(128)(4,1)S(1)}, pred[16]{0:T(512)(128)(4,1)}, u32[]{:S(2)}) copy-start(pred[16]{0:T(512)(128)(4,1)} %get-tuple-element.101) | copy-start | bytes 52
  107.3 11.3 %copy-start.16 = (pred[16]{0:T(512)(128)(4,1)S(1)}, pred[16]{0:T(512)(128)(4,1)}, u32[]{:S(2)}) copy-start(pred[16]{0:T(512)(128)(4,1)} %get-tuple-element.103) | copy-start | bytes 52
  107.3 12.0 %copy-start.15 = (pred[16]{0:T(512)(128)(4,1)S(1)}, pred[16]{0:T(512)(128)(4,1)}, u32[]{:S(2)}) copy-start(pred[16]{0:T(512)(128)(4,1)} %get-tuple-element.105) | copy-start | bytes 52
  114.5 5.5 %copy-start.14 = (pred[16]{0:T(512)(128)(4,1)S(1)}, pred[16]{0:T(512)(128)(4,1)}, u32[]{:S(2)}) copy-start(pred[16]{0:T(512)(128)(4,1)} %get-tuple-element.6) | copy-start | bytes 52
  115.2 5.0 %copy-start.5 = (f32[16,64]{1,0:T(8,128)S(1)}, f32[16,64]{1,0:T(8,128)}, u32[]{:S(2)}) copy-start(f32[16,64]{1,0:T(8,128)} %get-tuple-element.84) | copy-start | bytes 12292
  115.2 5.0 %copy-start.48 = (f32[16]{0:T(128)S(1)}, f32[16]{0:T(128)}, u32[]{:S(2)}) copy-start(f32[16]{0:T(128)} %get-tuple-element.86) | copy-start | bytes 196
  117.2 4.2 %copy-start.47 = (f32[16]{0:T(128)S(1)}, f32[16]{0:T(128)}, u32[]{:S(2)}) copy-start(f32[16]{0:T(128)} %get-tuple-element.87) | copy-start | bytes 196
  118.7 3.8 %copy-start.46 = (f32[16]{0:T(128)S(1)}, f32[16]{0:T(128)}, u32[]{:S(2)}) copy-start(f32[16]{0:T(128)} %get-tuple-element.88) | copy-start | bytes 196
  120.2 3.6 %copy-start.45 = (f32[16]{0:T(128)S(1)}, f32[16]{0:T(128)}, u32[]{:S(2)}) copy-start(f32[16]{0:T(128)} %get-tuple-element.89) | copy-start | bytes 196
  121.4 3.6 %copy-start.44 = (f32[16]{0:T(128)S(1)}, f32[16]{0:T(128)}, u32[]{:S(2)}) copy-start(f32[16]{0:T(128)} %get-tuple-element.90) | copy-start | bytes 196
  122.6 3.6 %copy-start.43 = (f32[16]{0:T(128)S(1)}, f32[16]{0:T(128)}, u32[]{:S(2)}) copy-start(f32[16]{0:T(128)} %get-tuple-element.91) | copy-start | bytes 196
  123.8 3.6 %copy-start.42 = (f32[16]{0:T(128)S(1)}, f32[16]{0:T(128)}, u32[]{:S(2)}) copy-start(f32[16]{0:T(128)} %get-tuple-element.92) | copy-start | bytes 196
  125.0 3.6 %copy-start.41 = (f32[16]{0:T(128)S(1)}, f32[16]{0:T(128)}, u32[]{:S(2)}) copy-start(f32[16]{0:T(128)} %get-tuple-element.85) | copy-start | bytes 196
  128.5 3.4 %copy-start.13 = (pred[16]{0:T(512)(128)(4,1)S(1)}, pred[16]{0:T(512)(128)(4,1)}, u32[]{:S(2)}) copy-start(pred[16]{0:T(512)(128)(4,1)} %get-tuple-element.118) | copy-start | bytes 52
  135.1 3.2 %copy-start.39 = (f32[16]{0:T(128)S(1)}, f32[16]{0:T(128)}, u32[]{:S(2)}) copy-start(f32[16]{0:T(128)} %get-tuple-element.109) | copy-start | bytes 196
  138.4 3.2 %copy-start.38 = (f32[16]{0:T(128)S(1)}, f32[16]{0:T(128)}, u32[]{:S(2)}) copy-start(f32[16]{0:T(128)} %get-tuple-element.110) | copy-start | bytes 196
  141.6 3.2 %copy-start.37 = (f32[16]{0:T(128)S(1)}, f32[16]{0:T(128)}, u32[]{:S(2)}) copy-start(f32[16]{0:T(128)} %get-tuple-element.111) | copy-start | bytes 196
  144.8 3.2 %copy-start.36 = (f32[16]{0:T(128)S(1)}, f32[16]{0:T(128)}, u32[]{:S(2)}) copy-start(f32[16]{0:T(128)} %get-tuple-element.107) | copy-start | bytes 196
  (19 other events, 47.4 us)
where the time goes:
time: 153 us; the launch traced here: 152 us
  starting transfers between devices  46.9 us (31%)
  local copies, waits for them, and re-layouts  41.5 us (27%)
  matrix products  29.2 us (19%)
  other arithmetic  13.4 us (9%)
  blocking collectives  12.4 us (8%)
  waiting for transfers between devices  7.18 us (5%)
  between operations  1.67 us (1%)
    ppermute x8, starting transfers between devices, passed_along(): lax.ppermute(value, axis, [(source, source + steps) for source in range(i...  28.2 us
    dot_general x5, matrix products, shards(): jnp.einsum('glp,gpq->glq', weights, dense, preferred_element_type=jnp.flo...  16.1 us
    ppermute x2, starting transfers between devices, extended(): lax.ppermute(head, axis, [((i + 1) % count, i) for i in range(ends)])  14.6 us
    gather x1, local copies, waits for them, and re-layouts, shards(): tree_points = jnp.take(points, order, axis=1)  14.2 us
    gather x2, local copies, waits for them, and re-layouts, shards(): tree_charges = jnp.take(charges, order, axis=1)  12.4 us
    all_gather x1, blocking collectives, shards(): group_table = lax.all_gather(cluster_entry, 'sub', axis=0, tiled=True)  12.4 us
    dot_general x8, matrix products, shards(): jnp.einsum('glr,grs->gls', picked[:, :nrhs] * keep_mask, coupling_matrix,...  9.36 us
    ppermute x2, waiting for transfers between devices, extended(): lax.ppermute(tail, axis, [(i, (i + 1) % count) for i in range(ends)])  7.16 us
  transfers between devices with their start and end apart: 12, of which 1 were waited for; matrix products, arithmetic and copies ran while one was open for 31% of the time, Pallas kernels for 0%

commit v1 on v0

v1 whole, which is shorter than its diff:
```python
import jax
import jax.numpy as jnp
from jax import lax
from jax.experimental import pallas as pl
from jax.experimental.pallas import tpu as pltpu
from jax.sharding import PartitionSpec as P

LEAF = 256
RANK = 64
NRHS = 8
OWN = 16
REACH = 2
FREACH = 6
PLANE = 8
HALF = PLANE // 2
NSUB = 4
PTS = OWN * LEAF
RANKS = OWN * RANK
LANES = 128
SCALE = 16.0
SHIFT = 2.56

NEAR_W = REACH * LEAF
FAR_W = FREACH * RANK
MSG = 2 * NEAR_W + 2 * FAR_W
AT_CHARGES, AT_POINTS, AT_COEFFS, AT_PROXY = 0, PTS, 2 * PTS, 2 * PTS + RANKS
OWN_W = 2 * PTS + 2 * RANKS

NT = (((1,), (1,)), ((), ()))
NN = (((1,), (0,)), ((), ()))


def dot(a, b, dims=NN):
    return lax.dot_general(a, b, dims, preferred_element_type=jnp.float32)


def split(x):
    high = x.astype(jnp.bfloat16)
    return high, (x - high.astype(jnp.float32)).astype(jnp.bfloat16)


def dot3(a, b, dims=NN):
    rows = a.shape[0]
    a_high, a_low = split(a)
    b_high, b_low = split(b)
    both = dot(jnp.concatenate([a_high, a_low], axis=0), b_high, dims)
    return both[:rows] + both[rows:] + dot(a_high, b_low, dims)


def prepare_kernel(
    charges, points, order, basis, transfer, leaf_proxy, cluster_proxy,
    own, right, left, entry, source,
):
    source[0:NRHS, :] = charges[...].astype(jnp.float32)
    source[NRHS : 2 * NRHS, :] = jnp.zeros((NRHS, PTS), jnp.float32)
    source[NRHS : NRHS + 3, :] = points[...] * SCALE

    def gather(block, carry):
        index = jnp.broadcast_to(order[pl.ds(block, 1), :], (8, LANES))
        high = lax.shift_right_logical(index, 7)
        low = jnp.bitwise_and(index, LANES - 1)
        lanes = pl.ds(pl.multiple_of(block * LANES, LANES), LANES)
        got = [None, None]
        for k in range(PTS // LANES):
            here = high == k
            for part in range(2):
                piece = source[8 * part : 8 * part + 8, k * LANES : (k + 1) * LANES]
                piece = jnp.take_along_axis(piece, low, axis=1)
                got[part] = piece if k == 0 else jnp.where(here, piece, got[part])
        own[:, lanes] = got[0]
        own[:, pl.ds(pl.multiple_of(PTS + block * LANES, LANES), LANES)] = got[1]
        return carry

    lax.fori_loop(0, PTS // LANES, gather, 0)

    own[:, AT_PROXY : AT_PROXY + RANKS] = jnp.zeros((8, RANKS), jnp.float32)
    for g in range(OWN):
        at = AT_PROXY + g * RANK
        own[0:3, at : at + RANK] = leaf_proxy[:, g, :] * SCALE

    first_half = lax.broadcasted_iota(jnp.int32, (NRHS, LANES), 1) < RANK
    parent = jnp.zeros((NRHS, RANK), jnp.float32)
    for m in range(OWN // 2):
        a = own[:, 2 * m * LEAF : (2 * m + 1) * LEAF].astype(jnp.bfloat16)
        b = own[:, (2 * m + 1) * LEAF : (2 * m + 2) * LEAF].astype(jnp.bfloat16)
        weights = jnp.reshape(basis[2 * m : 2 * m + 2], (2 * RANK, LEAF))
        pair = dot(jnp.concatenate([a, b], axis=0), weights, NT)
        coeffs = jnp.where(first_half, pair[:NRHS], pair[NRHS:])
        own[:, AT_COEFFS + m * LANES : AT_COEFFS + (m + 1) * LANES] = coeffs
        parent += dot3(coeffs, jnp.reshape(transfer[2 * m : 2 * m + 2], (2 * RANK, RANK)))

    entry[...] = jnp.zeros((NRHS, LANES), jnp.float32)
    entry[:, 0:RANK] = parent
    entry[0:3, RANK : 2 * RANK] = cluster_proxy[:, 0, :] * SCALE

    at = 0
    for start, whole, width in (
        (AT_CHARGES, PTS, NEAR_W), (AT_POINTS, PTS, NEAR_W),
        (AT_COEFFS, RANKS, FAR_W), (AT_PROXY, RANKS, FAR_W),
    ):
        left[:, at : at + width] = own[:, start : start + width]
        right[:, at : at + width] = own[:, start + whole - width : start + whole]
        at += width


def block_values(columns, rows):
    d0 = columns[0] - rows[0]
    d1 = columns[1] - rows[1]
    d2 = columns[2] - rows[2]
    return lax.rsqrt(d0 * d0 + d1 * d1 + d2 * d2 + SHIFT)


def product_kernel(
    near, far_cluster, far_leaf, own, from_left, from_right, table, cluster_proxy, transfer, basis,
    out,
    charges, points, coeffs, proxies, point_columns, proxy_columns, block, leaf_block, total, down,
    far_rows,
):
    group, member = lax.axis_index("leaf"), lax.axis_index("sub")
    cluster = group * NSUB + member
    first = cluster * OWN

    at = 0
    for window, start, whole, width in (
        (charges, AT_CHARGES, PTS, NEAR_W), (points, AT_POINTS, PTS, NEAR_W),
        (coeffs, AT_COEFFS, RANKS, FAR_W), (proxies, AT_PROXY, RANKS, FAR_W),
    ):
        window[:, 0:width] = from_left[:, at : at + width].astype(window.dtype)
        window[:, width : width + whole] = own[:, start : start + whole].astype(window.dtype)
        window[:, width + whole : 2 * width + whole] = from_right[:, at : at + width].astype(window.dtype)
        at += width
    for t in range(points.shape[1] // LANES):
        point_columns[t * LANES : (t + 1) * LANES, :] = points[:, t * LANES : (t + 1) * LANES].T
    for t in range(proxies.shape[1] // LANES):
        proxy_columns[t * LANES : (t + 1) * LANES, :] = proxies[:, t * LANES : (t + 1) * LANES].T

    total[...] = jnp.zeros_like(total)

    def listed(target, h):
        hit = near[0, target] == first + h
        for slot in range(1, near.shape[0]):
            hit = jnp.logical_or(hit, near[slot, target] == first + h)
        return hit.astype(jnp.float32)

    def strip(h, rows_at, lanes_at, width):
        rows = [points[c : c + 1, pl.ds(lanes_at, width)] for c in range(3)]
        step = 16
        for r in range(0, LEAF, step):
            column = point_columns[pl.ds(rows_at + r, step), :]
            values = block_values([column[:, c : c + 1] for c in range(3)], rows)
            block[r : r + step, 0:width] = values.astype(jnp.bfloat16)

    def near_leaf(h, carry):
        here = pl.multiple_of((h + REACH) * LEAF, LEAF)
        strip(h, here, here, (REACH + 1) * LEAF)
        forward = dot(charges[:, pl.ds(here, LEAF)], block[...])
        reverse = forward[:, 0:LEAF] * listed(h, h)
        for d in range(1, REACH + 1):
            there = pl.multiple_of((h + d + REACH) * LEAF, LEAF)
            lanes = slice(d * LEAF, (d + 1) * LEAF)
            total[:, pl.ds(there, LEAF)] += forward[:, lanes] * listed(jnp.minimum(h + d, OWN - 1), h)
            reverse += dot(charges[:, pl.ds(there, LEAF)], block[:, lanes], NT) * listed(h, h + d)
        total[:, pl.ds(here, LEAF)] += reverse
        return carry

    lax.fori_loop(0, OWN, near_leaf, 0)
    for h in range(-REACH, 0):
        width = (h + REACH + 1) * LEAF
        strip(h, (h + REACH) * LEAF, REACH * LEAF, width)
        forward = dot(charges[:, (h + REACH) * LEAF : (h + REACH + 1) * LEAF], block[:, 0:width])
        for g in range(h + REACH + 1):
            total[:, (g + REACH) * LEAF : (g + REACH + 1) * LEAF] += (
                forward[:, g * LEAF : (g + 1) * LEAF] * listed(g, h)
            )

    span = 3 * LANES
    first_lanes = lax.broadcasted_iota(jnp.int32, (NRHS, LANES), 1) < RANK
    down[...] = jnp.zeros_like(down)
    lists = far_leaf[...] - first + FREACH
    lists = jnp.where(far_leaf[...] >= 0, lists, -1)
    far_rows[...] = jnp.full_like(far_rows, -1)
    for m in range(OWN // 2):
        at = FAR_W + m * LANES
        far_rows[:, at : at + LANES] = jnp.where(
            first_lanes,
            jnp.broadcast_to(lists[:, 2 * m : 2 * m + 1], (8, LANES)),
            jnp.broadcast_to(lists[:, 2 * m + 1 : 2 * m + 2], (8, LANES)),
        )
    lane_leaf = lax.broadcasted_iota(jnp.int32, (8, span), 1) // RANK
    for m in range((FREACH + OWN) // 2):
        at = m * LANES
        to = at + LANES
        rows = [proxies[c : c + 1, to : to + span] for c in range(3)]
        for r in range(0, LANES, 32):
            column = proxy_columns[at + r : at + r + 32, :]
            leaf_block[r : r + 32, :] = block_values([column[:, c : c + 1] for c in range(3)], rows)
        high, low = split(leaf_block[...])
        pair = coeffs[:, at : at + LANES]
        sources = jnp.concatenate(
            [jnp.where(first_lanes, pair, 0.0), jnp.where(first_lanes, 0.0, pair)], axis=0
        )
        s_high, s_low = split(sources)
        both = dot(jnp.concatenate([s_high, s_low], axis=0), high)
        forward = both[:16] + both[16:] + dot(s_high, low)
        for i in range(2):
            hit = jnp.max((far_rows[:, to : to + span] == 2 * m + i).astype(jnp.float32), axis=0, keepdims=True)
            down[:, to : to + span] += forward[8 * i : 8 * i + 8] * hit
        if 2 * m >= FREACH:
            targets = coeffs[:, to : to + span]
            masked = []
            for i in range(2):
                column = lists[:, 2 * m + i - FREACH : 2 * m + i - FREACH + 1]
                hit = jnp.max((lane_leaf + (2 * m + 2) == column).astype(jnp.float32), axis=0, keepdims=True)
                masked.append(targets * hit)
            t_high, t_low = split(jnp.concatenate(masked, axis=0))
            both = dot(jnp.concatenate([t_high, t_low], axis=0), high, NT)
            reverse = both[:16] + both[16:] + dot(t_high, low, NT)
            down[:, at : at + LANES] += jnp.where(first_lanes, reverse[:8], reverse[8:])

    plane = group // PLANE
    entries, kept = [], []
    for slot in range(far_cluster.shape[1]):
        f = far_cluster[0, slot]
        valid = f >= 0
        f = jnp.where(valid, f, cluster)
        mine = f // (PLANE * NSUB) == plane
        place = lax.rem(f + jnp.where(mine, 0, HALF * NSUB), PLANE * NSUB)
        row = pl.multiple_of(jnp.where(mine, 0, NRHS), NRHS)
        e = table[place, pl.ds(row, NRHS), :]
        entries.append(e)
        kept.append(e * valid.astype(jnp.float32))
    parents, sources = [], []
    for m in range(len(entries) // 2):
        a, b = 2 * m, 2 * m + 1
        parents.append(jnp.where(first_lanes, kept[a], pltpu.roll(kept[b], RANK, 1)))
        sources.append(jnp.where(first_lanes, pltpu.roll(entries[a], RANK, 1), entries[b]))
    parents = jnp.concatenate(parents, axis=1)
    sources = jnp.concatenate(sources, axis=1)
    mine = jnp.concatenate([cluster_proxy[:, 0, :] * SCALE, jnp.zeros((5, RANK), jnp.float32)], axis=0)
    mine = jnp.concatenate([mine, mine], axis=1).T[:RANK]
    values = block_values(
        [mine[:, c : c + 1] for c in range(3)], [sources[c : c + 1, :] for c in range(3)]
    )
    coupled = dot3(parents, values, NT)

    for m in range(OWN // 2):
        weights = jnp.reshape(transfer[2 * m : 2 * m + 2], (2 * RANK, RANK))
        at = FAR_W + m * LANES
        pair = down[:, at : at + LANES] + dot3(coupled, weights, NT)
        d_high, d_low = split(
            jnp.concatenate([jnp.where(first_lanes, pair, 0.0), jnp.where(first_lanes, 0.0, pair)], axis=0)
        )
        both = dot(
            jnp.concatenate([d_high, d_low], axis=0), jnp.reshape(basis[2 * m : 2 * m + 2], (2 * RANK, LEAF))
        )
        far = both[:16] + both[16:]
        for i in range(2):
            at = (2 * m + i) * LEAF
            out[:, at : at + LEAF] = total[:, NEAR_W + at : NEAR_W + at + LEAF] + far[8 * i : 8 * i + 8]


def shards(
    points, charges, order, basis, transfer, leaf_proxy, cluster_proxy, near, far_leaf, far_cluster
):
    vmem = pl.BlockSpec(memory_space=pltpu.VMEM)
    smem = pl.BlockSpec(memory_space=pltpu.SMEM)
    f32 = jnp.float32
    leaf_proxy = leaf_proxy.transpose(1, 0, 2)
    cluster_proxy = cluster_proxy.transpose(1, 0, 2)
    own, right, left, entry = pl.pallas_call(
        prepare_kernel,
        in_specs=[vmem] * 7,
        out_specs=[vmem] * 4,
        out_shape=[
            jax.ShapeDtypeStruct((8, OWN_W), f32),
            jax.ShapeDtypeStruct((8, MSG), f32),
            jax.ShapeDtypeStruct((8, MSG), f32),
            jax.ShapeDtypeStruct((NRHS, LANES), f32),
        ],
        scratch_shapes=[pltpu.VMEM((2 * NRHS, PTS), f32)],
        compiler_params=pltpu.CompilerParams(vmem_limit_bytes=32 * 2**20),
        name="prepare",
    )(charges, points, order.reshape(PTS // LANES, LANES), basis, transfer, leaf_proxy, cluster_proxy)

    axes = ("leaf", "sub")
    groups, count = lax.axis_size("leaf"), lax.axis_size(axes)
    swap = []
    for start in range(HALF, groups - HALF, PLANE):
        for i in range(HALF):
            swap += [(start + i, start + HALF + i), (start + HALF + i, start + i)]
    partner = lax.ppermute(entry, "leaf", swap)
    from_left = lax.ppermute(right, axes, [(i, i + 1) for i in range(count - 1)])
    from_right = lax.ppermute(left, axes, [(i + 1, i) for i in range(count - 1)])
    size = PLANE * NSUB
    table = lax.all_to_all(
        jnp.broadcast_to(jnp.concatenate([entry, partner], axis=0), (size, 2 * NRHS, LANES)),
        axes, 0, 0, tiled=True,
        axis_index_groups=[list(range(i, i + size)) for i in range(0, count, size)],
    )

    window = OWN + 2 * REACH
    far_window = OWN + 2 * FREACH
    return pl.pallas_call(
        product_kernel,
        in_specs=[smem, smem] + [vmem] * 8,
        out_specs=vmem,
        out_shape=jax.ShapeDtypeStruct((NRHS, PTS), f32),
        scratch_shapes=[
            pltpu.VMEM((8, window * LEAF), jnp.bfloat16),
            pltpu.VMEM((8, window * LEAF), f32),
            pltpu.VMEM((8, far_window * RANK), f32),
            pltpu.VMEM((8, far_window * RANK), f32),
            pltpu.VMEM((window * LEAF, 8), f32),
            pltpu.VMEM((far_window * RANK, 8), f32),
            pltpu.VMEM((LEAF, (REACH + 1) * LEAF), jnp.bfloat16),
            pltpu.VMEM((2 * RANK, 3 * LANES), f32),
            pltpu.VMEM((NRHS, window * LEAF), f32),
            pltpu.VMEM((NRHS, far_window * RANK), f32),
            pltpu.VMEM((8, far_window * RANK), jnp.int32),
        ],
        compiler_params=pltpu.CompilerParams(vmem_limit_bytes=32 * 2**20),
        name="product",
    )(
        near.transpose(1, 0), far_cluster, far_leaf.transpose(1, 0), own, from_left, from_right, table,
        cluster_proxy, transfer, basis,
    )


def solution(mesh):
    in_specs = (
        P(None, ("leaf", "sub")),
        P(None, ("leaf", "sub")),
        P(("leaf", "sub")),
        P(("leaf", "sub"), None, None),
        P(("leaf", "sub"), None, None),
        P(("leaf", "sub"), None, None),
        P(("leaf", "sub"), None, None),
        P(("leaf", "sub"), None),
        P(("leaf", "sub"), None),
        P(("leaf", "sub"), None),
    )
    out_specs = P(None, ("leaf", "sub"))
    return jax.shard_map(shards, mesh=mesh, in_specs=in_specs, out_specs=out_specs, check_vma=False)
```

time: 153 us -> 58.7 us (0.38)
  the two profiles are of different devices: /device:TPU:384 before, /device:TPU:255 now
where the time goes in v1:
time: 58.7 us; the launch traced here: 58.1 us
  starting transfers between devices  19.8 us (34%)
  Pallas kernels  19.6 us (33%)
  waiting for transfers between devices  11.4 us (19%)
  local copies, waits for them, and re-layouts  7.25 us (12%)
    pallas_call x1, Pallas kernels, shards(): pl.pallas_call(product_kernel, in_specs=[smem, smem] + [vmem] * 8, out_sp...  14.6 us
    all_to_all x1, starting transfers between devices, shards(): lax.all_to_all(jnp.broadcast_to(jnp.concatenate([entry, partner], axis=0)...  8.76 us
    ppermute x1, waiting for transfers between devices, shards(): lax.ppermute(left, axes, [(i + 1, i) for i in range(count - 1)])  8.71 us
    unnamed x24, local copies, waits for them, and re-layouts  6.53 us
    ppermute x1, starting transfers between devices, shards(): partner = lax.ppermute(entry, 'leaf', swap)  5.73 us
    pallas_call x1, Pallas kernels, shards(): pl.pallas_call(prepare_kernel, in_specs=[vmem] * 7, out_specs=[vmem] * 4,...  5 us
    ppermute x1, starting transfers between devices, shards(): lax.ppermute(right, axes, [(i, i + 1) for i in range(count - 1)])  3.39 us
    ppermute x1, waiting for transfers between devices, shards(): partner = lax.ppermute(entry, 'leaf', swap)  2.36 us
  transfers between devices with their start and end apart: 4, of which 3 were waited for; matrix products, arithmetic and copies ran while one was open for 0% of the time, Pallas kernels for 0%

profile of v1, /device:TPU:255, one launch (start us, length us, event | category | flops | bytes accessed | tf_op | source)
XLA Modules:
  0.0 58.1 jit_solution(11927901539406951709)
XLA Ops:
  0.0 0.0 copy-start.8
  0.0 0.7 %copy-done.8 = f32[1,3,64]{2,0,1:T(1,128)S(1)} copy-done((f32[1,3,64]{2,0,1:T(1,128)S(1)}, f32[1,3,64]{2,0,1:T(1,128)}, u32[]{:S(2)}) %copy-start.8) | copy-done | bytes 792
  0.7 0.0 copy-start
  0.7 1.0 %copy-done = bf16[16,64,256]{2,1,0:T(8,128)(2,1)S(1)} copy-done((bf16[16,64,256]{2,1,0:T(8,128)(2,1)S(1)}, bf16[16,64,256]{2,1,0:T(8,128)(2,1)}, u32[]{:S(2)}) %copy-start) | copy-done | bytes 524312
  1.7 0.0 copy-start.2
  1.7 1.0 %copy-done.2 = f32[16,64,64]{2,1,0:T(8,128)S(1)} copy-done((f32[16,64,64]{2,1,0:T(8,128)S(1)}, f32[16,64,64]{2,1,0:T(8,128)}, u32[]{:S(2)}) %copy-start.2) | copy-done | bytes 262168
  2.8 0.0 copy-start.4
  2.8 0.8 %copy-done.4 = bf16[8,4096]{1,0:T(8,128)(2,1)S(1)} copy-done((bf16[8,4096]{1,0:T(8,128)(2,1)S(1)}, bf16[8,4096]{1,0:T(8,128)(2,1)}, u32[]{:S(2)}) %copy-start.4) | copy-done | bytes 65560
  3.6 0.0 copy-start.5
  3.6 0.8 %copy-done.5 = f32[3,4096]{1,0:T(4,128)S(1)} copy-done((f32[3,4096]{1,0:T(4,128)S(1)}, f32[3,4096]{1,0:T(4,128)}, u32[]{:S(2)}) %copy-start.5) | copy-done | bytes 49176
  4.4 0.0 copy-start.6
  4.4 0.7 %copy-done.6 = f32[16,3,64]{2,0,1:T(8,128)S(1)} copy-done((f32[16,3,64]{2,0,1:T(8,128)S(1)}, f32[16,3,64]{2,0,1:T(8,128)}, u32[]{:S(2)}) %copy-start.6) | copy-done | bytes 12312
  5.2 0.0 copy-start.7
  5.2 0.7 %copy-done.7 = s32[4096]{0:T(1024)S(1)} copy-done((s32[4096]{0:T(1024)S(1)}, s32[4096]{0:T(1024)}, u32[]{:S(2)}) %copy-start.7) | copy-done | bytes 16408
  5.9 0.0 copy-start.3
  5.9 5.0 %prepare.1 = (f32[8,10240]{1,0:T(8,128)S(1)}, f32[8,1792]{1,0:T(8,128)S(1)}, f32[8,1792]{1,0:T(8,128)S(1)}, f32[8,128]{1,0:T(8,128)S(1)}) custom-call(bf16[8,4096]{1,0:T(8,128)(2,1)S(1)} %copy-done.4, f32[3,4096]{1,0:T(4,128)S(1)} %copy-done.5, s32[32,128]{1,0:T(8,128)S(1)} %bitcast.6, bf16[16,64,256]{2,1,0:T(8,128)(2,1)S(1)} %copy-done, ...), custom_call_target="tpu_custom_call" | custom-call | tf_op jit(solution)/shard_map/prepare/pallas_call | solution.py:270
  10.9 0.0 copy-start.1
  10.9 5.7 %collective-permute-start.2 = (f32[8,128]{1,0:T(8,128)S(1)}, f32[8,128]{1,0:T(8,128)S(1)}, u32[]{:S(2)}, u32[]{:S(2)}) collective-permute-start(f32[8,128]{1,0:T(8,128)S(1)} %get-tuple-element.12), channel_id=1, source_target_pairs={{16,32},{32,16},{20,36},{36,20},{24,40},{40,24},{28,44},{44,28},{4... | collective-permute-start | bytes 12296 | tf_op jit(solution)/shard_map/ppermute | solution.py:291
  16.6 2.4 %collective-permute-done.2 = f32[8,128]{1,0:T(8,128)S(1)} collective-permute-done((f32[8,128]{1,0:T(8,128)S(1)}, f32[8,128]{1,0:T(8,128)S(1)}, u32[]{:S(2)}, u32[]{:S(2)}) %collective-permute-start.2) | collective-permute-done | bytes 4128 | tf_op jit(solution)/shard_map/ppermute | solution.py:291
  19.0 0.7 %broadcast_in_dim.3 = f32[32,16,128]{2,1,0:T(8,128)} broadcast(f32[16,128]{1,0:T(8,128)S(1)} %pad_maximum_fusion), dimensions={1,2} | broadcast | bytes 270336 | tf_op jit(solution)/shard_map/broadcast_in_dim | solution.py:296
  19.7 8.8 %all-to-all-start = ((f32[32,16,128]{2,1,0:T(8,128)}), f32[32,16,128]{2,1,0:T(8,128)S(1)}, u32[]{:S(2)}, u32[]{:S(2)}) async-start(f32[32,16,128]{2,1,0:T(8,128)} %broadcast_in_dim.3), calls=%async_computation | async-start | bytes 524288 | tf_op jit(solution)/shard_map/all_to_all | solution.py:295
  28.5 0.0 copy-start.10
  28.5 0.0 copy-start.9
  28.5 3.4 %collective-permute-start = (f32[8,1792]{1,0:T(8,128)S(1)}, f32[8,1792]{1,0:T(8,128)S(1)}, u32[]{:S(2)}, u32[]{:S(2)}) collective-permute-start(f32[8,1792]{1,0:T(8,128)S(1)} %get-tuple-element.10), channel_id=1, source_target_pairs={{0,1},{1,2},{2,3},{3,4},{4,5},{5,6},{6,7},{7,8},{8,9},{9,10},{10,1... | collective-permute-start | bytes 172040 | tf_op jit(solution)/shard_map/ppermute | solution.py:292
  31.9 1.9 %collective-permute-start.1 = (f32[8,1792]{1,0:T(8,128)S(1)}, f32[8,1792]{1,0:T(8,128)S(1)}, u32[]{:S(2)}, u32[]{:S(2)}) collective-permute-start(f32[8,1792]{1,0:T(8,128)S(1)} %get-tuple-element.11), channel_id=1, source_target_pairs={{1,0},{2,1},{3,2},{4,3},{5,4},{6,5},{7,6},{8,7},{9,8},{10,9},{11,1... | collective-permute-start | bytes 172040 | tf_op jit(solution)/shard_map/ppermute | solution.py:293
  33.8 0.3 collective-permute-done.from_left
  34.1 8.7 %collective-permute-done.1.from_right = f32[8,1792]{1,0:T(8,128)S(1)} collective-permute-done((f32[8,1792]{1,0:T(8,128)S(1)}, f32[8,1792]{1,0:T(8,128)S(1)}, u32[]{:S(2)}, u32[]{:S(2)}) %collective-permute-start.1) | collective-permute-done | bytes 57376 | tf_op jit(solution)/shard_map/ppermute | solution.py:293
  42.8 0.0 all-to-all-done.table
  42.8 0.0 copy-start.11
  42.8 0.0 copy-done.3
  42.8 0.0 copy-done.1
  42.9 0.0 copy-done.10
  42.9 0.0 copy-done.9
  42.9 0.6 %copy-done.11 = s32[1,16]{1,0:T(1,128)S(1)} copy-done((s32[1,16]{1,0:T(1,128)S(1)}, s32[1,16]{1,0:T(1,128)}, u32[]{:S(2)}) %copy-start.11) | copy-done | bytes 88
  43.5 14.6 %product.1 = f32[8,4096]{1,0:T(8,128)} custom-call(s32[5,16]{1,0:T(8,128)S(1)} %bitcast.9, s32[1,16]{1,0:T(1,128)S(1)} %copy-done.11, s32[8,16]{1,0:T(8,128)S(1)} %bitcast.10, f32[8,10240]{1,0:T(8,128)S(1)} %get-tuple-element.9.own, f32[8,1792]{1,0:T(8,128)S(1)} %collective-permute-done.from_left, f32[8,1792]{1,0:T(8,128)S(1)} %collective-permute-done.1.from_right, ...), custom_call_target="tpu_custom_call" | custom-call | tf_op jit(solution)/shard_map/product/pallas_call | solution.py:303
  (1 shorter events, 0.0 us)
Async XLA Ops:
  0.0 0.7 %copy-start.8 = (f32[1,3,64]{2,0,1:T(1,128)S(1)}, f32[1,3,64]{2,0,1:T(1,128)}, u32[]{:S(2)}) copy-start(f32[1,3,64]{2,0,1:T(1,128)} %param.16) | copy-start | bytes 2308
  0.7 1.0 %copy-start = (bf16[16,64,256]{2,1,0:T(8,128)(2,1)S(1)}, bf16[16,64,256]{2,1,0:T(8,128)(2,1)}, u32[]{:S(2)}) copy-start(bf16[16,64,256]{2,1,0:T(8,128)(2,1)} %basis.3) | copy-start | bytes 1572868
  1.7 1.0 %copy-start.2 = (f32[16,64,64]{2,1,0:T(8,128)S(1)}, f32[16,64,64]{2,1,0:T(8,128)}, u32[]{:S(2)}) copy-start(f32[16,64,64]{2,1,0:T(8,128)} %transfer.3) | copy-start | bytes 786436
  2.8 0.8 %copy-start.4 = (bf16[8,4096]{1,0:T(8,128)(2,1)S(1)}, bf16[8,4096]{1,0:T(8,128)(2,1)}, u32[]{:S(2)}) copy-start(bf16[8,4096]{1,0:T(8,128)(2,1)} %charges.1) | copy-start | bytes 196612
  3.6 0.8 %copy-start.5 = (f32[3,4096]{1,0:T(4,128)S(1)}, f32[3,4096]{1,0:T(4,128)}, u32[]{:S(2)}) copy-start(f32[3,4096]{1,0:T(4,128)} %points.1) | copy-start | bytes 147460
  4.4 0.7 %copy-start.6 = (f32[16,3,64]{2,0,1:T(8,128)S(1)}, f32[16,3,64]{2,0,1:T(8,128)}, u32[]{:S(2)}) copy-start(f32[16,3,64]{2,0,1:T(8,128)} %param.15) | copy-start | bytes 36868
  5.2 0.7 %copy-start.7 = (s32[4096]{0:T(1024)S(1)}, s32[4096]{0:T(1024)}, u32[]{:S(2)}) copy-start(s32[4096]{0:T(1024)} %param.12) | copy-start | bytes 49156
  5.9 36.9 %copy-start.3 = (f32[16,64,64]{2,1,0:T(8,128)S(1)}, f32[16,64,64]{2,1,0:T(8,128)}, u32[]{:S(2)}) copy-start(f32[16,64,64]{2,1,0:T(8,128)} %transfer.3) | copy-start | bytes 786436
  10.9 31.9 %copy-start.1 = (bf16[16,64,256]{2,1,0:T(8,128)(2,1)S(1)}, bf16[16,64,256]{2,1,0:T(8,128)(2,1)}, u32[]{:S(2)}) copy-start(bf16[16,64,256]{2,1,0:T(8,128)(2,1)} %basis.3) | copy-start | bytes 1572868
  10.9 8.1 %collective-permute-start.2 = (f32[8,128]{1,0:T(8,128)S(1)}, f32[8,128]{1,0:T(8,128)S(1)}, u32[]{:S(2)}, u32[]{:S(2)}) collective-permute-start(f32[8,128]{1,0:T(8,128)S(1)} %get-tuple-element.12), channel_id=1, source_target_pairs={{16,32},{32,16},{20,36},{36,20},{24,40},{40,24},{28,44},{44,28},{4... | collective-permute-start | bytes 12296 | tf_op jit(solution)/shard_map/ppermute | solution.py:291
  19.7 23.1 %all-to-all-start = ((f32[32,16,128]{2,1,0:T(8,128)}), f32[32,16,128]{2,1,0:T(8,128)S(1)}, u32[]{:S(2)}, u32[]{:S(2)}) async-start(f32[32,16,128]{2,1,0:T(8,128)} %broadcast_in_dim.3), calls=%async_computation | async-start | bytes 524288 | tf_op jit(solution)/shard_map/all_to_all | solution.py:295
  28.5 14.4 %copy-start.10 = (s32[16,8]{0,1:T(8,128)S(1)}, s32[16,8]{0,1:T(8,128)}, u32[]{:S(2)}) copy-start(s32[16,8]{0,1:T(8,128)} %param.18) | copy-start | bytes 1540
  28.5 14.4 %copy-start.9 = (s32[16,5]{0,1:T(8,128)S(1)}, s32[16,5]{0,1:T(8,128)}, u32[]{:S(2)}) copy-start(s32[16,5]{0,1:T(8,128)} %param.17) | copy-start | bytes 964
  28.5 5.6 %collective-permute-start = (f32[8,1792]{1,0:T(8,128)S(1)}, f32[8,1792]{1,0:T(8,128)S(1)}, u32[]{:S(2)}, u32[]{:S(2)}) collective-permute-start(f32[8,1792]{1,0:T(8,128)S(1)} %get-tuple-element.10), channel_id=1, source_target_pairs={{0,1},{1,2},{2,3},{3,4},{4,5},{5,6},{6,7},{7,8},{8,9},{9,10},{10,1... | collective-permute-start | bytes 172040 | tf_op jit(solution)/shard_map/ppermute | solution.py:292
  31.9 10.9 %collective-permute-start.1 = (f32[8,1792]{1,0:T(8,128)S(1)}, f32[8,1792]{1,0:T(8,128)S(1)}, u32[]{:S(2)}, u32[]{:S(2)}) collective-permute-start(f32[8,1792]{1,0:T(8,128)S(1)} %get-tuple-element.11), channel_id=1, source_target_pairs={{1,0},{2,1},{3,2},{4,3},{5,4},{6,5},{7,6},{8,7},{9,8},{10,9},{11,1... | collective-permute-start | bytes 172040 | tf_op jit(solution)/shard_map/ppermute | solution.py:293
  42.8 0.7 %copy-start.11 = (s32[1,16]{1,0:T(1,128)S(1)}, s32[1,16]{1,0:T(1,128)}, u32[]{:S(2)}) copy-start(s32[1,16]{1,0:T(1,128)} %far_cluster.1) | copy-start | bytes 196

commit v2 on v1

v2 whole, which is shorter than its diff:
```python
import jax
import jax.numpy as jnp
from jax import lax
from jax.experimental import pallas as pl
from jax.experimental.pallas import tpu as pltpu
from jax.sharding import PartitionSpec as P

LEAF = 256
RANK = 64
NRHS = 8
OWN = 16
REACH = 2
FREACH = 6
PLANE = 8
HALF = PLANE // 2
NSUB = 4
PTS = OWN * LEAF
RANKS = OWN * RANK
LANES = 128
SCALE = 16.0
SHIFT = 2.56

NEAR_W = REACH * LEAF
FAR_W = FREACH * RANK
MSG = 2 * NEAR_W + 2 * FAR_W
AT_CHARGES, AT_POINTS, AT_COEFFS, AT_PROXY = 0, PTS, 2 * PTS, 2 * PTS + RANKS
OWN_W = 2 * PTS + 2 * RANKS

NT = (((1,), (1,)), ((), ()))
NN = (((1,), (0,)), ((), ()))


def dot(a, b, dims=NN):
    return lax.dot_general(a, b, dims, preferred_element_type=jnp.float32)


def split(x):
    high = x.astype(jnp.bfloat16)
    return high, (x - high.astype(jnp.float32)).astype(jnp.bfloat16)


def dot3(a, b, dims=NN):
    rows = a.shape[0]
    a_high, a_low = split(a)
    b_high, b_low = split(b)
    both = dot(jnp.concatenate([a_high, a_low], axis=0), b_high, dims)
    return both[:rows] + both[rows:] + dot(a_high, b_low, dims)


def prepare_kernel(
    charges, points, order, basis, transfer, leaf_proxy, cluster_proxy,
    own, right, left, spread,
    source, entry, charges_in, points_in, order_in, basis_in, transfer_in, leaf_proxy_in, cluster_proxy_in, sems,
):
    copies = [
        pltpu.make_async_copy(a, b, sems.at[i])
        for i, (a, b) in enumerate(
            (
                (order, order_in), (charges, charges_in), (points, points_in), (leaf_proxy, leaf_proxy_in),
                (cluster_proxy, cluster_proxy_in), (basis, basis_in), (transfer, transfer_in),
            )
        )
    ]
    for copy in copies:
        copy.start()
    own[:, AT_PROXY : AT_PROXY + RANKS] = jnp.zeros((8, RANKS), jnp.float32)
    entry[...] = jnp.zeros((NRHS, LANES), jnp.float32)
    source[NRHS : 2 * NRHS, :] = jnp.zeros((NRHS, PTS), jnp.float32)
    for copy in copies[:3]:
        copy.wait()
    source[0:NRHS, :] = charges_in[...].astype(jnp.float32)
    source[NRHS : NRHS + 3, :] = points_in[...] * SCALE

    def gather(block, carry):
        index = jnp.broadcast_to(order_in[pl.ds(block, 1), :], (8, LANES))
        high = lax.shift_right_logical(index, 7)
        low = jnp.bitwise_and(index, LANES - 1)
        lanes = pl.ds(pl.multiple_of(block * LANES, LANES), LANES)
        got = [None, None]
        for k in range(PTS // LANES):
            here = high == k
            for part in range(2):
                piece = source[8 * part : 8 * part + 8, k * LANES : (k + 1) * LANES]
                piece = jnp.take_along_axis(piece, low, axis=1)
                got[part] = piece if k == 0 else jnp.where(here, piece, got[part])
        own[:, lanes] = got[0]
        own[:, pl.ds(pl.multiple_of(PTS + block * LANES, LANES), LANES)] = got[1]
        return carry

    lax.fori_loop(0, PTS // LANES, gather, 0)

    for copy in copies[3:]:
        copy.wait()
    for g in range(OWN):
        at = AT_PROXY + g * RANK
        own[0:3, at : at + RANK] = leaf_proxy_in[:, g, :] * SCALE

    first_half = lax.broadcasted_iota(jnp.int32, (NRHS, LANES), 1) < RANK
    parent = jnp.zeros((NRHS, RANK), jnp.float32)
    for m in range(OWN // 2):
        a = own[:, 2 * m * LEAF : (2 * m + 1) * LEAF].astype(jnp.bfloat16)
        b = own[:, (2 * m + 1) * LEAF : (2 * m + 2) * LEAF].astype(jnp.bfloat16)
        weights = jnp.reshape(basis_in[2 * m : 2 * m + 2], (2 * RANK, LEAF))
        pair = dot(jnp.concatenate([a, b], axis=0), weights, NT)
        coeffs = jnp.where(first_half, pair[:NRHS], pair[NRHS:])
        own[:, AT_COEFFS + m * LANES : AT_COEFFS + (m + 1) * LANES] = coeffs
        parent += dot3(coeffs, jnp.reshape(transfer_in[2 * m : 2 * m + 2], (2 * RANK, RANK)))

    entry[:, 0:RANK] = parent
    entry[0:3, RANK : 2 * RANK] = cluster_proxy_in[:, 0, :] * SCALE

    for place in range(PLANE * NSUB):
        spread[place] = entry[...]

    at = 0
    for start, whole, width in (
        (AT_CHARGES, PTS, NEAR_W), (AT_POINTS, PTS, NEAR_W),
        (AT_COEFFS, RANKS, FAR_W), (AT_PROXY, RANKS, FAR_W),
    ):
        left[:, at : at + width] = own[:, start : start + width]
        right[:, at : at + width] = own[:, start + whole - width : start + whole]
        at += width


def block_values(columns, rows):
    d0 = columns[0] - rows[0]
    d1 = columns[1] - rows[1]
    d2 = columns[2] - rows[2]
    return lax.rsqrt(d0 * d0 + d1 * d1 + d2 * d2 + SHIFT)


def strip(columns, rows, block):
    step = 16
    for r in range(0, LEAF, step):
        column = columns[r : r + step, :]
        values = block_values([column[:, c : c + 1] for c in range(3)], rows)
        block[r : r + step, 0 : values.shape[1]] = values.astype(jnp.bfloat16)


def listing(near, first):
    def listed(target, h):
        hit = near[0, target] == first + h
        for slot in range(1, near.shape[0]):
            hit = jnp.logical_or(hit, near[slot, target] == first + h)
        return hit.astype(jnp.float32)

    return listed


def near_kernel(near_list, own, total, charges, columns, block, near, sem):
    copy = pltpu.make_async_copy(near_list, near, sem)
    copy.start()
    first = (lax.axis_index("leaf") * NSUB + lax.axis_index("sub")) * OWN
    listed = listing(near, first)
    charges[...] = own[:, 0:PTS].astype(jnp.bfloat16)
    for t in range(PTS // LANES):
        columns[t * LANES : (t + 1) * LANES, :] = own[:, PTS + t * LANES : PTS + (t + 1) * LANES].T
    total[...] = jnp.zeros_like(total)
    copy.wait()

    def leaf(h, reach, block):
        here = h * LEAF
        if not isinstance(h, int):
            here = pl.multiple_of(here, LEAF)
        lanes_at = PTS + here
        if not isinstance(h, int):
            lanes_at = pl.multiple_of(lanes_at, LEAF)
        rows = [own[c : c + 1, pl.ds(lanes_at, (reach + 1) * LEAF)] for c in range(3)]
        strip(columns.at[pl.ds(here, LEAF), :], rows, block)
        forward = dot(charges[:, pl.ds(here, LEAF)], block[:, 0 : (reach + 1) * LEAF])
        reverse = forward[:, 0:LEAF] * listed(h, h)
        for d in range(1, reach + 1):
            there = (h + d) * LEAF
            if not isinstance(h, int):
                there = pl.multiple_of(there, LEAF)
            lanes = slice(d * LEAF, (d + 1) * LEAF)
            total[:, pl.ds(there, LEAF)] += forward[:, lanes] * listed(h + d, h)
            reverse += dot(charges[:, pl.ds(there, LEAF)], block[:, lanes], NT) * listed(h, h + d)
        total[:, pl.ds(here, LEAF)] += reverse

    def pair(i, carry):
        for k in range(2):
            leaf(2 * i + k, REACH, block.at[k])
        return carry

    lax.fori_loop(0, (OWN - REACH) // 2, pair, 0)
    for h in range(OWN - REACH, OWN):
        leaf(h, OWN - 1 - h, block.at[h % 2])


def product_kernel(
    near_list, leaf_list, cluster_list, cluster_proxy_list, transfer, basis,
    own, from_left, from_right, total, table, beyond,
    out,
    coeffs, proxies, edge_columns, proxy_columns, block, leaf_block, down, far_rows,
    near, far_leaf, far_cluster, cluster_proxy, transfer_in, basis_in, sems,
):
    copies = [
        pltpu.make_async_copy(a, b, sems.at[i])
        for i, (a, b) in enumerate(
            (
                (near_list, near), (leaf_list, far_leaf), (cluster_list, far_cluster),
                (cluster_proxy_list, cluster_proxy), (transfer, transfer_in), (basis, basis_in),
            )
        )
    ]
    for copy in copies:
        copy.start()
    group = lax.axis_index("leaf")
    cluster = group * NSUB + lax.axis_index("sub")
    first = cluster * OWN

    at = 2 * NEAR_W
    for window, start, whole, width in (
        (coeffs, AT_COEFFS, RANKS, FAR_W), (proxies, AT_PROXY, RANKS, FAR_W),
    ):
        window[:, 0:width] = from_left[:, at : at + width]
        window[:, width : width + whole] = own[:, start : start + whole]
        window[:, width + whole : 2 * width + whole] = from_right[:, at : at + width]
        at += width
    for t in range(proxies.shape[1] // LANES):
        proxy_columns[t * LANES : (t + 1) * LANES, :] = proxies[:, t * LANES : (t + 1) * LANES].T

    for copy in copies[:4]:
        copy.wait()
    listed = listing(near, first)
    out[...] = total[...]
    for side, message in enumerate((from_left, from_right)):
        for t in range(NEAR_W // LANES):
            edge_columns[t * LANES : (t + 1) * LANES, :] = message[
                :, NEAR_W + t * LANES : NEAR_W + (t + 1) * LANES
            ].T
        for i in range(REACH):
            h = i - REACH if side == 0 else OWN + i
            targets = [g for g in range(OWN) if abs(g - h) <= REACH]
            at, width = targets[0] * LEAF, len(targets) * LEAF
            rows = [own[c : c + 1, PTS + at : PTS + at + width] for c in range(3)]
            strip(edge_columns.at[i * LEAF : (i + 1) * LEAF, :], rows, block.at[i])
            sources = message[:, i * LEAF : (i + 1) * LEAF].astype(jnp.bfloat16)
            forward = dot(sources, block[i, :, 0:width])
            for k, g in enumerate(targets):
                out[:, g * LEAF : (g + 1) * LEAF] += forward[:, k * LEAF : (k + 1) * LEAF] * listed(g, h)

    span = 3 * LANES
    first_lanes = lax.broadcasted_iota(jnp.int32, (NRHS, LANES), 1) < RANK
    down[...] = jnp.zeros_like(down)
    lists = far_leaf[...] - first + FREACH
    lists = jnp.where(far_leaf[...] >= 0, lists, -1)
    far_rows[...] = jnp.full_like(far_rows, -1)
    for m in range(OWN // 2):
        at = FAR_W + m * LANES
        far_rows[:, at : at + LANES] = jnp.where(
            first_lanes,
            jnp.broadcast_to(lists[:, 2 * m : 2 * m + 1], (8, LANES)),
            jnp.broadcast_to(lists[:, 2 * m + 1 : 2 * m + 2], (8, LANES)),
        )
    lane_leaf = lax.broadcasted_iota(jnp.int32, (8, span), 1) // RANK
    for m in range((FREACH + OWN) // 2):
        at = m * LANES
        to = at + LANES
        rows = [proxies[c : c + 1, to : to + span] for c in range(3)]
        for r in range(0, LANES, 32):
            column = proxy_columns[at + r : at + r + 32, :]
            leaf_block[r : r + 32, :] = block_values([column[:, c : c + 1] for c in range(3)], rows)
        high, low = split(leaf_block[...])
        pair = coeffs[:, at : at + LANES]
        sources = jnp.concatenate(
            [jnp.where(first_lanes, pair, 0.0), jnp.where(first_lanes, 0.0, pair)], axis=0
        )
        s_high, s_low = split(sources)
        both = dot(jnp.concatenate([s_high, s_low], axis=0), high)
        forward = both[:16] + both[16:] + dot(s_high, low)
        for i in range(2):
            hit = jnp.max((far_rows[:, to : to + span] == 2 * m + i).astype(jnp.float32), axis=0, keepdims=True)
            down[:, to : to + span] += forward[8 * i : 8 * i + 8] * hit
        if 2 * m >= FREACH:
            targets = coeffs[:, to : to + span]
            masked = []
            for i in range(2):
                column = lists[:, 2 * m + i - FREACH : 2 * m + i - FREACH + 1]
                hit = jnp.max((lane_leaf + (2 * m + 2) == column).astype(jnp.float32), axis=0, keepdims=True)
                masked.append(targets * hit)
            t_high, t_low = split(jnp.concatenate(masked, axis=0))
            both = dot(jnp.concatenate([t_high, t_low], axis=0), high, NT)
            reverse = both[:16] + both[16:] + dot(t_high, low, NT)
            down[:, at : at + LANES] += jnp.where(first_lanes, reverse[:8], reverse[8:])

    plane = group // PLANE
    entries, kept = [], []
    for slot in range(far_cluster.shape[1]):
        f = far_cluster[0, slot]
        valid = f >= 0
        f = jnp.where(valid, f, cluster)
        mine = f // (PLANE * NSUB) == plane
        place = lax.rem(f, PLANE * NSUB)
        e = jnp.where(mine, table[place], beyond[place])
        entries.append(e)
        kept.append(e * valid.astype(jnp.float32))
    parents, sources = [], []
    for m in range(len(entries) // 2):
        a, b = 2 * m, 2 * m + 1
        parents.append(jnp.where(first_lanes, kept[a], pltpu.roll(kept[b], RANK, 1)))
        sources.append(jnp.where(first_lanes, pltpu.roll(entries[a], RANK, 1), entries[b]))
    parents = jnp.concatenate(parents, axis=1)
    sources = jnp.concatenate(sources, axis=1)
    mine = jnp.concatenate([cluster_proxy[:, 0, :] * SCALE, jnp.zeros((5, RANK), jnp.float32)], axis=0)
    mine = jnp.concatenate([mine, mine], axis=1).T[:RANK]
    values = block_values(
        [mine[:, c : c + 1] for c in range(3)], [sources[c : c + 1, :] for c in range(3)]
    )
    coupled = dot3(parents, values, NT)

    for copy in copies[4:]:
        copy.wait()
    for m in range(OWN // 2):
        weights = jnp.reshape(transfer_in[2 * m : 2 * m + 2], (2 * RANK, RANK))
        at = FAR_W + m * LANES
        pair = down[:, at : at + LANES] + dot3(coupled, weights, NT)
        d_high, d_low = split(
            jnp.concatenate([jnp.where(first_lanes, pair, 0.0), jnp.where(first_lanes, 0.0, pair)], axis=0)
        )
        both = dot(
            jnp.concatenate([d_high, d_low], axis=0), jnp.reshape(basis_in[2 * m : 2 * m + 2], (2 * RANK, LEAF))
        )
        far = both[:16] + both[16:]
        for i in range(2):
            at = (2 * m + i) * LEAF
            out[:, at : at + LEAF] += far[8 * i : 8 * i + 8]


def shards(
    points, charges, order, basis, transfer, leaf_proxy, cluster_proxy, near, far_leaf, far_cluster
):
    vmem = pl.BlockSpec(memory_space=pltpu.VMEM)
    smem = pl.BlockSpec(memory_space=pltpu.SMEM)
    hbm = pl.BlockSpec(memory_space=pltpu.HBM)
    params = pltpu.CompilerParams(vmem_limit_bytes=48 * 2**20)
    f32 = jnp.float32
    leaf_proxy = leaf_proxy.transpose(1, 0, 2)
    cluster_proxy = cluster_proxy.transpose(1, 0, 2)
    near, far_leaf = near.transpose(1, 0), far_leaf.transpose(1, 0)
    given = (charges, points, order.reshape(PTS // LANES, LANES), basis, transfer, leaf_proxy, cluster_proxy)
    size = PLANE * NSUB
    own, right, left, spread = pl.pallas_call(
        prepare_kernel,
        in_specs=[hbm] * 7,
        out_specs=[vmem] * 4,
        out_shape=[
            jax.ShapeDtypeStruct((8, OWN_W), f32),
            jax.ShapeDtypeStruct((8, MSG), f32),
            jax.ShapeDtypeStruct((8, MSG), f32),
            jax.ShapeDtypeStruct((size, NRHS, LANES), f32),
        ],
        scratch_shapes=[pltpu.VMEM((2 * NRHS, PTS), f32), pltpu.VMEM((NRHS, LANES), f32)]
        + [pltpu.VMEM(a.shape, a.dtype) for a in given]
        + [pltpu.SemaphoreType.DMA((7,))],
        name="prepare",
    )(*given)

    axes = ("leaf", "sub")
    groups, count = lax.axis_size("leaf"), lax.axis_size(axes)
    table = lax.all_to_all(
        spread, axes, 0, 0, tiled=True,
        axis_index_groups=[list(range(i, i + size)) for i in range(0, count, size)],
    )
    from_left = lax.ppermute(right, axes, [(i, i + 1) for i in range(count - 1)])
    from_right = lax.ppermute(left, axes, [(i + 1, i) for i in range(count - 1)])
    shift = [(g - PLANE, g) for g in range(PLANE, groups) if g % PLANE < HALF]
    shift += [(g + PLANE, g) for g in range(groups - PLANE) if g % PLANE >= HALF]
    beyond = lax.ppermute(table, "leaf", shift)
    total = pl.pallas_call(
        near_kernel,
        in_specs=[hbm, vmem],
        out_specs=vmem,
        out_shape=jax.ShapeDtypeStruct((NRHS, PTS), f32),
        scratch_shapes=[
            pltpu.VMEM((8, PTS), jnp.bfloat16),
            pltpu.VMEM((PTS, 8), f32),
            pltpu.VMEM((2, LEAF, (REACH + 1) * LEAF), jnp.bfloat16),
            pltpu.SMEM(near.shape, near.dtype),
            pltpu.SemaphoreType.DMA,
        ],
        cost_estimate=pl.CostEstimate(flops=9 * 10**9, bytes_accessed=10**6, transcendentals=3 * 10**6),
        compiler_params=params,
        name="near_field",
    )(near, own)
    far_window = OWN + 2 * FREACH
    return pl.pallas_call(
        product_kernel,
        in_specs=[hbm] * 6 + [vmem] * 6,
        out_specs=vmem,
        out_shape=jax.ShapeDtypeStruct((NRHS, PTS), f32),
        scratch_shapes=[
            pltpu.VMEM((8, far_window * RANK), f32),
            pltpu.VMEM((8, far_window * RANK), f32),
            pltpu.VMEM((NEAR_W, 8), f32),
            pltpu.VMEM((far_window * RANK, 8), f32),
            pltpu.VMEM((REACH, LEAF, REACH * LEAF), jnp.bfloat16),
            pltpu.VMEM((2 * RANK, 3 * LANES), f32),
            pltpu.VMEM((8, far_window * RANK), f32),
            pltpu.VMEM((8, far_window * RANK), jnp.int32),
            pltpu.SMEM(near.shape, near.dtype),
            pltpu.VMEM(far_leaf.shape, far_leaf.dtype),
            pltpu.SMEM(far_cluster.shape, far_cluster.dtype),
            pltpu.VMEM(cluster_proxy.shape, cluster_proxy.dtype),
            pltpu.VMEM(transfer.shape, transfer.dtype),
            pltpu.VMEM(basis.shape, basis.dtype),
            pltpu.SemaphoreType.DMA((6,)),
        ],
        compiler_params=params,
        name="product",
    )(
        near, far_leaf, far_cluster, cluster_proxy, transfer, basis,
        own, from_left, from_right, total, table, beyond,
    )


def solution(mesh):
    in_specs = (
        P(None, ("leaf", "sub")),
        P(None, ("leaf", "sub")),
        P(("leaf", "sub")),
        P(("leaf", "sub"), None, None),
        P(("leaf", "sub"), None, None),
        P(("leaf", "sub"), None, None),
        P(("leaf", "sub"), None, None),
        P(("leaf", "sub"), None),
        P(("leaf", "sub"), None),
        P(("leaf", "sub"), None),
    )
    out_specs = P(None, ("leaf", "sub"))
    return jax.shard_map(shards, mesh=mesh, in_specs=in_specs, out_specs=out_specs, check_vma=False)
```

time: 58.7 us -> 44.5 us (0.76)
  the two profiles are of different devices: /device:TPU:255 before, /device:TPU:96 now
where the time goes in v2:
time: 44.5 us; the launch traced here: 44.1 us
  starting transfers between devices  23.5 us (53%)
  Pallas kernels  18.8 us (42%)
  local copies, waits for them, and re-layouts  1.6 us (4%)
    all_to_all x1, starting transfers between devices, shards(): lax.all_to_all(spread, axes, 0, 0, tiled=True, axis_index_groups=[list(ra...  7.46 us
    pallas_call x1, Pallas kernels, shards(): pl.pallas_call(near_kernel, in_specs=[hbm, vmem], out_specs=vmem, out_sha...  7.08 us
    pallas_call x1, Pallas kernels, shards(): pl.pallas_call(prepare_kernel, in_specs=[hbm] * 7, out_specs=[vmem] * 4,...  6.71 us
    ppermute x1, starting transfers between devices, shards(): beyond = lax.ppermute(table, 'leaf', shift)  6.25 us
    ppermute x1, starting transfers between devices, shards(): lax.ppermute(left, axes, [(i + 1, i) for i in range(count - 1)])  6.08 us
    pallas_call x1, Pallas kernels, shards(): pl.pallas_call(product_kernel, in_specs=[hbm] * 6 + [vmem] * 6, out_specs...  5.03 us
    ppermute x1, starting transfers between devices, shards(): lax.ppermute(right, axes, [(i, i + 1) for i in range(count - 1)])  3.7 us
    unnamed x18, local copies, waits for them, and re-layouts  1.6 us
  transfers between devices with their start and end apart: 4, of which 0 were waited for; matrix products, arithmetic and copies ran while one was open for 0% of the time, Pallas kernels for 16%

profile of v2, /device:TPU:96, one launch (start us, length us, event | category | flops | bytes accessed | tf_op | source)
XLA Modules:
  0.0 44.1 jit_solution(10346071978663393095)
XLA Ops:
  0.0 6.7 %prepare.1 = (f32[8,10240]{1,0:T(8,128)}, f32[8,1792]{1,0:T(8,128)}, f32[8,1792]{1,0:T(8,128)}, f32[32,8,128]{2,1,0:T(8,128)}) custom-call(bf16[8,4096]{1,0:T(8,128)(2,1)} %charges.1, f32[3,4096]{1,0:T(4,128)} %points.1, s32[32,128]{1,0:T(8,128)} %bitcast.11, bf16[16,64,256]{2,1,0:T(8,128)(2,1)} %basis.3, f32[16,64,64]{2,1,0:T(8,128)} %transfer.3, ...), custom_call_target="tpu_custom_call" | custom-call | tf_op jit(solution)/shard_map/prepare/pallas_call | solution.py:344
  6.7 0.0 copy-start.8
  6.7 0.0 copy-start.7
  6.7 7.5 %all-to-all-start = ((f32[32,8,128]{2,1,0:T(8,128)}), f32[32,8,128]{2,1,0:T(8,128)S(1)}, u32[]{:S(2)}, u32[]{:S(2)}) async-start(f32[32,8,128]{2,1,0:T(8,128)} %get-tuple-element.12), calls=%async_computation | async-start | bytes 262144 | tf_op jit(solution)/shard_map/all_to_all | solution.py:362
  14.2 0.0 copy-start.4
  14.2 0.0 copy-done.8
  14.2 3.7 %collective-permute-start = (f32[8,1792]{1,0:T(8,128)S(1)}, f32[8,1792]{1,0:T(8,128)S(1)}, u32[]{:S(2)}, u32[]{:S(2)}) collective-permute-start(f32[8,1792]{1,0:T(8,128)S(1)} %copy-done.8), channel_id=1, source_target_pairs={{0,1},{1,2},{2,3},{3,4},{4,5},{5,6},{6,7},{7,8},{8,9},{9,10},{10,1... | collective-permute-start | bytes 172040 | tf_op jit(solution)/shard_map/ppermute | solution.py:366
  17.9 0.0 copy-done.7
  18.0 6.1 %collective-permute-start.1 = (f32[8,1792]{1,0:T(8,128)S(1)}, f32[8,1792]{1,0:T(8,128)S(1)}, u32[]{:S(2)}, u32[]{:S(2)}) collective-permute-start(f32[8,1792]{1,0:T(8,128)S(1)} %copy-done.7), channel_id=1, source_target_pairs={{1,0},{2,1},{3,2},{4,3},{5,4},{6,5},{7,6},{8,7},{9,8},{10,9},{11,1... | collective-permute-start | bytes 172040 | tf_op jit(solution)/shard_map/ppermute | solution.py:367
  24.0 0.0 all-to-all-done.table
  24.1 6.2 %collective-permute-start.2 = (f32[32,8,128]{2,1,0:T(8,128)S(1)}, f32[32,8,128]{2,1,0:T(8,128)S(1)}, u32[]{:S(2)}, u32[]{:S(2)}) collective-permute-start(f32[32,8,128]{2,1,0:T(8,128)S(1)} %all-to-all-done.table), channel_id=1, source_target_pairs={{0,32},{4,36},{8,40},{12,44},{32,64},{36,68},{40,72},{44,76},{64,9... | collective-permute-start | bytes 393224 | tf_op jit(solution)/shard_map/ppermute | solution.py:370
  30.3 0.0 copy-done.4
  30.3 0.0 copy-start.2
  30.3 1.0 %copy-done.2 = f32[8,10240]{1,0:T(8,128)S(1)} copy-done((f32[8,10240]{1,0:T(8,128)S(1)}, f32[8,10240]{1,0:T(8,128)}, u32[]{:S(2)}) %copy-start.2) | copy-done | bytes 327704
  31.3 0.0 copy-start
  31.3 0.0 copy-start.1
  31.3 0.0 copy-start.5
  31.3 0.0 copy-start.6
  31.3 7.1 %near_field.1.total = f32[8,4096]{1,0:T(8,128)S(1)} custom-call(s32[5,16]{1,0:T(8,128)S(1)} %bitcast.7, f32[8,10240]{1,0:T(8,128)S(1)} %copy-done.2), custom_call_target="tpu_custom_call" | custom-call | flops 8999999488 | bytes 1000000 | tf_op jit(solution)/shard_map/near_field/pallas_call | solution.py:371
  38.4 0.0 copy-start.3
  38.4 0.0 collective-permute-done.from_left
  38.4 0.0 collective-permute-done.1.from_right
  38.4 0.0 collective-permute-done.2.beyond
  38.4 0.0 copy-done
  38.4 0.0 copy-done.1
  38.5 0.0 copy-done.5
  38.5 0.0 copy-done.6
  38.5 0.6 %copy-done.3 = f32[1,3,64]{2,0,1:T(1,128)S(1)} copy-done((f32[1,3,64]{2,0,1:T(1,128)S(1)}, f32[1,3,64]{2,0,1:T(1,128)}, u32[]{:S(2)}) %copy-start.3) | copy-done | bytes 792
  39.1 5.0 %product.1 = f32[8,4096]{1,0:T(8,128)} custom-call(s32[5,16]{1,0:T(8,128)S(1)} %bitcast.8, s32[8,16]{1,0:T(8,128)S(1)} %bitcast.9, s32[1,16]{1,0:T(1,128)S(1)} %copy-done.6, f32[3,1,64]{2,1,0:T(1,128)S(1)} %bitcast.6, f32[16,64,64]{2,1,0:T(8,128)S(1)} %copy-done, bf16[16,64,256]{2,1,0:T(8,128)(2,1)S(1)} %copy-done.1, f32[8,10240]{1,0:T(8,128)S(1)} %copy-done.2, ...), custom_call_target="tpu_custom_call" | custom-call | tf_op jit(solution)/shard_map/product/pallas_call | solution.py:388
Async XLA Ops:
  6.7 7.5 %copy-start.8 = (f32[8,1792]{1,0:T(8,128)S(1)}, f32[8,1792]{1,0:T(8,128)}, u32[]{:S(2)}) copy-start(f32[8,1792]{1,0:T(8,128)} %get-tuple-element.10) | copy-start | bytes 172036
  6.7 11.2 %copy-start.7 = (f32[8,1792]{1,0:T(8,128)S(1)}, f32[8,1792]{1,0:T(8,128)}, u32[]{:S(2)}) copy-start(f32[8,1792]{1,0:T(8,128)} %get-tuple-element.11) | copy-start | bytes 172036
  6.7 17.3 %all-to-all-start = ((f32[32,8,128]{2,1,0:T(8,128)}), f32[32,8,128]{2,1,0:T(8,128)S(1)}, u32[]{:S(2)}, u32[]{:S(2)}) async-start(f32[32,8,128]{2,1,0:T(8,128)} %get-tuple-element.12), calls=%async_computation | async-start | bytes 262144 | tf_op jit(solution)/shard_map/all_to_all | solution.py:362
  14.2 16.1 %copy-start.4 = (s32[16,5]{0,1:T(8,128)S(1)}, s32[16,5]{0,1:T(8,128)}, u32[]{:S(2)}) copy-start(s32[16,5]{0,1:T(8,128)} %param.17) | copy-start | bytes 964
  14.2 24.2 %collective-permute-start = (f32[8,1792]{1,0:T(8,128)S(1)}, f32[8,1792]{1,0:T(8,128)S(1)}, u32[]{:S(2)}, u32[]{:S(2)}) collective-permute-start(f32[8,1792]{1,0:T(8,128)S(1)} %copy-done.8), channel_id=1, source_target_pairs={{0,1},{1,2},{2,3},{3,4},{4,5},{5,6},{6,7},{7,8},{8,9},{9,10},{10,1... | collective-permute-start | bytes 172040 | tf_op jit(solution)/shard_map/ppermute | solution.py:366
  18.0 20.5 %collective-permute-start.1 = (f32[8,1792]{1,0:T(8,128)S(1)}, f32[8,1792]{1,0:T(8,128)S(1)}, u32[]{:S(2)}, u32[]{:S(2)}) collective-permute-start(f32[8,1792]{1,0:T(8,128)S(1)} %copy-done.7), channel_id=1, source_target_pairs={{1,0},{2,1},{3,2},{4,3},{5,4},{6,5},{7,6},{8,7},{9,8},{10,9},{11,1... | collective-permute-start | bytes 172040 | tf_op jit(solution)/shard_map/ppermute | solution.py:367
  24.1 14.4 %collective-permute-start.2 = (f32[32,8,128]{2,1,0:T(8,128)S(1)}, f32[32,8,128]{2,1,0:T(8,128)S(1)}, u32[]{:S(2)}, u32[]{:S(2)}) collective-permute-start(f32[32,8,128]{2,1,0:T(8,128)S(1)} %all-to-all-done.table), channel_id=1, source_target_pairs={{0,32},{4,36},{8,40},{12,44},{32,64},{36,68},{40,72},{44,76},{64,9... | collective-permute-start | bytes 393224 | tf_op jit(solution)/shard_map/ppermute | solution.py:370
  30.3 1.0 %copy-start.2 = (f32[8,10240]{1,0:T(8,128)S(1)}, f32[8,10240]{1,0:T(8,128)}, u32[]{:S(2)}) copy-start(f32[8,10240]{1,0:T(8,128)} %get-tuple-element.9.own) | copy-start | bytes 983044
  31.3 7.1 %copy-start = (f32[16,64,64]{2,1,0:T(8,128)S(1)}, f32[16,64,64]{2,1,0:T(8,128)}, u32[]{:S(2)}) copy-start(f32[16,64,64]{2,1,0:T(8,128)} %transfer.3) | copy-start | bytes 786436
  31.3 7.2 %copy-start.1 = (bf16[16,64,256]{2,1,0:T(8,128)(2,1)S(1)}, bf16[16,64,256]{2,1,0:T(8,128)(2,1)}, u32[]{:S(2)}) copy-start(bf16[16,64,256]{2,1,0:T(8,128)(2,1)} %basis.3) | copy-start | bytes 1572868
  31.3 7.2 %copy-start.5 = (s32[16,8]{0,1:T(8,128)S(1)}, s32[16,8]{0,1:T(8,128)}, u32[]{:S(2)}) copy-start(s32[16,8]{0,1:T(8,128)} %param.18) | copy-start | bytes 1540
  31.3 7.2 %copy-start.6 = (s32[1,16]{1,0:T(1,128)S(1)}, s32[1,16]{1,0:T(1,128)}, u32[]{:S(2)}) copy-start(s32[1,16]{1,0:T(1,128)} %cluster_list.1) | copy-start | bytes 196
  38.4 0.7 %copy-start.3 = (f32[1,3,64]{2,0,1:T(1,128)S(1)}, f32[1,3,64]{2,0,1:T(1,128)}, u32[]{:S(2)}) copy-start(f32[1,3,64]{2,0,1:T(1,128)} %param.16) | copy-start | bytes 2308

commit v3 on v2

--- a/solution.py
+++ b/solution.py
@@ -17,6 +17,7 @@
 PTS = OWN * LEAF
 RANKS = OWN * RANK
 LANES = 128
+BUFFERS = 4
 SCALE = 16.0
 SHIFT = 2.56
 
@@ -47,10 +48,34 @@
     return both[:rows] + both[rows:] + dot(a_high, b_low, dims)
 
 
+ALONG_LANES = lax.GatherDimensionNumbers(
+    offset_dims=(), collapsed_slice_dims=(1,), start_index_map=(1,), operand_batching_dims=(0,),
+    start_indices_batching_dims=(0,),
+)
+
+
+def picked(source, index, count, dtype):
+    low = jnp.bitwise_and(index, dtype(LANES - 1))[..., None]
+    bits, k = [], 1
+    while k < count:
+        bits.append(jnp.bitwise_and(index, dtype(k * LANES)) != 0)
+        k *= 2
+
+    def among(first, level):
+        if level == 0:
+            return lax.gather(
+                source(first), low, ALONG_LANES, (1, 1), mode=lax.GatherScatterMode.PROMISE_IN_BOUNDS
+            )
+        size = 1 << (level - 1)
+        return jnp.where(bits[level - 1], among(first + size, level - 1), among(first, level - 1))
+
+    return among(0, len(bits))
+
+
 def prepare_kernel(
     charges, points, order, basis, transfer, leaf_proxy, cluster_proxy,
     own, right, left, spread,
-    source, entry, charges_in, points_in, order_in, basis_in, transfer_in, leaf_proxy_in, cluster_proxy_in, sems,
+    twice, entry, charges_in, points_in, order_in, basis_in, transfer_in, leaf_proxy_in, cluster_proxy_in, sems,
 ):
     copies = [
         pltpu.make_async_copy(a, b, sems.at[i])
@@ -65,29 +90,33 @@
         copy.start()
     own[:, AT_PROXY : AT_PROXY + RANKS] = jnp.zeros((8, RANKS), jnp.float32)
     entry[...] = jnp.zeros((NRHS, LANES), jnp.float32)
-    source[NRHS : 2 * NRHS, :] = jnp.zeros((NRHS, PTS), jnp.float32)
+    own[:, AT_POINTS : AT_POINTS + PTS] = jnp.zeros((8, PTS), jnp.float32)
     for copy in copies[:3]:
         copy.wait()
-    source[0:NRHS, :] = charges_in[...].astype(jnp.float32)
-    source[NRHS : NRHS + 3, :] = points_in[...] * SCALE
-
-    def gather(block, carry):
-        index = jnp.broadcast_to(order_in[pl.ds(block, 1), :], (8, LANES))
-        high = lax.shift_right_logical(index, 7)
-        low = jnp.bitwise_and(index, LANES - 1)
-        lanes = pl.ds(pl.multiple_of(block * LANES, LANES), LANES)
-        got = [None, None]
-        for k in range(PTS // LANES):
-            here = high == k
-            for part in range(2):
-                piece = source[8 * part : 8 * part + 8, k * LANES : (k + 1) * LANES]
-                piece = jnp.take_along_axis(piece, low, axis=1)
-                got[part] = piece if k == 0 else jnp.where(here, piece, got[part])
-        own[:, lanes] = got[0]
-        own[:, pl.ds(pl.multiple_of(PTS + block * LANES, LANES), LANES)] = got[1]
-        return carry
-
-    lax.fori_loop(0, PTS // LANES, gather, 0)
+    blocks = PTS // LANES
+    both = charges_in[...].astype(jnp.float32)
+    twice[...] = jnp.concatenate([both, both], axis=0).astype(jnp.bfloat16)
+
+    for i in range(blocks // 2):
+        index = jnp.concatenate(
+            [jnp.broadcast_to(order_in[2 * i + k : 2 * i + k + 1, :], (NRHS, LANES)) for k in range(2)], axis=0
+        ).astype(jnp.int16)
+        got = picked(
+            lambda k: twice[:, k * LANES : (k + 1) * LANES], index, blocks, jnp.int16
+        ).astype(jnp.float32)
+        for k in range(2):
+            own[:, (2 * i + k) * LANES : (2 * i + k + 1) * LANES] = got[NRHS * k : NRHS * (k + 1)]
+
+    for j in range(blocks // 8):
+        index = order_in[8 * j : 8 * j + 8, :]
+        for c in range(3):
+            got = picked(
+                lambda k: jnp.broadcast_to(points_in[c : c + 1, k * LANES : (k + 1) * LANES], (8, LANES)),
+                index, blocks, jnp.int32,
+            ) * SCALE
+            for s in range(8):
+                at = AT_POINTS + (8 * j + s) * LANES
+                own[c : c + 1, at : at + LANES] = got[s : s + 1]
 
     for copy in copies[3:]:
         copy.wait()
@@ -129,12 +158,40 @@
     return lax.rsqrt(d0 * d0 + d1 * d1 + d2 * d2 + SHIFT)
 
 
-def strip(columns, rows, block):
-    step = 16
-    for r in range(0, LEAF, step):
-        column = columns[r : r + step, :]
-        values = block_values([column[:, c : c + 1] for c in range(3)], rows)
-        block[r : r + step, 0 : values.shape[1]] = values.astype(jnp.bfloat16)
+def features(points, as_source):
+    row = lax.broadcasted_iota(jnp.int32, points.shape, 0)
+    h = jnp.floor(points * 2.0 + 0.5) * 0.5
+    l = points - h
+    l1 = l.astype(jnp.bfloat16).astype(jnp.float32)
+    l2 = l - l1
+    n = jnp.sum(h * h, axis=0, keepdims=True)
+    n1 = jnp.floor(n * (1 / 128) + 0.5) * 128.0
+    n2 = n - n1
+    s = jnp.sum((2.0 * h + l) * l, axis=0, keepdims=True) + SHIFT / 2
+    s1 = s.astype(jnp.bfloat16).astype(jnp.float32)
+    s2 = (s - s1).astype(jnp.bfloat16).astype(jnp.float32)
+    s3 = s - s1 - s2
+
+    def stack(vector, *others):
+        for i, other in enumerate(others):
+            vector = jnp.where(row == 3 + i, other, vector)
+        return vector
+
+    if as_source:
+        groups = [
+            stack(h, n1, n2, 1.0, 1.0), stack(h, s1, s2, s3, 1.0, 1.0), stack(h, 1.0), l1, l2, l1, l1, l2
+        ]
+    else:
+        h, l1, l2 = -2.0 * h, -2.0 * l1, -2.0 * l2
+        groups = [
+            stack(h, 1.0, 1.0, n1, n2), stack(l1, 1.0, 1.0, 1.0, s1, s2), stack(l2, s3), h, h, l1, l2, l1
+        ]
+    return jnp.concatenate(groups, axis=0).astype(jnp.bfloat16)
+
+
+def strip(sources, targets, block):
+    for at in range(0, targets.shape[1], LEAF):
+        block[:, at : at + LEAF] = lax.rsqrt(dot(sources, targets[:, at : at + LEAF])).astype(jnp.bfloat16)
 
 
 def listing(near, first):
@@ -147,52 +204,45 @@
     return listed
 
 
-def near_kernel(near_list, own, total, charges, columns, block, near, sem):
+def near_kernel(near_list, own, total, charges, sources, targets, block, near, sem):
     copy = pltpu.make_async_copy(near_list, near, sem)
     copy.start()
     first = (lax.axis_index("leaf") * NSUB + lax.axis_index("sub")) * OWN
     listed = listing(near, first)
     charges[...] = own[:, 0:PTS].astype(jnp.bfloat16)
     for t in range(PTS // LANES):
-        columns[t * LANES : (t + 1) * LANES, :] = own[:, PTS + t * LANES : PTS + (t + 1) * LANES].T
-    total[...] = jnp.zeros_like(total)
+        points = own[:, PTS + t * LANES : PTS + (t + 1) * LANES]
+        sources[t * LANES : (t + 1) * LANES, :] = features(points, True).T
+        targets[:, t * LANES : (t + 1) * LANES] = features(points, False)
     copy.wait()
 
-    def leaf(h, reach, block):
-        here = h * LEAF
-        if not isinstance(h, int):
-            here = pl.multiple_of(here, LEAF)
-        lanes_at = PTS + here
-        if not isinstance(h, int):
-            lanes_at = pl.multiple_of(lanes_at, LEAF)
-        rows = [own[c : c + 1, pl.ds(lanes_at, (reach + 1) * LEAF)] for c in range(3)]
-        strip(columns.at[pl.ds(here, LEAF), :], rows, block)
-        forward = dot(charges[:, pl.ds(here, LEAF)], block[:, 0 : (reach + 1) * LEAF])
-        reverse = forward[:, 0:LEAF] * listed(h, h)
-        for d in range(1, reach + 1):
-            there = (h + d) * LEAF
-            if not isinstance(h, int):
-                there = pl.multiple_of(there, LEAF)
-            lanes = slice(d * LEAF, (d + 1) * LEAF)
-            total[:, pl.ds(there, LEAF)] += forward[:, lanes] * listed(h + d, h)
-            reverse += dot(charges[:, pl.ds(there, LEAF)], block[:, lanes], NT) * listed(h, h + d)
-        total[:, pl.ds(here, LEAF)] += reverse
-
-    def pair(i, carry):
-        for k in range(2):
-            leaf(2 * i + k, REACH, block.at[k])
-        return carry
-
-    lax.fori_loop(0, (OWN - REACH) // 2, pair, 0)
-    for h in range(OWN - REACH, OWN):
-        leaf(h, OWN - 1 - h, block.at[h % 2])
+    sums = [0.0] * OWN
+    for step in range(OWN + 1):
+        for d in range(REACH + 1):
+            h = step
+            if h + d < OWN:
+                strip(
+                    sources[h * LEAF : (h + 1) * LEAF, :],
+                    targets[:, (h + d) * LEAF : (h + d + 1) * LEAF],
+                    block.at[h % BUFFERS, d],
+                )
+            h = step - 1
+            if h >= 0 and h + d < OWN:
+                here = slice(h * LEAF, (h + 1) * LEAF)
+                there = slice((h + d) * LEAF, (h + d + 1) * LEAF)
+                values = block[h % BUFFERS, d]
+                sums[h + d] += dot(charges[:, here], values) * listed(h + d, h)
+                if d > 0:
+                    sums[h] += dot(charges[:, there], values, NT) * listed(h, h + d)
+        if step > 0:
+            total[:, (step - 1) * LEAF : step * LEAF] = sums[step - 1]
 
 
 def product_kernel(
     near_list, leaf_list, cluster_list, cluster_proxy_list, transfer, basis,
     own, from_left, from_right, total, table, beyond,
     out,
-    coeffs, proxies, edge_columns, proxy_columns, block, leaf_block, down, far_rows,
+    coeffs, proxies, proxy_columns, block, leaf_block, down, far_rows,
     near, far_leaf, far_cluster, cluster_proxy, transfer_in, basis_in, sems,
 ):
     copies = [
@@ -226,19 +276,18 @@
     listed = listing(near, first)
     out[...] = total[...]
     for side, message in enumerate((from_left, from_right)):
-        for t in range(NEAR_W // LANES):
-            edge_columns[t * LANES : (t + 1) * LANES, :] = message[
-                :, NEAR_W + t * LANES : NEAR_W + (t + 1) * LANES
-            ].T
+        sources = features(message[:, NEAR_W : 2 * NEAR_W], True).T
+        at = 0 if side == 0 else PTS - NEAR_W
+        targets = features(own[:, PTS + at : PTS + at + NEAR_W], False)
         for i in range(REACH):
             h = i - REACH if side == 0 else OWN + i
-            targets = [g for g in range(OWN) if abs(g - h) <= REACH]
-            at, width = targets[0] * LEAF, len(targets) * LEAF
-            rows = [own[c : c + 1, PTS + at : PTS + at + width] for c in range(3)]
-            strip(edge_columns.at[i * LEAF : (i + 1) * LEAF, :], rows, block.at[i])
-            sources = message[:, i * LEAF : (i + 1) * LEAF].astype(jnp.bfloat16)
-            forward = dot(sources, block[i, :, 0:width])
-            for k, g in enumerate(targets):
+            leaves = [g for g in range(OWN) if abs(g - h) <= REACH]
+            width = len(leaves) * LEAF
+            skip = leaves[0] * LEAF - at
+            strip(sources[i * LEAF : (i + 1) * LEAF], targets[:, skip : skip + width], block.at[i])
+            weights = message[:, i * LEAF : (i + 1) * LEAF].astype(jnp.bfloat16)
+            forward = dot(weights, block[i, :, 0:width])
+            for k, g in enumerate(leaves):
                 out[:, g * LEAF : (g + 1) * LEAF] += forward[:, k * LEAF : (k + 1) * LEAF] * listed(g, h)
 
     span = 3 * LANES
@@ -351,7 +400,7 @@
             jax.ShapeDtypeStruct((8, MSG), f32),
             jax.ShapeDtypeStruct((size, NRHS, LANES), f32),
         ],
-        scratch_shapes=[pltpu.VMEM((2 * NRHS, PTS), f32), pltpu.VMEM((NRHS, LANES), f32)]
+        scratch_shapes=[pltpu.VMEM((2 * NRHS, PTS), jnp.bfloat16), pltpu.VMEM((NRHS, LANES), f32)]
         + [pltpu.VMEM(a.shape, a.dtype) for a in given]
         + [pltpu.SemaphoreType.DMA((7,))],
         name="prepare",
@@ -375,8 +424,9 @@
         out_shape=jax.ShapeDtypeStruct((NRHS, PTS), f32),
         scratch_shapes=[
             pltpu.VMEM((8, PTS), jnp.bfloat16),
-            pltpu.VMEM((PTS, 8), f32),
-            pltpu.VMEM((2, LEAF, (REACH + 1) * LEAF), jnp.bfloat16),
+            pltpu.VMEM((PTS, 64), jnp.bfloat16),
+            pltpu.VMEM((64, PTS), jnp.bfloat16),
+            pltpu.VMEM((BUFFERS, REACH + 1, LEAF, LEAF), jnp.bfloat16),
             pltpu.SMEM(near.shape, near.dtype),
             pltpu.SemaphoreType.DMA,
         ],
@@ -393,7 +443,6 @@
         scratch_shapes=[
             pltpu.VMEM((8, far_window * RANK), f32),
             pltpu.VMEM((8, far_window * RANK), f32),
-            pltpu.VMEM((NEAR_W, 8), f32),
             pltpu.VMEM((far_window * RANK, 8), f32),
             pltpu.VMEM((REACH, LEAF, REACH * LEAF), jnp.bfloat16),
             pltpu.VMEM((2 * RANK, 3 * LANES), f32),

time: 44.5 us -> 37 us (0.83)
  Pallas kernels: 18.8 us -> 11.4 us
    pallas_call x1, Pallas kernels: 7.08 us -> 3.36 us  [shards(): pl.pallas_call(near_kernel, in_specs=[hbm, vmem], out_specs=vmem, out_sha...]
    pallas_call x1, Pallas kernels: 6.71 us -> 3.29 us  [shards(): pl.pallas_call(prepare_kernel, in_specs=[hbm] * 7, out_specs=[vmem] * 4,...]
  transfers between devices with their start and end apart: 4 -> 4, of which waited for: 0 -> 0; matrix products, arithmetic and copies ran while one was open for 0% -> 0% of each run, Pallas kernels for 16% -> 9%
where the time goes in v3:
time: 37 us; the launch traced here: 36.6 us
  starting transfers between devices  23.5 us (64%)
  Pallas kernels  11.4 us (31%)
  local copies, waits for them, and re-layouts  1.6 us (4%)
    all_to_all x1, starting transfers between devices, shards(): lax.all_to_all(spread, axes, 0, 0, tiled=True, axis_index_groups=[list(ra...  7.46 us
    ppermute x1, starting transfers between devices, shards(): beyond = lax.ppermute(table, 'leaf', shift)  6.25 us
    ppermute x1, starting transfers between devices, shards(): lax.ppermute(left, axes, [(i + 1, i) for i in range(count - 1)])  6.08 us
    pallas_call x1, Pallas kernels, shards(): pl.pallas_call(product_kernel, in_specs=[hbm] * 6 + [vmem] * 6, out_specs...  4.71 us
    ppermute x1, starting transfers between devices, shards(): lax.ppermute(right, axes, [(i, i + 1) for i in range(count - 1)])  3.7 us
    pallas_call x1, Pallas kernels, shards(): pl.pallas_call(near_kernel, in_specs=[hbm, vmem], out_specs=vmem, out_sha...  3.36 us
    pallas_call x1, Pallas kernels, shards(): pl.pallas_call(prepare_kernel, in_specs=[hbm] * 7, out_specs=[vmem] * 4,...  3.29 us
    unnamed x18, local copies, waits for them, and re-layouts  1.6 us
  transfers between devices with their start and end apart: 4, of which 0 were waited for; matrix products, arithmetic and copies ran while one was open for 0% of the time, Pallas kernels for 9%

profile of v3, /device:TPU:96, one launch (start us, length us, event | category | flops | bytes accessed | tf_op | source)
XLA Modules:
  0.0 36.6 jit_solution(14959636659569266833)
XLA Ops:
  0.0 3.3 %prepare.1 = (f32[8,10240]{1,0:T(8,128)}, f32[8,1792]{1,0:T(8,128)}, f32[8,1792]{1,0:T(8,128)}, f32[32,8,128]{2,1,0:T(8,128)}) custom-call(bf16[8,4096]{1,0:T(8,128)(2,1)} %charges.1, f32[3,4096]{1,0:T(4,128)} %points.1, s32[32,128]{1,0:T(8,128)} %bitcast.11, bf16[16,64,256]{2,1,0:T(8,128)(2,1)} %basis.3, f32[16,64,64]{2,1,0:T(8,128)} %transfer.3, ...), custom_call_target="tpu_custom_call" | custom-call | tf_op jit(solution)/shard_map/prepare/pallas_call | solution.py:393
  3.3 0.0 copy-start.8
  3.3 0.0 copy-start.7
  3.3 7.5 %all-to-all-start = ((f32[32,8,128]{2,1,0:T(8,128)}), f32[32,8,128]{2,1,0:T(8,128)S(1)}, u32[]{:S(2)}, u32[]{:S(2)}) async-start(f32[32,8,128]{2,1,0:T(8,128)} %get-tuple-element.12), calls=%async_computation | async-start | bytes 262144 | tf_op jit(solution)/shard_map/all_to_all | solution.py:411
  10.8 0.0 copy-start.4
  10.8 0.0 copy-done.8
  10.8 3.7 %collective-permute-start = (f32[8,1792]{1,0:T(8,128)S(1)}, f32[8,1792]{1,0:T(8,128)S(1)}, u32[]{:S(2)}, u32[]{:S(2)}) collective-permute-start(f32[8,1792]{1,0:T(8,128)S(1)} %copy-done.8), channel_id=1, source_target_pairs={{0,1},{1,2},{2,3},{3,4},{4,5},{5,6},{6,7},{7,8},{8,9},{9,10},{10,1... | collective-permute-start | bytes 172040 | tf_op jit(solution)/shard_map/ppermute | solution.py:415
  14.5 0.0 copy-done.7
  14.5 6.1 %collective-permute-start.1 = (f32[8,1792]{1,0:T(8,128)S(1)}, f32[8,1792]{1,0:T(8,128)S(1)}, u32[]{:S(2)}, u32[]{:S(2)}) collective-permute-start(f32[8,1792]{1,0:T(8,128)S(1)} %copy-done.7), channel_id=1, source_target_pairs={{1,0},{2,1},{3,2},{4,3},{5,4},{6,5},{7,6},{8,7},{9,8},{10,9},{11,1... | collective-permute-start | bytes 172040 | tf_op jit(solution)/shard_map/ppermute | solution.py:416
  20.6 0.0 all-to-all-done.table
  20.6 6.2 %collective-permute-start.2 = (f32[32,8,128]{2,1,0:T(8,128)S(1)}, f32[32,8,128]{2,1,0:T(8,128)S(1)}, u32[]{:S(2)}, u32[]{:S(2)}) collective-permute-start(f32[32,8,128]{2,1,0:T(8,128)S(1)} %all-to-all-done.table), channel_id=1, source_target_pairs={{0,32},{4,36},{8,40},{12,44},{32,64},{36,68},{40,72},{44,76},{64,9... | collective-permute-start | bytes 393224 | tf_op jit(solution)/shard_map/ppermute | solution.py:419
  26.9 0.0 copy-done.4
  26.9 0.0 copy-start.2
  26.9 1.0 %copy-done.2 = f32[8,10240]{1,0:T(8,128)S(1)} copy-done((f32[8,10240]{1,0:T(8,128)S(1)}, f32[8,10240]{1,0:T(8,128)}, u32[]{:S(2)}) %copy-start.2) | copy-done | bytes 327704
  27.9 0.0 copy-start
  27.9 0.0 copy-start.1
  27.9 0.0 copy-start.5
  27.9 0.0 copy-start.6
  27.9 3.4 %near_field.1.total = f32[8,4096]{1,0:T(8,128)S(1)} custom-call(s32[5,16]{1,0:T(8,128)S(1)} %bitcast.7, f32[8,10240]{1,0:T(8,128)S(1)} %copy-done.2), custom_call_target="tpu_custom_call" | custom-call | flops 8999999488 | bytes 1000000 | tf_op jit(solution)/shard_map/near_field/pallas_call | solution.py:420
  31.2 0.0 copy-start.3
  31.3 0.0 collective-permute-done.from_left
  31.3 0.0 collective-permute-done.1.from_right
  31.3 0.0 collective-permute-done.2.beyond
  31.3 0.0 copy-done
  31.3 0.0 copy-done.1
  31.3 0.0 copy-done.5
  31.3 0.0 copy-done.6
  31.3 0.6 %copy-done.3 = f32[1,3,64]{2,0,1:T(1,128)S(1)} copy-done((f32[1,3,64]{2,0,1:T(1,128)S(1)}, f32[1,3,64]{2,0,1:T(1,128)}, u32[]{:S(2)}) %copy-start.3) | copy-done | bytes 792
  31.9 4.7 %product.1 = f32[8,4096]{1,0:T(8,128)} custom-call(s32[5,16]{1,0:T(8,128)S(1)} %bitcast.8, s32[8,16]{1,0:T(8,128)S(1)} %bitcast.9, s32[1,16]{1,0:T(1,128)S(1)} %copy-done.6, f32[3,1,64]{2,1,0:T(1,128)S(1)} %bitcast.6, f32[16,64,64]{2,1,0:T(8,128)S(1)} %copy-done, bf16[16,64,256]{2,1,0:T(8,128)(2,1)S(1)} %copy-done.1, f32[8,10240]{1,0:T(8,128)S(1)} %copy-done.2, ...), custom_call_target="tpu_custom_call" | custom-call | tf_op jit(solution)/shard_map/product/pallas_call | solution.py:438
Async XLA Ops:
  3.3 7.5 %copy-start.8 = (f32[8,1792]{1,0:T(8,128)S(1)}, f32[8,1792]{1,0:T(8,128)}, u32[]{:S(2)}) copy-start(f32[8,1792]{1,0:T(8,128)} %get-tuple-element.10) | copy-start | bytes 172036
  3.3 11.2 %copy-start.7 = (f32[8,1792]{1,0:T(8,128)S(1)}, f32[8,1792]{1,0:T(8,128)}, u32[]{:S(2)}) copy-start(f32[8,1792]{1,0:T(8,128)} %get-tuple-element.11) | copy-start | bytes 172036
  3.3 17.3 %all-to-all-start = ((f32[32,8,128]{2,1,0:T(8,128)}), f32[32,8,128]{2,1,0:T(8,128)S(1)}, u32[]{:S(2)}, u32[]{:S(2)}) async-start(f32[32,8,128]{2,1,0:T(8,128)} %get-tuple-element.12), calls=%async_computation | async-start | bytes 262144 | tf_op jit(solution)/shard_map/all_to_all | solution.py:411
  10.8 16.1 %copy-start.4 = (s32[16,5]{0,1:T(8,128)S(1)}, s32[16,5]{0,1:T(8,128)}, u32[]{:S(2)}) copy-start(s32[16,5]{0,1:T(8,128)} %param.17) | copy-start | bytes 964
  10.8 20.4 %collective-permute-start = (f32[8,1792]{1,0:T(8,128)S(1)}, f32[8,1792]{1,0:T(8,128)S(1)}, u32[]{:S(2)}, u32[]{:S(2)}) collective-permute-start(f32[8,1792]{1,0:T(8,128)S(1)} %copy-done.8), channel_id=1, source_target_pairs={{0,1},{1,2},{2,3},{3,4},{4,5},{5,6},{6,7},{7,8},{8,9},{9,10},{10,1... | collective-permute-start | bytes 172040 | tf_op jit(solution)/shard_map/ppermute | solution.py:415
  14.5 16.7 %collective-permute-start.1 = (f32[8,1792]{1,0:T(8,128)S(1)}, f32[8,1792]{1,0:T(8,128)S(1)}, u32[]{:S(2)}, u32[]{:S(2)}) collective-permute-start(f32[8,1792]{1,0:T(8,128)S(1)} %copy-done.7), channel_id=1, source_target_pairs={{1,0},{2,1},{3,2},{4,3},{5,4},{6,5},{7,6},{8,7},{9,8},{10,9},{11,1... | collective-permute-start | bytes 172040 | tf_op jit(solution)/shard_map/ppermute | solution.py:416
  20.6 10.7 %collective-permute-start.2 = (f32[32,8,128]{2,1,0:T(8,128)S(1)}, f32[32,8,128]{2,1,0:T(8,128)S(1)}, u32[]{:S(2)}, u32[]{:S(2)}) collective-permute-start(f32[32,8,128]{2,1,0:T(8,128)S(1)} %all-to-all-done.table), channel_id=1, source_target_pairs={{0,32},{4,36},{8,40},{12,44},{32,64},{36,68},{40,72},{44,76},{64,9... | collective-permute-start | bytes 393224 | tf_op jit(solution)/shard_map/ppermute | solution.py:419
  26.9 1.0 %copy-start.2 = (f32[8,10240]{1,0:T(8,128)S(1)}, f32[8,10240]{1,0:T(8,128)}, u32[]{:S(2)}) copy-start(f32[8,10240]{1,0:T(8,128)} %get-tuple-element.9.own) | copy-start | bytes 983044
  27.9 3.4 %copy-start = (f32[16,64,64]{2,1,0:T(8,128)S(1)}, f32[16,64,64]{2,1,0:T(8,128)}, u32[]{:S(2)}) copy-start(f32[16,64,64]{2,1,0:T(8,128)} %transfer.3) | copy-start | bytes 786436
  27.9 3.4 %copy-start.1 = (bf16[16,64,256]{2,1,0:T(8,128)(2,1)S(1)}, bf16[16,64,256]{2,1,0:T(8,128)(2,1)}, u32[]{:S(2)}) copy-start(bf16[16,64,256]{2,1,0:T(8,128)(2,1)} %basis.3) | copy-start | bytes 1572868
  27.9 3.4 %copy-start.5 = (s32[16,8]{0,1:T(8,128)S(1)}, s32[16,8]{0,1:T(8,128)}, u32[]{:S(2)}) copy-start(s32[16,8]{0,1:T(8,128)} %param.18) | copy-start | bytes 1540
  27.9 3.4 %copy-start.6 = (s32[1,16]{1,0:T(1,128)S(1)}, s32[1,16]{1,0:T(1,128)}, u32[]{:S(2)}) copy-start(s32[1,16]{1,0:T(1,128)} %cluster_list.1) | copy-start | bytes 196
  31.2 0.7 %copy-start.3 = (f32[1,3,64]{2,0,1:T(1,128)S(1)}, f32[1,3,64]{2,0,1:T(1,128)}, u32[]{:S(2)}) copy-start(f32[1,3,64]{2,0,1:T(1,128)} %param.16) | copy-start | bytes 2308

commit v4 on v3

--- a/solution.py
+++ b/solution.py
@@ -14,10 +14,12 @@
 PLANE = 8
 HALF = PLANE // 2
 NSUB = 4
+FAR1 = 16
 PTS = OWN * LEAF
 RANKS = OWN * RANK
 LANES = 128
 BUFFERS = 4
+AHEAD = 2
 SCALE = 16.0
 SHIFT = 2.56
 
@@ -25,7 +27,8 @@
 FAR_W = FREACH * RANK
 MSG = 2 * NEAR_W + 2 * FAR_W
 AT_CHARGES, AT_POINTS, AT_COEFFS, AT_PROXY = 0, PTS, 2 * PTS, 2 * PTS + RANKS
-OWN_W = 2 * PTS + 2 * RANKS
+AT_LIST = 2 * PTS + 2 * RANKS
+OWN_W = AT_LIST + LANES
 
 NT = (((1,), (1,)), ((), ()))
 NN = (((1,), (0,)), ((), ()))
@@ -73,16 +76,17 @@
 
 
 def prepare_kernel(
-    charges, points, order, basis, transfer, leaf_proxy, cluster_proxy,
+    charges, points, order, basis, transfer, leaf_proxy, cluster_proxy, far_cluster,
     own, right, left, spread,
-    twice, entry, charges_in, points_in, order_in, basis_in, transfer_in, leaf_proxy_in, cluster_proxy_in, sems,
+    twice, entry, charges_in, points_in, order_in, basis_in, transfer_in, leaf_proxy_in, cluster_proxy_in, far_cluster_in, sems,
 ):
     copies = [
         pltpu.make_async_copy(a, b, sems.at[i])
         for i, (a, b) in enumerate(
             (
                 (order, order_in), (charges, charges_in), (points, points_in), (leaf_proxy, leaf_proxy_in),
-                (cluster_proxy, cluster_proxy_in), (basis, basis_in), (transfer, transfer_in),
+                (cluster_proxy, cluster_proxy_in), (far_cluster, far_cluster_in), (basis, basis_in),
+                (transfer, transfer_in),
             )
         )
     ]
@@ -124,16 +128,26 @@
         at = AT_PROXY + g * RANK
         own[0:3, at : at + RANK] = leaf_proxy_in[:, g, :] * SCALE
 
+    own[:, AT_LIST:] = jnp.zeros((8, LANES), jnp.float32)
+    own[0:1, AT_LIST : AT_LIST + far_cluster_in.shape[1]] = far_cluster_in[...].astype(jnp.float32)
+
     first_half = lax.broadcasted_iota(jnp.int32, (NRHS, LANES), 1) < RANK
     parent = jnp.zeros((NRHS, RANK), jnp.float32)
-    for m in range(OWN // 2):
-        a = own[:, 2 * m * LEAF : (2 * m + 1) * LEAF].astype(jnp.bfloat16)
-        b = own[:, (2 * m + 1) * LEAF : (2 * m + 2) * LEAF].astype(jnp.bfloat16)
-        weights = jnp.reshape(basis_in[2 * m : 2 * m + 2], (2 * RANK, LEAF))
-        pair = dot(jnp.concatenate([a, b], axis=0), weights, NT)
-        coeffs = jnp.where(first_half, pair[:NRHS], pair[NRHS:])
-        own[:, AT_COEFFS + m * LANES : AT_COEFFS + (m + 1) * LANES] = coeffs
-        parent += dot3(coeffs, jnp.reshape(transfer_in[2 * m : 2 * m + 2], (2 * RANK, RANK)))
+    pairs = range(OWN // 2)
+    both = [
+        dot(
+            jnp.concatenate(
+                [own[:, g * LEAF : (g + 1) * LEAF].astype(jnp.bfloat16) for g in (2 * m, 2 * m + 1)], axis=0
+            ),
+            jnp.reshape(basis_in[2 * m : 2 * m + 2], (2 * RANK, LEAF)),
+            NT,
+        )
+        for m in pairs
+    ]
+    coeffs = [jnp.where(first_half, both[m][:NRHS], both[m][NRHS:]) for m in pairs]
+    for m in pairs:
+        own[:, AT_COEFFS + m * LANES : AT_COEFFS + (m + 1) * LANES] = coeffs[m]
+        parent += dot3(coeffs[m], jnp.reshape(transfer_in[2 * m : 2 * m + 2], (2 * RANK, RANK)))
 
     entry[:, 0:RANK] = parent
     entry[0:3, RANK : 2 * RANK] = cluster_proxy_in[:, 0, :] * SCALE
@@ -239,20 +253,13 @@
 
 
 def product_kernel(
-    near_list, leaf_list, cluster_list, cluster_proxy_list, transfer, basis,
-    own, from_left, from_right, total, table, beyond,
+    near_list, far_leaf, transfer, basis, own, from_left, from_right, total, table, beyond,
     out,
-    coeffs, proxies, proxy_columns, block, leaf_block, down, far_rows,
-    near, far_leaf, far_cluster, cluster_proxy, transfer_in, basis_in, sems,
+    down, coeffs, sources, targets, block, high, low, far_rows, near, far_cluster, sems,
 ):
     copies = [
         pltpu.make_async_copy(a, b, sems.at[i])
-        for i, (a, b) in enumerate(
-            (
-                (near_list, near), (leaf_list, far_leaf), (cluster_list, far_cluster),
-                (cluster_proxy_list, cluster_proxy), (transfer, transfer_in), (basis, basis_in),
-            )
-        )
+        for i, (a, b) in enumerate(((near_list, near), (own.at[:, AT_LIST:], far_cluster)))
     ]
     for copy in copies:
         copy.start()
@@ -260,41 +267,49 @@
     cluster = group * NSUB + lax.axis_index("sub")
     first = cluster * OWN
 
+    out[...] = total[...]
+    down[...] = jnp.zeros_like(down)
     at = 2 * NEAR_W
-    for window, start, whole, width in (
-        (coeffs, AT_COEFFS, RANKS, FAR_W), (proxies, AT_PROXY, RANKS, FAR_W),
-    ):
-        window[:, 0:width] = from_left[:, at : at + width]
-        window[:, width : width + whole] = own[:, start : start + whole]
-        window[:, width + whole : 2 * width + whole] = from_right[:, at : at + width]
+    pieces = []
+    for start, width in ((AT_COEFFS, FAR_W), (AT_PROXY, FAR_W)):
+        pieces.append((from_left[:, at : at + width], own[:, start : start + RANKS], from_right[:, at : at + width]))
         at += width
-    for t in range(proxies.shape[1] // LANES):
-        proxy_columns[t * LANES : (t + 1) * LANES, :] = proxies[:, t * LANES : (t + 1) * LANES].T
-
-    for copy in copies[:4]:
+    coeffs[...] = jnp.concatenate(pieces[0], axis=1)
+    for t, proxies in enumerate(pieces[1]):
+        at = (0, FAR_W, FAR_W + RANKS)[t]
+        sources[at : at + proxies.shape[1], :] = features(proxies, True).T
+        targets[:, at : at + proxies.shape[1]] = features(proxies, False)
+    for copy in copies:
         copy.wait()
     listed = listing(near, first)
-    out[...] = total[...]
-    for side, message in enumerate((from_left, from_right)):
-        sources = features(message[:, NEAR_W : 2 * NEAR_W], True).T
+
+    def edges(side, message):
         at = 0 if side == 0 else PTS - NEAR_W
-        targets = features(own[:, PTS + at : PTS + at + NEAR_W], False)
+        columns = features(message[:, NEAR_W : 2 * NEAR_W], True).T
+        rows = features(own[:, PTS + at : PTS + at + NEAR_W], False)
+        steps = []
         for i in range(REACH):
             h = i - REACH if side == 0 else OWN + i
             leaves = [g for g in range(OWN) if abs(g - h) <= REACH]
-            width = len(leaves) * LEAF
-            skip = leaves[0] * LEAF - at
-            strip(sources[i * LEAF : (i + 1) * LEAF], targets[:, skip : skip + width], block.at[i])
-            weights = message[:, i * LEAF : (i + 1) * LEAF].astype(jnp.bfloat16)
-            forward = dot(weights, block[i, :, 0:width])
-            for k, g in enumerate(leaves):
-                out[:, g * LEAF : (g + 1) * LEAF] += forward[:, k * LEAF : (k + 1) * LEAF] * listed(g, h)
+            skip, width = leaves[0] * LEAF - at, len(leaves) * LEAF
+            values = block.at[REACH * side + i]
+
+            def evaluate(i=i, values=values, skip=skip, width=width):
+                strip(columns[i * LEAF : (i + 1) * LEAF], rows[:, skip : skip + width], values)
+
+            def multiply(i=i, values=values, width=width):
+                return dot(message[:, i * LEAF : (i + 1) * LEAF].astype(jnp.bfloat16), values[:, 0:width])
+
+            def add(forward, h=h, leaves=leaves):
+                for k, g in enumerate(leaves):
+                    out[:, g * LEAF : (g + 1) * LEAF] += forward[:, k * LEAF : (k + 1) * LEAF] * listed(g, h)
+
+            steps.append((evaluate, multiply, add))
+        return steps
 
     span = 3 * LANES
     first_lanes = lax.broadcasted_iota(jnp.int32, (NRHS, LANES), 1) < RANK
-    down[...] = jnp.zeros_like(down)
-    lists = far_leaf[...] - first + FREACH
-    lists = jnp.where(far_leaf[...] >= 0, lists, -1)
+    lists = jnp.where(far_leaf[...] >= 0, far_leaf[...] - first + FREACH, -1)
     far_rows[...] = jnp.full_like(far_rows, -1)
     for m in range(OWN // 2):
         at = FAR_W + m * LANES
@@ -304,40 +319,60 @@
             jnp.broadcast_to(lists[:, 2 * m + 1 : 2 * m + 2], (8, LANES)),
         )
     lane_leaf = lax.broadcasted_iota(jnp.int32, (8, span), 1) // RANK
-    for m in range((FREACH + OWN) // 2):
+
+    def coupling(m):
         at = m * LANES
         to = at + LANES
-        rows = [proxies[c : c + 1, to : to + span] for c in range(3)]
-        for r in range(0, LANES, 32):
-            column = proxy_columns[at + r : at + r + 32, :]
-            leaf_block[r : r + 32, :] = block_values([column[:, c : c + 1] for c in range(3)], rows)
-        high, low = split(leaf_block[...])
-        pair = coeffs[:, at : at + LANES]
-        sources = jnp.concatenate(
-            [jnp.where(first_lanes, pair, 0.0), jnp.where(first_lanes, 0.0, pair)], axis=0
-        )
-        s_high, s_low = split(sources)
-        both = dot(jnp.concatenate([s_high, s_low], axis=0), high)
-        forward = both[:16] + both[16:] + dot(s_high, low)
-        for i in range(2):
-            hit = jnp.max((far_rows[:, to : to + span] == 2 * m + i).astype(jnp.float32), axis=0, keepdims=True)
-            down[:, to : to + span] += forward[8 * i : 8 * i + 8] * hit
-        if 2 * m >= FREACH:
-            targets = coeffs[:, to : to + span]
-            masked = []
+        slot = m % BUFFERS
+
+        def evaluate():
+            values = lax.rsqrt(dot(sources[at : at + LANES, :], targets[:, to : to + span]))
+            high[slot], low[slot] = split(values)
+
+        def multiply():
+            pair = coeffs[:, at : at + LANES]
+            s_high, s_low = split(
+                jnp.concatenate([jnp.where(first_lanes, pair, 0.0), jnp.where(first_lanes, 0.0, pair)], axis=0)
+            )
+            got = [dot(jnp.concatenate([s_high, s_low], axis=0), high[slot]), dot(s_high, low[slot])]
+            if 2 * m >= FREACH:
+                masked = []
+                for i in range(2):
+                    column = lists[:, 2 * m + i - FREACH : 2 * m + i - FREACH + 1]
+                    hit = (lane_leaf + (2 * m + 2) == column).astype(jnp.float32)
+                    masked.append(coeffs[:, to : to + span] * jnp.max(hit, axis=0, keepdims=True))
+                t_high, t_low = split(jnp.concatenate(masked, axis=0))
+                got.append(dot(jnp.concatenate([t_high, t_low], axis=0), high[slot], NT))
+                got.append(dot(t_high, low[slot], NT))
+            return got
+
+        def add(got):
+            forward = got[0][:16] + got[0][16:] + got[1]
             for i in range(2):
-                column = lists[:, 2 * m + i - FREACH : 2 * m + i - FREACH + 1]
-                hit = jnp.max((lane_leaf + (2 * m + 2) == column).astype(jnp.float32), axis=0, keepdims=True)
-                masked.append(targets * hit)
-            t_high, t_low = split(jnp.concatenate(masked, axis=0))
-            both = dot(jnp.concatenate([t_high, t_low], axis=0), high, NT)
-            reverse = both[:16] + both[16:] + dot(t_high, low, NT)
-            down[:, at : at + LANES] += jnp.where(first_lanes, reverse[:8], reverse[8:])
+                hit = (far_rows[:, to : to + span] == 2 * m + i).astype(jnp.float32)
+                hit = jnp.max(hit, axis=0, keepdims=True)
+                down[:, to : to + span] += forward[8 * i : 8 * i + 8] * hit
+            if len(got) > 2:
+                reverse = got[2][:16] + got[2][16:] + got[3]
+                down[:, at : at + LANES] += jnp.where(first_lanes, reverse[:8], reverse[8:])
+
+        return evaluate, multiply, add
+
+    steps = [coupling(m) for m in range((FREACH + OWN) // 2)]
+    steps += edges(0, from_left) + edges(1, from_right)
+    products = {}
+    for i in range(len(steps) + AHEAD + 1):
+        if i < len(steps):
+            steps[i][0]()
+        if 0 <= i - AHEAD < len(steps):
+            products[i - AHEAD] = steps[i - AHEAD][1]()
+        if 0 <= i - AHEAD - 1:
+            steps[i - AHEAD - 1][2](products.pop(i - AHEAD - 1))
 
     plane = group // PLANE
     entries, kept = [], []
-    for slot in range(far_cluster.shape[1]):
-        f = far_cluster[0, slot]
+    for slot in range(FAR1):
+        f = far_cluster[0, slot].astype(jnp.int32)
         valid = f >= 0
         f = jnp.where(valid, f, cluster)
         mine = f // (PLANE * NSUB) == plane
@@ -352,29 +387,29 @@
         sources.append(jnp.where(first_lanes, pltpu.roll(entries[a], RANK, 1), entries[b]))
     parents = jnp.concatenate(parents, axis=1)
     sources = jnp.concatenate(sources, axis=1)
-    mine = jnp.concatenate([cluster_proxy[:, 0, :] * SCALE, jnp.zeros((5, RANK), jnp.float32)], axis=0)
-    mine = jnp.concatenate([mine, mine], axis=1).T[:RANK]
+    mine = table[lax.rem(cluster, PLANE * NSUB)].T[RANK : 2 * RANK]
     values = block_values(
         [mine[:, c : c + 1] for c in range(3)], [sources[c : c + 1, :] for c in range(3)]
     )
     coupled = dot3(parents, values, NT)
 
-    for copy in copies[4:]:
-        copy.wait()
-    for m in range(OWN // 2):
-        weights = jnp.reshape(transfer_in[2 * m : 2 * m + 2], (2 * RANK, RANK))
-        at = FAR_W + m * LANES
-        pair = down[:, at : at + LANES] + dot3(coupled, weights, NT)
-        d_high, d_low = split(
-            jnp.concatenate([jnp.where(first_lanes, pair, 0.0), jnp.where(first_lanes, 0.0, pair)], axis=0)
+    pairs = range(OWN // 2)
+    lowered = [dot3(coupled, jnp.reshape(transfer[2 * m : 2 * m + 2], (2 * RANK, RANK)), NT) for m in pairs]
+    parts = []
+    for m in pairs:
+        pair = lowered[m] + down[:, FAR_W + m * LANES : FAR_W + (m + 1) * LANES]
+        parts.append(
+            split(jnp.concatenate([jnp.where(first_lanes, pair, 0.0), jnp.where(first_lanes, 0.0, pair)], axis=0))
         )
-        both = dot(
-            jnp.concatenate([d_high, d_low], axis=0), jnp.reshape(basis_in[2 * m : 2 * m + 2], (2 * RANK, LEAF))
-        )
-        far = both[:16] + both[16:]
+    far = [
+        dot(jnp.concatenate(parts[m], axis=0), jnp.reshape(basis[2 * m : 2 * m + 2], (2 * RANK, LEAF)))
+        for m in pairs
+    ]
+    for m in pairs:
+        value = far[m][:16] + far[m][16:]
         for i in range(2):
             at = (2 * m + i) * LEAF
-            out[:, at : at + LEAF] += far[8 * i : 8 * i + 8]
+            out[:, at : at + LEAF] += value[8 * i : 8 * i + 8]
 
 
 def shards(
@@ -388,11 +423,11 @@
     leaf_proxy = leaf_proxy.transpose(1, 0, 2)
     cluster_proxy = cluster_proxy.transpose(1, 0, 2)
     near, far_leaf = near.transpose(1, 0), far_leaf.transpose(1, 0)
-    given = (charges, points, order.reshape(PTS // LANES, LANES), basis, transfer, leaf_proxy, cluster_proxy)
+    given = (charges, points, order.reshape(PTS // LANES, LANES), basis, transfer, leaf_proxy, cluster_proxy, far_cluster)
     size = PLANE * NSUB
     own, right, left, spread = pl.pallas_call(
         prepare_kernel,
-        in_specs=[hbm] * 7,
+        in_specs=[hbm] * 8,
         out_specs=[vmem] * 4,
         out_shape=[
             jax.ShapeDtypeStruct((8, OWN_W), f32),
@@ -402,7 +437,7 @@
         ],
         scratch_shapes=[pltpu.VMEM((2 * NRHS, PTS), jnp.bfloat16), pltpu.VMEM((NRHS, LANES), f32)]
         + [pltpu.VMEM(a.shape, a.dtype) for a in given]
-        + [pltpu.SemaphoreType.DMA((7,))],
+        + [pltpu.SemaphoreType.DMA((8,))],
         name="prepare",
     )(*given)
 
@@ -437,31 +472,25 @@
     far_window = OWN + 2 * FREACH
     return pl.pallas_call(
         product_kernel,
-        in_specs=[hbm] * 6 + [vmem] * 6,
+        in_specs=[hbm] + [vmem] * 9,
         out_specs=vmem,
         out_shape=jax.ShapeDtypeStruct((NRHS, PTS), f32),
         scratch_shapes=[
+            pltpu.VMEM((NRHS, far_window * RANK), f32),
             pltpu.VMEM((8, far_window * RANK), f32),
-            pltpu.VMEM((8, far_window * RANK), f32),
-            pltpu.VMEM((far_window * RANK, 8), f32),
-            pltpu.VMEM((REACH, LEAF, REACH * LEAF), jnp.bfloat16),
-            pltpu.VMEM((2 * RANK, 3 * LANES), f32),
-            pltpu.VMEM((8, far_window * RANK), f32),
+            pltpu.VMEM((far_window * RANK, 64), jnp.bfloat16),
+            pltpu.VMEM((64, far_window * RANK), jnp.bfloat16),
+            pltpu.VMEM((2 * REACH, LEAF, REACH * LEAF), jnp.bfloat16),
+            pltpu.VMEM((BUFFERS, 2 * RANK, 3 * LANES), jnp.bfloat16),
+            pltpu.VMEM((BUFFERS, 2 * RANK, 3 * LANES), jnp.bfloat16),
             pltpu.VMEM((8, far_window * RANK), jnp.int32),
             pltpu.SMEM(near.shape, near.dtype),
-            pltpu.VMEM(far_leaf.shape, far_leaf.dtype),
-            pltpu.SMEM(far_cluster.shape, far_cluster.dtype),
-            pltpu.VMEM(cluster_proxy.shape, cluster_proxy.dtype),
-            pltpu.VMEM(transfer.shape, transfer.dtype),
-            pltpu.VMEM(basis.shape, basis.dtype),
-            pltpu.SemaphoreType.DMA((6,)),
+            pltpu.SMEM((8, LANES), f32),
+            pltpu.SemaphoreType.DMA((2,)),
         ],
         compiler_params=params,
         name="product",
-    )(
-        near, far_leaf, far_cluster, cluster_proxy, transfer, basis,
-        own, from_left, from_right, total, table, beyond,
-    )
+    )(near, far_leaf, transfer, basis, own, from_left, from_right, total, table, beyond)
 
 
 def solution(mesh):

time: 37 us -> 35.3 us (0.954)
  Pallas kernels: 11.4 us -> 10.2 us
  local copies, waits for them, and re-layouts: 1.6 us -> 0.99 us
    pallas_call x2, Pallas kernels: 8 us -> 6.89 us  [the longest x1 3.72 us: shards(): pl.pallas_call(product_kernel, in_specs=[hbm] + [vmem] * 9, out_specs=vme...]
    unnamed x18 -> x14, local copies, waits for them, and re-layouts: 1.6 us -> 0.99 us
  transfers between devices with their start and end apart: 4 -> 4, of which waited for: 0 -> 0; matrix products, arithmetic and copies ran while one was open for 0% -> 0% of each run, Pallas kernels for 9% -> 10%
where the time goes in v4:
time: 35.3 us; the launch traced here: 34.9 us
  starting transfers between devices  23.5 us (67%)
  Pallas kernels  10.2 us (29%)
  local copies, waits for them, and re-layouts  0.99 us (3%)
    all_to_all x1, starting transfers between devices, shards(): lax.all_to_all(spread, axes, 0, 0, tiled=True, axis_index_groups=[list(ra...  7.46 us
    ppermute x1, starting transfers between devices, shards(): beyond = lax.ppermute(table, 'leaf', shift)  6.25 us
    ppermute x1, starting transfers between devices, shards(): lax.ppermute(left, axes, [(i + 1, i) for i in range(count - 1)])  6.08 us
    pallas_call x1, Pallas kernels, shards(): pl.pallas_call(product_kernel, in_specs=[hbm] + [vmem] * 9, out_specs=vme...  3.72 us
    ppermute x1, starting transfers between devices, shards(): lax.ppermute(right, axes, [(i, i + 1) for i in range(count - 1)])  3.7 us
    pallas_call x1, Pallas kernels, shards(): pl.pallas_call(near_kernel, in_specs=[hbm, vmem], out_specs=vmem, out_sha...  3.36 us
    pallas_call x1, Pallas kernels, shards(): pl.pallas_call(prepare_kernel, in_specs=[hbm] * 8, out_specs=[vmem] * 4,...  3.17 us
    unnamed x14, local copies, waits for them, and re-layouts  0.99 us
  transfers between devices with their start and end apart: 4, of which 0 were waited for; matrix products, arithmetic and copies ran while one was open for 0% of the time, Pallas kernels for 10%

profile of v4, /device:TPU:96, one launch (start us, length us, event | category | flops | bytes accessed | tf_op | source)
XLA Modules:
  0.0 34.9 jit_solution(5423291036320372881)
XLA Ops:
  0.0 3.2 %prepare.1 = (f32[8,10368]{1,0:T(8,128)}, f32[8,1792]{1,0:T(8,128)}, f32[8,1792]{1,0:T(8,128)}, f32[32,8,128]{2,1,0:T(8,128)}) custom-call(bf16[8,4096]{1,0:T(8,128)(2,1)} %charges.1, f32[3,4096]{1,0:T(4,128)} %points.1, s32[32,128]{1,0:T(8,128)} %bitcast.9, bf16[16,64,256]{2,1,0:T(8,128)(2,1)} %basis.3, f32[16,64,64]{2,1,0:T(8,128)} %transfer.3, ...), custom_call_target="tpu_custom_call" | custom-call | tf_op jit(solution)/shard_map/prepare/pallas_call | solution.py:428
  3.2 0.0 copy-start.6
  3.2 0.0 copy-start.5
  3.2 7.5 %all-to-all-start = ((f32[32,8,128]{2,1,0:T(8,128)}), f32[32,8,128]{2,1,0:T(8,128)S(1)}, u32[]{:S(2)}, u32[]{:S(2)}) async-start(f32[32,8,128]{2,1,0:T(8,128)} %get-tuple-element.12), calls=%async_computation | async-start | bytes 262144 | tf_op jit(solution)/shard_map/all_to_all | solution.py:446
  10.7 0.0 copy-start.3
  10.7 0.0 copy-done.6
  10.7 3.7 %collective-permute-start = (f32[8,1792]{1,0:T(8,128)S(1)}, f32[8,1792]{1,0:T(8,128)S(1)}, u32[]{:S(2)}, u32[]{:S(2)}) collective-permute-start(f32[8,1792]{1,0:T(8,128)S(1)} %copy-done.6), channel_id=1, source_target_pairs={{0,1},{1,2},{2,3},{3,4},{4,5},{5,6},{6,7},{7,8},{8,9},{9,10},{10,1... | collective-permute-start | bytes 172040 | tf_op jit(solution)/shard_map/ppermute | solution.py:450
  14.4 0.0 copy-done.5
  14.4 6.1 %collective-permute-start.1 = (f32[8,1792]{1,0:T(8,128)S(1)}, f32[8,1792]{1,0:T(8,128)S(1)}, u32[]{:S(2)}, u32[]{:S(2)}) collective-permute-start(f32[8,1792]{1,0:T(8,128)S(1)} %copy-done.5), channel_id=1, source_target_pairs={{1,0},{2,1},{3,2},{4,3},{5,4},{6,5},{7,6},{8,7},{9,8},{10,9},{11,1... | collective-permute-start | bytes 172040 | tf_op jit(solution)/shard_map/ppermute | solution.py:451
  20.5 0.0 all-to-all-done.table
  20.5 6.2 %collective-permute-start.2 = (f32[32,8,128]{2,1,0:T(8,128)S(1)}, f32[32,8,128]{2,1,0:T(8,128)S(1)}, u32[]{:S(2)}, u32[]{:S(2)}) collective-permute-start(f32[32,8,128]{2,1,0:T(8,128)S(1)} %all-to-all-done.table), channel_id=1, source_target_pairs={{0,32},{4,36},{8,40},{12,44},{32,64},{36,68},{40,72},{44,76},{64,9... | collective-permute-start | bytes 393224 | tf_op jit(solution)/shard_map/ppermute | solution.py:454
  26.8 0.0 copy-done.3
  26.8 0.0 copy-start.2
  26.8 1.0 %copy-done.2 = f32[8,10368]{1,0:T(8,128)S(1)} copy-done((f32[8,10368]{1,0:T(8,128)S(1)}, f32[8,10368]{1,0:T(8,128)}, u32[]{:S(2)}) %copy-start.2) | copy-done | bytes 331800
  27.8 0.0 copy-start
  27.8 0.0 copy-start.1
  27.8 0.0 copy-start.4
  27.8 3.4 %near_field.1.total = f32[8,4096]{1,0:T(8,128)S(1)} custom-call(s32[5,16]{1,0:T(8,128)S(1)} %bitcast.5, f32[8,10368]{1,0:T(8,128)S(1)} %copy-done.2), custom_call_target="tpu_custom_call" | custom-call | flops 8999999488 | bytes 1000000 | tf_op jit(solution)/shard_map/near_field/pallas_call | solution.py:455
  31.1 0.0 collective-permute-done.from_left
  31.1 0.0 collective-permute-done.1.from_right
  31.1 0.0 collective-permute-done.2.beyond
  31.2 0.0 copy-done
  31.2 0.0 copy-done.1
  31.2 0.0 copy-done.4
  31.2 3.7 %product.1 = f32[8,4096]{1,0:T(8,128)} custom-call(s32[5,16]{1,0:T(8,128)S(1)} %bitcast.6, s32[8,16]{1,0:T(8,128)S(1)} %bitcast.7, f32[16,64,64]{2,1,0:T(8,128)S(1)} %copy-done, bf16[16,64,256]{2,1,0:T(8,128)(2,1)S(1)} %copy-done.1, f32[8,10368]{1,0:T(8,128)S(1)} %copy-done.2, f32[8,1792]{1,0:T(8,128)S(1)} %collective-permute-done.from_left, ...), custom_call_target="tpu_custom_call" | custom-call | tf_op jit(solution)/shard_map/product/pallas_call | solution.py:473
Async XLA Ops:
  3.2 7.5 %copy-start.6 = (f32[8,1792]{1,0:T(8,128)S(1)}, f32[8,1792]{1,0:T(8,128)}, u32[]{:S(2)}) copy-start(f32[8,1792]{1,0:T(8,128)} %get-tuple-element.10) | copy-start | bytes 172036
  3.2 11.2 %copy-start.5 = (f32[8,1792]{1,0:T(8,128)S(1)}, f32[8,1792]{1,0:T(8,128)}, u32[]{:S(2)}) copy-start(f32[8,1792]{1,0:T(8,128)} %get-tuple-element.11) | copy-start | bytes 172036
  3.2 17.3 %all-to-all-start = ((f32[32,8,128]{2,1,0:T(8,128)}), f32[32,8,128]{2,1,0:T(8,128)S(1)}, u32[]{:S(2)}, u32[]{:S(2)}) async-start(f32[32,8,128]{2,1,0:T(8,128)} %get-tuple-element.12), calls=%async_computation | async-start | bytes 262144 | tf_op jit(solution)/shard_map/all_to_all | solution.py:446
  10.7 16.1 %copy-start.3 = (s32[16,5]{0,1:T(8,128)S(1)}, s32[16,5]{0,1:T(8,128)}, u32[]{:S(2)}) copy-start(s32[16,5]{0,1:T(8,128)} %param.17) | copy-start | bytes 964
  10.7 20.4 %collective-permute-start = (f32[8,1792]{1,0:T(8,128)S(1)}, f32[8,1792]{1,0:T(8,128)S(1)}, u32[]{:S(2)}, u32[]{:S(2)}) collective-permute-start(f32[8,1792]{1,0:T(8,128)S(1)} %copy-done.6), channel_id=1, source_target_pairs={{0,1},{1,2},{2,3},{3,4},{4,5},{5,6},{6,7},{7,8},{8,9},{9,10},{10,1... | collective-permute-start | bytes 172040 | tf_op jit(solution)/shard_map/ppermute | solution.py:450
  14.4 16.7 %collective-permute-start.1 = (f32[8,1792]{1,0:T(8,128)S(1)}, f32[8,1792]{1,0:T(8,128)S(1)}, u32[]{:S(2)}, u32[]{:S(2)}) collective-permute-start(f32[8,1792]{1,0:T(8,128)S(1)} %copy-done.5), channel_id=1, source_target_pairs={{1,0},{2,1},{3,2},{4,3},{5,4},{6,5},{7,6},{8,7},{9,8},{10,9},{11,1... | collective-permute-start | bytes 172040 | tf_op jit(solution)/shard_map/ppermute | solution.py:451
  20.5 10.6 %collective-permute-start.2 = (f32[32,8,128]{2,1,0:T(8,128)S(1)}, f32[32,8,128]{2,1,0:T(8,128)S(1)}, u32[]{:S(2)}, u32[]{:S(2)}) collective-permute-start(f32[32,8,128]{2,1,0:T(8,128)S(1)} %all-to-all-done.table), channel_id=1, source_target_pairs={{0,32},{4,36},{8,40},{12,44},{32,64},{36,68},{40,72},{44,76},{64,9... | collective-permute-start | bytes 393224 | tf_op jit(solution)/shard_map/ppermute | solution.py:454
  26.8 1.0 %copy-start.2 = (f32[8,10368]{1,0:T(8,128)S(1)}, f32[8,10368]{1,0:T(8,128)}, u32[]{:S(2)}) copy-start(f32[8,10368]{1,0:T(8,128)} %get-tuple-element.9.own) | copy-start | bytes 995332
  27.8 3.4 %copy-start = (f32[16,64,64]{2,1,0:T(8,128)S(1)}, f32[16,64,64]{2,1,0:T(8,128)}, u32[]{:S(2)}) copy-start(f32[16,64,64]{2,1,0:T(8,128)} %transfer.3) | copy-start | bytes 786436
  27.8 3.4 %copy-start.1 = (bf16[16,64,256]{2,1,0:T(8,128)(2,1)S(1)}, bf16[16,64,256]{2,1,0:T(8,128)(2,1)}, u32[]{:S(2)}) copy-start(bf16[16,64,256]{2,1,0:T(8,128)(2,1)} %basis.3) | copy-start | bytes 1572868
  27.8 3.4 %copy-start.4 = (s32[16,8]{0,1:T(8,128)S(1)}, s32[16,8]{0,1:T(8,128)}, u32[]{:S(2)}) copy-start(s32[16,8]{0,1:T(8,128)} %param.18) | copy-start | bytes 1540

commit v5 on v4

--- a/solution.py
+++ b/solution.py
@@ -77,7 +77,7 @@
 
 def prepare_kernel(
     charges, points, order, basis, transfer, leaf_proxy, cluster_proxy, far_cluster,
-    own, right, left, spread,
+    own, inner, outer, spread,
     twice, entry, charges_in, points_in, order_in, basis_in, transfer_in, leaf_proxy_in, cluster_proxy_in, far_cluster_in, sems,
 ):
     copies = [
@@ -155,13 +155,16 @@
     for place in range(PLANE * NSUB):
         spread[place] = entry[...]
 
+    odd = lax.rem(lax.axis_index("sub"), 2) == 1
     at = 0
     for start, whole, width in (
         (AT_CHARGES, PTS, NEAR_W), (AT_POINTS, PTS, NEAR_W),
         (AT_COEFFS, RANKS, FAR_W), (AT_PROXY, RANKS, FAR_W),
     ):
-        left[:, at : at + width] = own[:, start : start + width]
-        right[:, at : at + width] = own[:, start + whole - width : start + whole]
+        low = own[:, start : start + width]
+        high = own[:, start + whole - width : start + whole]
+        inner[:, at : at + width] = jnp.where(odd, low, high)
+        outer[:, at : at + width] = jnp.where(odd, high, low)
         at += width
 
 
@@ -253,7 +256,7 @@
 
 
 def product_kernel(
-    near_list, far_leaf, transfer, basis, own, from_left, from_right, total, table, beyond,
+    near_list, far_leaf, transfer, basis, own, outer, inner, total, table, beyond,
     out,
     down, coeffs, sources, targets, block, high, low, far_rows, near, far_cluster, sems,
 ):
@@ -266,6 +269,9 @@
     group = lax.axis_index("leaf")
     cluster = group * NSUB + lax.axis_index("sub")
     first = cluster * OWN
+    odd = lax.rem(lax.axis_index("sub"), 2) == 1
+    from_left = jnp.where(odd, inner[...], outer[...])
+    from_right = jnp.where(odd, outer[...], inner[...])
 
     out[...] = total[...]
     down[...] = jnp.zeros_like(down)
@@ -425,7 +431,7 @@
     near, far_leaf = near.transpose(1, 0), far_leaf.transpose(1, 0)
     given = (charges, points, order.reshape(PTS // LANES, LANES), basis, transfer, leaf_proxy, cluster_proxy, far_cluster)
     size = PLANE * NSUB
-    own, right, left, spread = pl.pallas_call(
+    own, inner, outer, spread = pl.pallas_call(
         prepare_kernel,
         in_specs=[hbm] * 8,
         out_specs=[vmem] * 4,
@@ -447,8 +453,8 @@
         spread, axes, 0, 0, tiled=True,
         axis_index_groups=[list(range(i, i + size)) for i in range(0, count, size)],
     )
-    from_left = lax.ppermute(right, axes, [(i, i + 1) for i in range(count - 1)])
-    from_right = lax.ppermute(left, axes, [(i + 1, i) for i in range(count - 1)])
+    outer = lax.ppermute(outer, axes, [(i, ((i + 1) ^ 1) - 1) for i in range(1, count - 1)])
+    inner = lax.ppermute(inner, axes, [(i, i ^ 1) for i in range(count)])
     shift = [(g - PLANE, g) for g in range(PLANE, groups) if g % PLANE < HALF]
     shift += [(g + PLANE, g) for g in range(groups - PLANE) if g % PLANE >= HALF]
     beyond = lax.ppermute(table, "leaf", shift)
@@ -490,7 +496,7 @@
         ],
         compiler_params=params,
         name="product",
-    )(near, far_leaf, transfer, basis, own, from_left, from_right, total, table, beyond)
+    )(near, far_leaf, transfer, basis, own, outer, inner, total, table, beyond)
 
 
 def solution(mesh):

time: 35.3 us -> 33.8 us (0.958)
  the two profiles are of different devices: /device:TPU:96 before, /device:TPU:392 now
where the time goes in v5:
time: 33.8 us; the launch traced here: 33.4 us
  starting transfers between devices  20.2 us (60%)
  Pallas kernels  10.3 us (30%)
  waiting for transfers between devices  1.78 us (5%)
  local copies, waits for them, and re-layouts  0.99 us (3%)
    all_to_all x1, starting transfers between devices, shards(): lax.all_to_all(spread, axes, 0, 0, tiled=True, axis_index_groups=[list(ra...  7.68 us
    ppermute x1, starting transfers between devices, shards(): inner = lax.ppermute(inner, axes, [(i, i ^ 1) for i in range(count)])  7.27 us
    pallas_call x1, Pallas kernels, shards(): pl.pallas_call(product_kernel, in_specs=[hbm] + [vmem] * 9, out_specs=vme...  3.73 us
    ppermute x1, starting transfers between devices, shards(): lax.ppermute(outer, axes, [(i, (i + 1 ^ 1) - 1) for i in range(1, count -...  3.37 us
    pallas_call x1, Pallas kernels, shards(): pl.pallas_call(near_kernel, in_specs=[hbm, vmem], out_specs=vmem, out_sha...  3.35 us
    pallas_call x1, Pallas kernels, shards(): pl.pallas_call(prepare_kernel, in_specs=[hbm] * 8, out_specs=[vmem] * 4,...  3.18 us
    ppermute x1, starting transfers between devices, shards(): beyond = lax.ppermute(table, 'leaf', shift)  1.92 us
    ppermute x1, waiting for transfers between devices, shards(): beyond = lax.ppermute(table, 'leaf', shift)  1.77 us
  transfers between devices with their start and end apart: 4, of which 1 were waited for; matrix products, arithmetic and copies ran while one was open for 0% of the time, Pallas kernels for 10%

profile of v5, /device:TPU:392, one launch (start us, length us, event | category | flops | bytes accessed | tf_op | source)
XLA Modules:
  0.0 33.4 jit_solution(5169342890091756680)
XLA Ops:
  0.0 3.2 %prepare.1 = (f32[8,10368]{1,0:T(8,128)}, f32[8,1792]{1,0:T(8,128)}, f32[8,1792]{1,0:T(8,128)}, f32[32,8,128]{2,1,0:T(8,128)}) custom-call(bf16[8,4096]{1,0:T(8,128)(2,1)} %charges.1, f32[3,4096]{1,0:T(4,128)} %points.1, s32[32,128]{1,0:T(8,128)} %bitcast.9, bf16[16,64,256]{2,1,0:T(8,128)(2,1)} %basis.3, f32[16,64,64]{2,1,0:T(8,128)} %transfer.3, ...), custom_call_target="tpu_custom_call" | custom-call | tf_op jit(solution)/shard_map/prepare/pallas_call | solution.py:434
  3.2 0.0 copy-start.6
  3.2 0.0 copy-start.5
  3.2 7.7 %all-to-all-start = ((f32[32,8,128]{2,1,0:T(8,128)}), f32[32,8,128]{2,1,0:T(8,128)S(1)}, u32[]{:S(2)}, u32[]{:S(2)}) async-start(f32[32,8,128]{2,1,0:T(8,128)} %get-tuple-element.12), calls=%async_computation | async-start | bytes 262144 | tf_op jit(solution)/shard_map/all_to_all | solution.py:452
  10.9 0.0 copy-start.3
  10.9 0.0 copy-done.6
  10.9 3.4 %collective-permute-start = (f32[8,1792]{1,0:T(8,128)S(1)}, f32[8,1792]{1,0:T(8,128)S(1)}, u32[]{:S(2)}, u32[]{:S(2)}) collective-permute-start(f32[8,1792]{1,0:T(8,128)S(1)} %copy-done.6), channel_id=1, source_target_pairs={{1,2},{2,1},{3,4},{4,3},{5,6},{6,5},{7,8},{8,7},{9,10},{10,9},{11,... | collective-permute-start | bytes 172040 | tf_op jit(solution)/shard_map/ppermute | solution.py:456
  14.3 0.0 copy-done.5
  14.3 7.3 %collective-permute-start.1 = (f32[8,1792]{1,0:T(8,128)S(1)}, f32[8,1792]{1,0:T(8,128)S(1)}, u32[]{:S(2)}, u32[]{:S(2)}) collective-permute-start(f32[8,1792]{1,0:T(8,128)S(1)} %copy-done.5), channel_id=1, source_target_pairs={{0,1},{1,0},{2,3},{3,2},{4,5},{5,4},{6,7},{7,6},{8,9},{9,8},{10,11... | collective-permute-start | bytes 172040 | tf_op jit(solution)/shard_map/ppermute | solution.py:457
  21.6 0.0 all-to-all-done.table
  21.6 1.9 %collective-permute-start.2 = (f32[32,8,128]{2,1,0:T(8,128)S(1)}, f32[32,8,128]{2,1,0:T(8,128)S(1)}, u32[]{:S(2)}, u32[]{:S(2)}) collective-permute-start(f32[32,8,128]{2,1,0:T(8,128)S(1)} %all-to-all-done.table), channel_id=1, source_target_pairs={{0,32},{4,36},{8,40},{12,44},{32,64},{36,68},{40,72},{44,76},{64,9... | collective-permute-start | bytes 393224 | tf_op jit(solution)/shard_map/ppermute | solution.py:460
  23.5 0.0 copy-done.3
  23.5 0.0 copy-start.2
  23.5 1.0 %copy-done.2 = f32[8,10368]{1,0:T(8,128)S(1)} copy-done((f32[8,10368]{1,0:T(8,128)S(1)}, f32[8,10368]{1,0:T(8,128)}, u32[]{:S(2)}) %copy-start.2) | copy-done | bytes 331800
  24.5 0.0 copy-start
  24.5 0.0 copy-start.1
  24.5 0.0 copy-start.4
  24.5 3.4 %near_field.1.total = f32[8,4096]{1,0:T(8,128)S(1)} custom-call(s32[5,16]{1,0:T(8,128)S(1)} %bitcast.5, f32[8,10368]{1,0:T(8,128)S(1)} %copy-done.2), custom_call_target="tpu_custom_call" | custom-call | flops 8999999488 | bytes 1000000 | tf_op jit(solution)/shard_map/near_field/pallas_call | solution.py:461
  27.9 0.0 collective-permute-done.outer
  27.9 0.0 collective-permute-done.1.inner
  27.9 1.8 %collective-permute-done.2.beyond = f32[32,8,128]{2,1,0:T(8,128)S(1)} collective-permute-done((f32[32,8,128]{2,1,0:T(8,128)S(1)}, f32[32,8,128]{2,1,0:T(8,128)S(1)}, u32[]{:S(2)}, u32[]{:S(2)}) %collective-permute-start.2) | collective-permute-done | bytes 131104 | tf_op jit(solution)/shard_map/ppermute | solution.py:460
  29.7 0.0 copy-done
  29.7 0.0 copy-done.1
  29.7 0.0 copy-done.4
  29.7 3.7 %product.1 = f32[8,4096]{1,0:T(8,128)} custom-call(s32[5,16]{1,0:T(8,128)S(1)} %bitcast.6, s32[8,16]{1,0:T(8,128)S(1)} %bitcast.7, f32[16,64,64]{2,1,0:T(8,128)S(1)} %copy-done, bf16[16,64,256]{2,1,0:T(8,128)(2,1)S(1)} %copy-done.1, f32[8,10368]{1,0:T(8,128)S(1)} %copy-done.2, f32[8,1792]{1,0:T(8,128)S(1)} %collective-permute-done.outer, ...), custom_call_target="tpu_custom_call" | custom-call | tf_op jit(solution)/shard_map/product/pallas_call | solution.py:479
Async XLA Ops:
  3.2 7.7 %copy-start.6 = (f32[8,1792]{1,0:T(8,128)S(1)}, f32[8,1792]{1,0:T(8,128)}, u32[]{:S(2)}) copy-start(f32[8,1792]{1,0:T(8,128)} %get-tuple-element.10) | copy-start | bytes 172036
  3.2 11.1 %copy-start.5 = (f32[8,1792]{1,0:T(8,128)S(1)}, f32[8,1792]{1,0:T(8,128)}, u32[]{:S(2)}) copy-start(f32[8,1792]{1,0:T(8,128)} %get-tuple-element.11) | copy-start | bytes 172036
  3.2 18.4 %all-to-all-start = ((f32[32,8,128]{2,1,0:T(8,128)}), f32[32,8,128]{2,1,0:T(8,128)S(1)}, u32[]{:S(2)}, u32[]{:S(2)}) async-start(f32[32,8,128]{2,1,0:T(8,128)} %get-tuple-element.12), calls=%async_computation | async-start | bytes 262144 | tf_op jit(solution)/shard_map/all_to_all | solution.py:452
  10.9 12.6 %copy-start.3 = (s32[16,5]{0,1:T(8,128)S(1)}, s32[16,5]{0,1:T(8,128)}, u32[]{:S(2)}) copy-start(s32[16,5]{0,1:T(8,128)} %param.17) | copy-start | bytes 964
  10.9 17.0 %collective-permute-start = (f32[8,1792]{1,0:T(8,128)S(1)}, f32[8,1792]{1,0:T(8,128)S(1)}, u32[]{:S(2)}, u32[]{:S(2)}) collective-permute-start(f32[8,1792]{1,0:T(8,128)S(1)} %copy-done.6), channel_id=1, source_target_pairs={{1,2},{2,1},{3,4},{4,3},{5,6},{6,5},{7,8},{8,7},{9,10},{10,9},{11,... | collective-permute-start | bytes 172040 | tf_op jit(solution)/shard_map/ppermute | solution.py:456
  14.3 13.6 %collective-permute-start.1 = (f32[8,1792]{1,0:T(8,128)S(1)}, f32[8,1792]{1,0:T(8,128)S(1)}, u32[]{:S(2)}, u32[]{:S(2)}) collective-permute-start(f32[8,1792]{1,0:T(8,128)S(1)} %copy-done.5), channel_id=1, source_target_pairs={{0,1},{1,0},{2,3},{3,2},{4,5},{5,4},{6,7},{7,6},{8,9},{9,8},{10,11... | collective-permute-start | bytes 172040 | tf_op jit(solution)/shard_map/ppermute | solution.py:457
  21.6 8.1 %collective-permute-start.2 = (f32[32,8,128]{2,1,0:T(8,128)S(1)}, f32[32,8,128]{2,1,0:T(8,128)S(1)}, u32[]{:S(2)}, u32[]{:S(2)}) collective-permute-start(f32[32,8,128]{2,1,0:T(8,128)S(1)} %all-to-all-done.table), channel_id=1, source_target_pairs={{0,32},{4,36},{8,40},{12,44},{32,64},{36,68},{40,72},{44,76},{64,9... | collective-permute-start | bytes 393224 | tf_op jit(solution)/shard_map/ppermute | solution.py:460
  23.5 1.0 %copy-start.2 = (f32[8,10368]{1,0:T(8,128)S(1)}, f32[8,10368]{1,0:T(8,128)}, u32[]{:S(2)}) copy-start(f32[8,10368]{1,0:T(8,128)} %get-tuple-element.9.own) | copy-start | bytes 995332
  24.5 5.2 %copy-start = (f32[16,64,64]{2,1,0:T(8,128)S(1)}, f32[16,64,64]{2,1,0:T(8,128)}, u32[]{:S(2)}) copy-start(f32[16,64,64]{2,1,0:T(8,128)} %transfer.3) | copy-start | bytes 786436
  24.5 5.2 %copy-start.1 = (bf16[16,64,256]{2,1,0:T(8,128)(2,1)S(1)}, bf16[16,64,256]{2,1,0:T(8,128)(2,1)}, u32[]{:S(2)}) copy-start(bf16[16,64,256]{2,1,0:T(8,128)(2,1)} %basis.3) | copy-start | bytes 1572868
  24.5 5.2 %copy-start.4 = (s32[16,8]{0,1:T(8,128)S(1)}, s32[16,8]{0,1:T(8,128)}, u32[]{:S(2)}) copy-start(s32[16,8]{0,1:T(8,128)} %param.18) | copy-start | bytes 1540

commit v6 on v5

--- a/solution.py
+++ b/solution.py
@@ -18,8 +18,9 @@
 PTS = OWN * LEAF
 RANKS = OWN * RANK
 LANES = 128
-BUFFERS = 4
-AHEAD = 2
+BUFFERS = 6
+LATER = 3
+AHEAD = 3
 SCALE = 16.0
 SHIFT = 2.56
 
@@ -111,7 +112,28 @@
         for k in range(2):
             own[:, (2 * i + k) * LANES : (2 * i + k + 1) * LANES] = got[NRHS * k : NRHS * (k + 1)]
 
+    for copy in copies[3:]:
+        copy.wait()
+    for g in range(OWN):
+        at = AT_PROXY + g * RANK
+        own[0:3, at : at + RANK] = leaf_proxy_in[:, g, :] * SCALE
+    own[:, AT_LIST:] = jnp.zeros((8, LANES), jnp.float32)
+    own[0:1, AT_LIST : AT_LIST + far_cluster_in.shape[1]] = far_cluster_in[...].astype(jnp.float32)
+
+    first_half = lax.broadcasted_iota(jnp.int32, (NRHS, LANES), 1) < RANK
+    parent = jnp.zeros((NRHS, RANK), jnp.float32)
     for j in range(blocks // 8):
+        pairs = range(2 * j, 2 * j + 2)
+        both = [
+            dot(
+                jnp.concatenate(
+                    [own[:, g * LEAF : (g + 1) * LEAF].astype(jnp.bfloat16) for g in (2 * m, 2 * m + 1)], axis=0
+                ),
+                jnp.reshape(basis_in[2 * m : 2 * m + 2], (2 * RANK, LEAF)),
+                NT,
+            )
+            for m in pairs
+        ]
         index = order_in[8 * j : 8 * j + 8, :]
         for c in range(3):
             got = picked(
@@ -121,33 +143,10 @@
             for s in range(8):
                 at = AT_POINTS + (8 * j + s) * LANES
                 own[c : c + 1, at : at + LANES] = got[s : s + 1]
-
-    for copy in copies[3:]:
-        copy.wait()
-    for g in range(OWN):
-        at = AT_PROXY + g * RANK
-        own[0:3, at : at + RANK] = leaf_proxy_in[:, g, :] * SCALE
-
-    own[:, AT_LIST:] = jnp.zeros((8, LANES), jnp.float32)
-    own[0:1, AT_LIST : AT_LIST + far_cluster_in.shape[1]] = far_cluster_in[...].astype(jnp.float32)
-
-    first_half = lax.broadcasted_iota(jnp.int32, (NRHS, LANES), 1) < RANK
-    parent = jnp.zeros((NRHS, RANK), jnp.float32)
-    pairs = range(OWN // 2)
-    both = [
-        dot(
-            jnp.concatenate(
-                [own[:, g * LEAF : (g + 1) * LEAF].astype(jnp.bfloat16) for g in (2 * m, 2 * m + 1)], axis=0
-            ),
-            jnp.reshape(basis_in[2 * m : 2 * m + 2], (2 * RANK, LEAF)),
-            NT,
-        )
-        for m in pairs
-    ]
-    coeffs = [jnp.where(first_half, both[m][:NRHS], both[m][NRHS:]) for m in pairs]
-    for m in pairs:
-        own[:, AT_COEFFS + m * LANES : AT_COEFFS + (m + 1) * LANES] = coeffs[m]
-        parent += dot3(coeffs[m], jnp.reshape(transfer_in[2 * m : 2 * m + 2], (2 * RANK, RANK)))
+        for m, pair in zip(pairs, both):
+            coeffs = jnp.where(first_half, pair[:NRHS], pair[NRHS:])
+            own[:, AT_COEFFS + m * LANES : AT_COEFFS + (m + 1) * LANES] = coeffs
+            parent += dot3(coeffs, jnp.reshape(transfer_in[2 * m : 2 * m + 2], (2 * RANK, RANK)))
 
     entry[:, 0:RANK] = parent
     entry[0:3, RANK : 2 * RANK] = cluster_proxy_in[:, 0, :] * SCALE
@@ -234,7 +233,7 @@
     copy.wait()
 
     sums = [0.0] * OWN
-    for step in range(OWN + 1):
+    for step in range(OWN + LATER):
         for d in range(REACH + 1):
             h = step
             if h + d < OWN:
@@ -243,7 +242,7 @@
                     targets[:, (h + d) * LEAF : (h + d + 1) * LEAF],
                     block.at[h % BUFFERS, d],
                 )
-            h = step - 1
+            h = step - LATER
             if h >= 0 and h + d < OWN:
                 here = slice(h * LEAF, (h + 1) * LEAF)
                 there = slice((h + d) * LEAF, (h + d + 1) * LEAF)
@@ -251,8 +250,8 @@
                 sums[h + d] += dot(charges[:, here], values) * listed(h + d, h)
                 if d > 0:
                     sums[h] += dot(charges[:, there], values, NT) * listed(h, h + d)
-        if step > 0:
-            total[:, (step - 1) * LEAF : step * LEAF] = sums[step - 1]
+        if step >= LATER:
+            total[:, (step - LATER) * LEAF : (step - LATER + 1) * LEAF] = sums[step - LATER]
 
 
 def product_kernel(
@@ -285,8 +284,6 @@
         at = (0, FAR_W, FAR_W + RANKS)[t]
         sources[at : at + proxies.shape[1], :] = features(proxies, True).T
         targets[:, at : at + proxies.shape[1]] = features(proxies, False)
-    for copy in copies:
-        copy.wait()
     listed = listing(near, first)
 
     def edges(side, message):
@@ -368,6 +365,9 @@
     steps += edges(0, from_left) + edges(1, from_right)
     products = {}
     for i in range(len(steps) + AHEAD + 1):
+        if i == (FREACH + OWN) // 2:
+            for copy in copies:
+                copy.wait()
         if i < len(steps):
             steps[i][0]()
         if 0 <= i - AHEAD < len(steps):

time: 33.8 us -> 33.3 us (0.985)
  Pallas kernels: 10.3 us -> 9.64 us
    pallas_call x1, Pallas kernels: 3.73 us -> 3.32 us  [shards(): pl.pallas_call(product_kernel, in_specs=[hbm] + [vmem] * 9, out_specs=vme...]
where the time goes in v6:
time: 33.3 us; the launch traced here: 32.9 us
  starting transfers between devices  20.2 us (61%)
  Pallas kernels  9.64 us (29%)
  waiting for transfers between devices  1.93 us (6%)
  local copies, waits for them, and re-layouts  0.99 us (3%)
    all_to_all x1, starting transfers between devices, shards(): lax.all_to_all(spread, axes, 0, 0, tiled=True, axis_index_groups=[list(ra...  7.68 us
    ppermute x1, starting transfers between devices, shards(): inner = lax.ppermute(inner, axes, [(i, i ^ 1) for i in range(count)])  7.27 us
    ppermute x1, starting transfers between devices, shards(): lax.ppermute(outer, axes, [(i, (i + 1 ^ 1) - 1) for i in range(1, count -...  3.37 us
    pallas_call x1, Pallas kernels, shards(): pl.pallas_call(product_kernel, in_specs=[hbm] + [vmem] * 9, out_specs=vme...  3.32 us
    pallas_call x1, Pallas kernels, shards(): pl.pallas_call(near_kernel, in_specs=[hbm, vmem], out_specs=vmem, out_sha...  3.2 us
    pallas_call x1, Pallas kernels, shards(): pl.pallas_call(prepare_kernel, in_specs=[hbm] * 8, out_specs=[vmem] * 4,...  3.12 us
    ppermute x1, starting transfers between devices, shards(): beyond = lax.ppermute(table, 'leaf', shift)  1.92 us
    ppermute x1, waiting for transfers between devices, shards(): beyond = lax.ppermute(table, 'leaf', shift)  1.92 us
  transfers between devices with their start and end apart: 4, of which 1 were waited for; matrix products, arithmetic and copies ran while one was open for 0% of the time, Pallas kernels for 10%

profile of v6, /device:TPU:392, one launch (start us, length us, event | category | flops | bytes accessed | tf_op | source)
XLA Modules:
  0.0 32.9 jit_solution(1489660513119192416)
XLA Ops:
  0.0 3.1 %prepare.1 = (f32[8,10368]{1,0:T(8,128)}, f32[8,1792]{1,0:T(8,128)}, f32[8,1792]{1,0:T(8,128)}, f32[32,8,128]{2,1,0:T(8,128)}) custom-call(bf16[8,4096]{1,0:T(8,128)(2,1)} %charges.1, f32[3,4096]{1,0:T(4,128)} %points.1, s32[32,128]{1,0:T(8,128)} %bitcast.9, bf16[16,64,256]{2,1,0:T(8,128)(2,1)} %basis.3, f32[16,64,64]{2,1,0:T(8,128)} %transfer.3, ...), custom_call_target="tpu_custom_call" | custom-call | tf_op jit(solution)/shard_map/prepare/pallas_call | solution.py:434
  3.1 0.0 copy-start.6
  3.1 0.0 copy-start.5
  3.1 7.7 %all-to-all-start = ((f32[32,8,128]{2,1,0:T(8,128)}), f32[32,8,128]{2,1,0:T(8,128)S(1)}, u32[]{:S(2)}, u32[]{:S(2)}) async-start(f32[32,8,128]{2,1,0:T(8,128)} %get-tuple-element.12), calls=%async_computation | async-start | bytes 262144 | tf_op jit(solution)/shard_map/all_to_all | solution.py:452
  10.8 0.0 copy-start.3
  10.8 0.0 copy-done.6
  10.9 3.4 %collective-permute-start = (f32[8,1792]{1,0:T(8,128)S(1)}, f32[8,1792]{1,0:T(8,128)S(1)}, u32[]{:S(2)}, u32[]{:S(2)}) collective-permute-start(f32[8,1792]{1,0:T(8,128)S(1)} %copy-done.6), channel_id=1, source_target_pairs={{1,2},{2,1},{3,4},{4,3},{5,6},{6,5},{7,8},{8,7},{9,10},{10,9},{11,... | collective-permute-start | bytes 172040 | tf_op jit(solution)/shard_map/ppermute | solution.py:456
  14.2 0.0 copy-done.5
  14.2 7.3 %collective-permute-start.1 = (f32[8,1792]{1,0:T(8,128)S(1)}, f32[8,1792]{1,0:T(8,128)S(1)}, u32[]{:S(2)}, u32[]{:S(2)}) collective-permute-start(f32[8,1792]{1,0:T(8,128)S(1)} %copy-done.5), channel_id=1, source_target_pairs={{0,1},{1,0},{2,3},{3,2},{4,5},{5,4},{6,7},{7,6},{8,9},{9,8},{10,11... | collective-permute-start | bytes 172040 | tf_op jit(solution)/shard_map/ppermute | solution.py:457
  21.5 0.0 all-to-all-done.table
  21.5 1.9 %collective-permute-start.2 = (f32[32,8,128]{2,1,0:T(8,128)S(1)}, f32[32,8,128]{2,1,0:T(8,128)S(1)}, u32[]{:S(2)}, u32[]{:S(2)}) collective-permute-start(f32[32,8,128]{2,1,0:T(8,128)S(1)} %all-to-all-done.table), channel_id=1, source_target_pairs={{0,32},{4,36},{8,40},{12,44},{32,64},{36,68},{40,72},{44,76},{64,9... | collective-permute-start | bytes 393224 | tf_op jit(solution)/shard_map/ppermute | solution.py:460
  23.5 0.0 copy-done.3
  23.5 0.0 copy-start.2
  23.5 1.0 %copy-done.2 = f32[8,10368]{1,0:T(8,128)S(1)} copy-done((f32[8,10368]{1,0:T(8,128)S(1)}, f32[8,10368]{1,0:T(8,128)}, u32[]{:S(2)}) %copy-start.2) | copy-done | bytes 331800
  24.4 0.0 copy-start
  24.4 0.0 copy-start.1
  24.5 0.0 copy-start.4
  24.5 3.2 %near_field.1.total = f32[8,4096]{1,0:T(8,128)S(1)} custom-call(s32[5,16]{1,0:T(8,128)S(1)} %bitcast.5, f32[8,10368]{1,0:T(8,128)S(1)} %copy-done.2), custom_call_target="tpu_custom_call" | custom-call | flops 8999999488 | bytes 1000000 | tf_op jit(solution)/shard_map/near_field/pallas_call | solution.py:461
  27.7 0.0 collective-permute-done.outer
  27.7 0.0 collective-permute-done.1.inner
  27.7 1.9 %collective-permute-done.2.beyond = f32[32,8,128]{2,1,0:T(8,128)S(1)} collective-permute-done((f32[32,8,128]{2,1,0:T(8,128)S(1)}, f32[32,8,128]{2,1,0:T(8,128)S(1)}, u32[]{:S(2)}, u32[]{:S(2)}) %collective-permute-start.2) | collective-permute-done | bytes 131104 | tf_op jit(solution)/shard_map/ppermute | solution.py:460
  29.6 0.0 copy-done
  29.6 0.0 copy-done.1
  29.6 0.0 copy-done.4
  29.6 3.3 %product.1 = f32[8,4096]{1,0:T(8,128)} custom-call(s32[5,16]{1,0:T(8,128)S(1)} %bitcast.6, s32[8,16]{1,0:T(8,128)S(1)} %bitcast.7, f32[16,64,64]{2,1,0:T(8,128)S(1)} %copy-done, bf16[16,64,256]{2,1,0:T(8,128)(2,1)S(1)} %copy-done.1, f32[8,10368]{1,0:T(8,128)S(1)} %copy-done.2, f32[8,1792]{1,0:T(8,128)S(1)} %collective-permute-done.outer, ...), custom_call_target="tpu_custom_call" | custom-call | tf_op jit(solution)/shard_map/product/pallas_call | solution.py:479
Async XLA Ops:
  3.1 7.7 %copy-start.6 = (f32[8,1792]{1,0:T(8,128)S(1)}, f32[8,1792]{1,0:T(8,128)}, u32[]{:S(2)}) copy-start(f32[8,1792]{1,0:T(8,128)} %get-tuple-element.10) | copy-start | bytes 172036
  3.1 11.1 %copy-start.5 = (f32[8,1792]{1,0:T(8,128)S(1)}, f32[8,1792]{1,0:T(8,128)}, u32[]{:S(2)}) copy-start(f32[8,1792]{1,0:T(8,128)} %get-tuple-element.11) | copy-start | bytes 172036
  3.1 18.4 %all-to-all-start = ((f32[32,8,128]{2,1,0:T(8,128)}), f32[32,8,128]{2,1,0:T(8,128)S(1)}, u32[]{:S(2)}, u32[]{:S(2)}) async-start(f32[32,8,128]{2,1,0:T(8,128)} %get-tuple-element.12), calls=%async_computation | async-start | bytes 262144 | tf_op jit(solution)/shard_map/all_to_all | solution.py:452
  10.8 12.6 %copy-start.3 = (s32[16,5]{0,1:T(8,128)S(1)}, s32[16,5]{0,1:T(8,128)}, u32[]{:S(2)}) copy-start(s32[16,5]{0,1:T(8,128)} %param.17) | copy-start | bytes 964
  10.9 16.8 %collective-permute-start = (f32[8,1792]{1,0:T(8,128)S(1)}, f32[8,1792]{1,0:T(8,128)S(1)}, u32[]{:S(2)}, u32[]{:S(2)}) collective-permute-start(f32[8,1792]{1,0:T(8,128)S(1)} %copy-done.6), channel_id=1, source_target_pairs={{1,2},{2,1},{3,4},{4,3},{5,6},{6,5},{7,8},{8,7},{9,10},{10,9},{11,... | collective-permute-start | bytes 172040 | tf_op jit(solution)/shard_map/ppermute | solution.py:456
  14.2 13.4 %collective-permute-start.1 = (f32[8,1792]{1,0:T(8,128)S(1)}, f32[8,1792]{1,0:T(8,128)S(1)}, u32[]{:S(2)}, u32[]{:S(2)}) collective-permute-start(f32[8,1792]{1,0:T(8,128)S(1)} %copy-done.5), channel_id=1, source_target_pairs={{0,1},{1,0},{2,3},{3,2},{4,5},{5,4},{6,7},{7,6},{8,9},{9,8},{10,11... | collective-permute-start | bytes 172040 | tf_op jit(solution)/shard_map/ppermute | solution.py:457
  21.5 8.1 %collective-permute-start.2 = (f32[32,8,128]{2,1,0:T(8,128)S(1)}, f32[32,8,128]{2,1,0:T(8,128)S(1)}, u32[]{:S(2)}, u32[]{:S(2)}) collective-permute-start(f32[32,8,128]{2,1,0:T(8,128)S(1)} %all-to-all-done.table), channel_id=1, source_target_pairs={{0,32},{4,36},{8,40},{12,44},{32,64},{36,68},{40,72},{44,76},{64,9... | collective-permute-start | bytes 393224 | tf_op jit(solution)/shard_map/ppermute | solution.py:460
  23.5 1.0 %copy-start.2 = (f32[8,10368]{1,0:T(8,128)S(1)}, f32[8,10368]{1,0:T(8,128)}, u32[]{:S(2)}) copy-start(f32[8,10368]{1,0:T(8,128)} %get-tuple-element.9.own) | copy-start | bytes 995332
  24.4 5.2 %copy-start = (f32[16,64,64]{2,1,0:T(8,128)S(1)}, f32[16,64,64]{2,1,0:T(8,128)}, u32[]{:S(2)}) copy-start(f32[16,64,64]{2,1,0:T(8,128)} %transfer.3) | copy-start | bytes 786436
  24.4 5.2 %copy-start.1 = (bf16[16,64,256]{2,1,0:T(8,128)(2,1)S(1)}, bf16[16,64,256]{2,1,0:T(8,128)(2,1)}, u32[]{:S(2)}) copy-start(bf16[16,64,256]{2,1,0:T(8,128)(2,1)} %basis.3) | copy-start | bytes 1572868
  24.5 5.2 %copy-start.4 = (s32[16,8]{0,1:T(8,128)S(1)}, s32[16,8]{0,1:T(8,128)}, u32[]{:S(2)}) copy-start(s32[16,8]{0,1:T(8,128)} %param.18) | copy-start | bytes 1540

commit v7 on v6

--- a/solution.py
+++ b/solution.py
@@ -363,41 +363,44 @@
 
     steps = [coupling(m) for m in range((FREACH + OWN) // 2)]
     steps += edges(0, from_left) + edges(1, from_right)
+    def couple():
+        plane = group // PLANE
+        entries, kept = [], []
+        for slot in range(FAR1):
+            f = far_cluster[0, slot].astype(jnp.int32)
+            valid = f >= 0
+            f = jnp.where(valid, f, cluster)
+            mine = f // (PLANE * NSUB) == plane
+            place = lax.rem(f, PLANE * NSUB)
+            e = jnp.where(mine, table[place], beyond[place])
+            entries.append(e)
+            kept.append(e * valid.astype(jnp.float32))
+        parents, sources = [], []
+        for m in range(len(entries) // 2):
+            a, b = 2 * m, 2 * m + 1
+            parents.append(jnp.where(first_lanes, kept[a], pltpu.roll(kept[b], RANK, 1)))
+            sources.append(jnp.where(first_lanes, pltpu.roll(entries[a], RANK, 1), entries[b]))
+        parents = jnp.concatenate(parents, axis=1)
+        sources = jnp.concatenate(sources, axis=1)
+        mine = table[lax.rem(cluster, PLANE * NSUB)].T[RANK : 2 * RANK]
+        values = block_values(
+            [mine[:, c : c + 1] for c in range(3)], [sources[c : c + 1, :] for c in range(3)]
+        )
+        return dot3(parents, values, NT)
+
     products = {}
     for i in range(len(steps) + AHEAD + 1):
         if i == (FREACH + OWN) // 2:
             for copy in copies:
                 copy.wait()
+        if i == (FREACH + OWN) // 2 + 1:
+            coupled = couple()
         if i < len(steps):
             steps[i][0]()
         if 0 <= i - AHEAD < len(steps):
             products[i - AHEAD] = steps[i - AHEAD][1]()
         if 0 <= i - AHEAD - 1:
             steps[i - AHEAD - 1][2](products.pop(i - AHEAD - 1))
-
-    plane = group // PLANE
-    entries, kept = [], []
-    for slot in range(FAR1):
-        f = far_cluster[0, slot].astype(jnp.int32)
-        valid = f >= 0
-        f = jnp.where(valid, f, cluster)
-        mine = f // (PLANE * NSUB) == plane
-        place = lax.rem(f, PLANE * NSUB)
-        e = jnp.where(mine, table[place], beyond[place])
-        entries.append(e)
-        kept.append(e * valid.astype(jnp.float32))
-    parents, sources = [], []
-    for m in range(len(entries) // 2):
-        a, b = 2 * m, 2 * m + 1
-        parents.append(jnp.where(first_lanes, kept[a], pltpu.roll(kept[b], RANK, 1)))
-        sources.append(jnp.where(first_lanes, pltpu.roll(entries[a], RANK, 1), entries[b]))
-    parents = jnp.concatenate(parents, axis=1)
-    sources = jnp.concatenate(sources, axis=1)
-    mine = table[lax.rem(cluster, PLANE * NSUB)].T[RANK : 2 * RANK]
-    values = block_values(
-        [mine[:, c : c + 1] for c in range(3)], [sources[c : c + 1, :] for c in range(3)]
-    )
-    coupled = dot3(parents, values, NT)
 
     pairs = range(OWN // 2)
     lowered = [dot3(coupled, jnp.reshape(transfer[2 * m : 2 * m + 2], (2 * RANK, RANK)), NT) for m in pairs]

time: 33.3 us -> 33.3 us (level)
  no operation moved by 1% of the time
where the time goes in v7:
time: 33.3 us; the launch traced here: 33 us
  starting transfers between devices  20.2 us (61%)
  Pallas kernels  9.67 us (29%)
  waiting for transfers between devices  1.93 us (6%)
  local copies, waits for them, and re-layouts  0.99 us (3%)
    all_to_all x1, starting transfers between devices, shards(): lax.all_to_all(spread, axes, 0, 0, tiled=True, axis_index_groups=[list(ra...  7.68 us
    ppermute x1, starting transfers between devices, shards(): inner = lax.ppermute(inner, axes, [(i, i ^ 1) for i in range(count)])  7.27 us
    ppermute x1, starting transfers between devices, shards(): lax.ppermute(outer, axes, [(i, (i + 1 ^ 1) - 1) for i in range(1, count -...  3.37 us
    pallas_call x1, Pallas kernels, shards(): pl.pallas_call(product_kernel, in_specs=[hbm] + [vmem] * 9, out_specs=vme...  3.35 us
    pallas_call x1, Pallas kernels, shards(): pl.pallas_call(near_kernel, in_specs=[hbm, vmem], out_specs=vmem, out_sha...  3.2 us
    pallas_call x1, Pallas kernels, shards(): pl.pallas_call(prepare_kernel, in_specs=[hbm] * 8, out_specs=[vmem] * 4,...  3.12 us
    ppermute x1, starting transfers between devices, shards(): beyond = lax.ppermute(table, 'leaf', shift)  1.92 us
    ppermute x1, waiting for transfers between devices, shards(): beyond = lax.ppermute(table, 'leaf', shift)  1.92 us
  transfers between devices with their start and end apart: 4, of which 1 were waited for; matrix products, arithmetic and copies ran while one was open for 0% of the time, Pallas kernels for 10%

profile of v7, /device:TPU:392, one launch (start us, length us, event | category | flops | bytes accessed | tf_op | source)
XLA Modules:
  0.0 33.0 jit_solution(10578663228400661322)
XLA Ops:
  0.0 3.1 %prepare.1 = (f32[8,10368]{1,0:T(8,128)}, f32[8,1792]{1,0:T(8,128)}, f32[8,1792]{1,0:T(8,128)}, f32[32,8,128]{2,1,0:T(8,128)}) custom-call(bf16[8,4096]{1,0:T(8,128)(2,1)} %charges.1, f32[3,4096]{1,0:T(4,128)} %points.1, s32[32,128]{1,0:T(8,128)} %bitcast.9, bf16[16,64,256]{2,1,0:T(8,128)(2,1)} %basis.3, f32[16,64,64]{2,1,0:T(8,128)} %transfer.3, ...), custom_call_target="tpu_custom_call" | custom-call | tf_op jit(solution)/shard_map/prepare/pallas_call | solution.py:437
  3.1 0.0 copy-start.6
  3.1 0.0 copy-start.5
  3.1 7.7 %all-to-all-start = ((f32[32,8,128]{2,1,0:T(8,128)}), f32[32,8,128]{2,1,0:T(8,128)S(1)}, u32[]{:S(2)}, u32[]{:S(2)}) async-start(f32[32,8,128]{2,1,0:T(8,128)} %get-tuple-element.12), calls=%async_computation | async-start | bytes 262144 | tf_op jit(solution)/shard_map/all_to_all | solution.py:455
  10.8 0.0 copy-start.3
  10.8 0.0 copy-done.6
  10.9 3.4 %collective-permute-start = (f32[8,1792]{1,0:T(8,128)S(1)}, f32[8,1792]{1,0:T(8,128)S(1)}, u32[]{:S(2)}, u32[]{:S(2)}) collective-permute-start(f32[8,1792]{1,0:T(8,128)S(1)} %copy-done.6), channel_id=1, source_target_pairs={{1,2},{2,1},{3,4},{4,3},{5,6},{6,5},{7,8},{8,7},{9,10},{10,9},{11,... | collective-permute-start | bytes 172040 | tf_op jit(solution)/shard_map/ppermute | solution.py:459
  14.2 0.0 copy-done.5
  14.2 7.3 %collective-permute-start.1 = (f32[8,1792]{1,0:T(8,128)S(1)}, f32[8,1792]{1,0:T(8,128)S(1)}, u32[]{:S(2)}, u32[]{:S(2)}) collective-permute-start(f32[8,1792]{1,0:T(8,128)S(1)} %copy-done.5), channel_id=1, source_target_pairs={{0,1},{1,0},{2,3},{3,2},{4,5},{5,4},{6,7},{7,6},{8,9},{9,8},{10,11... | collective-permute-start | bytes 172040 | tf_op jit(solution)/shard_map/ppermute | solution.py:460
  21.5 0.0 all-to-all-done.table
  21.5 1.9 %collective-permute-start.2 = (f32[32,8,128]{2,1,0:T(8,128)S(1)}, f32[32,8,128]{2,1,0:T(8,128)S(1)}, u32[]{:S(2)}, u32[]{:S(2)}) collective-permute-start(f32[32,8,128]{2,1,0:T(8,128)S(1)} %all-to-all-done.table), channel_id=1, source_target_pairs={{0,32},{4,36},{8,40},{12,44},{32,64},{36,68},{40,72},{44,76},{64,9... | collective-permute-start | bytes 393224 | tf_op jit(solution)/shard_map/ppermute | solution.py:463
  23.5 0.0 copy-done.3
  23.5 0.0 copy-start.2
  23.5 1.0 %copy-done.2 = f32[8,10368]{1,0:T(8,128)S(1)} copy-done((f32[8,10368]{1,0:T(8,128)S(1)}, f32[8,10368]{1,0:T(8,128)}, u32[]{:S(2)}) %copy-start.2) | copy-done | bytes 331800
  24.4 0.0 copy-start
  24.4 0.0 copy-start.1
  24.5 0.0 copy-start.4
  24.5 3.2 %near_field.1.total = f32[8,4096]{1,0:T(8,128)S(1)} custom-call(s32[5,16]{1,0:T(8,128)S(1)} %bitcast.5, f32[8,10368]{1,0:T(8,128)S(1)} %copy-done.2), custom_call_target="tpu_custom_call" | custom-call | flops 8999999488 | bytes 1000000 | tf_op jit(solution)/shard_map/near_field/pallas_call | solution.py:464
  27.7 0.0 collective-permute-done.outer
  27.7 0.0 collective-permute-done.1.inner
  27.7 1.9 %collective-permute-done.2.beyond = f32[32,8,128]{2,1,0:T(8,128)S(1)} collective-permute-done((f32[32,8,128]{2,1,0:T(8,128)S(1)}, f32[32,8,128]{2,1,0:T(8,128)S(1)}, u32[]{:S(2)}, u32[]{:S(2)}) %collective-permute-start.2) | collective-permute-done | bytes 131104 | tf_op jit(solution)/shard_map/ppermute | solution.py:463
  29.6 0.0 copy-done
  29.6 0.0 copy-done.1
  29.6 0.0 copy-done.4
  29.6 3.3 %product.1 = f32[8,4096]{1,0:T(8,128)} custom-call(s32[5,16]{1,0:T(8,128)S(1)} %bitcast.6, s32[8,16]{1,0:T(8,128)S(1)} %bitcast.7, f32[16,64,64]{2,1,0:T(8,128)S(1)} %copy-done, bf16[16,64,256]{2,1,0:T(8,128)(2,1)S(1)} %copy-done.1, f32[8,10368]{1,0:T(8,128)S(1)} %copy-done.2, f32[8,1792]{1,0:T(8,128)S(1)} %collective-permute-done.outer, ...), custom_call_target="tpu_custom_call" | custom-call | tf_op jit(solution)/shard_map/product/pallas_call | solution.py:482
Async XLA Ops:
  3.1 7.7 %copy-start.6 = (f32[8,1792]{1,0:T(8,128)S(1)}, f32[8,1792]{1,0:T(8,128)}, u32[]{:S(2)}) copy-start(f32[8,1792]{1,0:T(8,128)} %get-tuple-element.10) | copy-start | bytes 172036
  3.1 11.1 %copy-start.5 = (f32[8,1792]{1,0:T(8,128)S(1)}, f32[8,1792]{1,0:T(8,128)}, u32[]{:S(2)}) copy-start(f32[8,1792]{1,0:T(8,128)} %get-tuple-element.11) | copy-start | bytes 172036
  3.1 18.4 %all-to-all-start = ((f32[32,8,128]{2,1,0:T(8,128)}), f32[32,8,128]{2,1,0:T(8,128)S(1)}, u32[]{:S(2)}, u32[]{:S(2)}) async-start(f32[32,8,128]{2,1,0:T(8,128)} %get-tuple-element.12), calls=%async_computation | async-start | bytes 262144 | tf_op jit(solution)/shard_map/all_to_all | solution.py:455
  10.8 12.6 %copy-start.3 = (s32[16,5]{0,1:T(8,128)S(1)}, s32[16,5]{0,1:T(8,128)}, u32[]{:S(2)}) copy-start(s32[16,5]{0,1:T(8,128)} %param.17) | copy-start | bytes 964
  10.9 16.8 %collective-permute-start = (f32[8,1792]{1,0:T(8,128)S(1)}, f32[8,1792]{1,0:T(8,128)S(1)}, u32[]{:S(2)}, u32[]{:S(2)}) collective-permute-start(f32[8,1792]{1,0:T(8,128)S(1)} %copy-done.6), channel_id=1, source_target_pairs={{1,2},{2,1},{3,4},{4,3},{5,6},{6,5},{7,8},{8,7},{9,10},{10,9},{11,... | collective-permute-start | bytes 172040 | tf_op jit(solution)/shard_map/ppermute | solution.py:459
  14.2 13.4 %collective-permute-start.1 = (f32[8,1792]{1,0:T(8,128)S(1)}, f32[8,1792]{1,0:T(8,128)S(1)}, u32[]{:S(2)}, u32[]{:S(2)}) collective-permute-start(f32[8,1792]{1,0:T(8,128)S(1)} %copy-done.5), channel_id=1, source_target_pairs={{0,1},{1,0},{2,3},{3,2},{4,5},{5,4},{6,7},{7,6},{8,9},{9,8},{10,11... | collective-permute-start | bytes 172040 | tf_op jit(solution)/shard_map/ppermute | solution.py:460
  21.5 8.1 %collective-permute-start.2 = (f32[32,8,128]{2,1,0:T(8,128)S(1)}, f32[32,8,128]{2,1,0:T(8,128)S(1)}, u32[]{:S(2)}, u32[]{:S(2)}) collective-permute-start(f32[32,8,128]{2,1,0:T(8,128)S(1)} %all-to-all-done.table), channel_id=1, source_target_pairs={{0,32},{4,36},{8,40},{12,44},{32,64},{36,68},{40,72},{44,76},{64,9... | collective-permute-start | bytes 393224 | tf_op jit(solution)/shard_map/ppermute | solution.py:463
  23.5 1.0 %copy-start.2 = (f32[8,10368]{1,0:T(8,128)S(1)}, f32[8,10368]{1,0:T(8,128)}, u32[]{:S(2)}) copy-start(f32[8,10368]{1,0:T(8,128)} %get-tuple-element.9.own) | copy-start | bytes 995332
  24.4 5.2 %copy-start = (f32[16,64,64]{2,1,0:T(8,128)S(1)}, f32[16,64,64]{2,1,0:T(8,128)}, u32[]{:S(2)}) copy-start(f32[16,64,64]{2,1,0:T(8,128)} %transfer.3) | copy-start | bytes 786436
  24.4 5.2 %copy-start.1 = (bf16[16,64,256]{2,1,0:T(8,128)(2,1)S(1)}, bf16[16,64,256]{2,1,0:T(8,128)(2,1)}, u32[]{:S(2)}) copy-start(bf16[16,64,256]{2,1,0:T(8,128)(2,1)} %basis.3) | copy-start | bytes 1572868
  24.5 5.2 %copy-start.4 = (s32[16,8]{0,1:T(8,128)S(1)}, s32[16,8]{0,1:T(8,128)}, u32[]{:S(2)}) copy-start(s32[16,8]{0,1:T(8,128)} %param.18) | copy-start | bytes 1540
